TPU v7x, 256 devices: a whole 4x4x8 slice. The times are simulated.
256 devices in a mesh: pipe: 8 (over z), dp: 32 (over y, x, core).
Axes of the slice: x: 4, y: 4, z: 8, core: 2. Of those that a mesh axis runs over, the one named last changes fastest.
Arguments:
- acts: bfloat16 [32768, 6144], P(('pipe', 'dp'))
- grads_out: bfloat16 [32768, 24576], P(('pipe', 'dp')), may hold values from -6 to 6
- weight_grad: bfloat16 [6144, 24576], P('pipe', 'dp'), may hold values from -6 to 6
- slot_table: int32 [256], replicated, may hold values from -1 to 239, as said below
- row_counts: int32 [256], P(('pipe', 'dp')), may hold values from 32 to 128
- old_cov: float32 [32, 8, 128, 128], P('dp', 'pipe'), as said below
Outputs:
- precond_grad: bfloat16 [6144, 24576], P('pipe', 'dp')
- new_cov: float32 [32, 8, 128, 128], P('dp', 'pipe')
Inputs may be any that keep to these rules, and one draw needn't show every extreme that they name: `slot_table`: every block 0 to 239 stands in exactly one slot; the other slots hold -1. `old_cov`: each block is symmetric and its diagonal dominates its row.
All inputs are finite; a program needn't handle non-finite values.
Results may differ from a plain program's by a relative error of at most 0.0045.
The roundings to bfloat16 on the way count: a program that leaves them out, or rounds other values in their place, can miss the bound.
Values may be sent and summed in bfloat16 or wider, within the bound.
No kernel may reach another device: no remote copies, remote signals or barrier semaphores. Data moves between devices by JAX's collectives and lax.ppermute only.
A program may use at most 128 MiB of HBM per device.

v0:
```python
import jax
import jax.numpy as jnp
from jax import lax
from jax.sharding import PartitionSpec as P


def invert_blocks(cov):
    eye = jnp.eye(cov.shape[-1], dtype=cov.dtype)
    chol = jnp.linalg.cholesky(cov + 0.1 * eye)
    solve_one = lambda factor: jax.scipy.linalg.cho_solve((factor, True), eye)
    return jax.vmap(solve_one)(chol)


def slot_gram(piece):
    return jnp.einsum("tuxb,tuxc->xbc", piece, piece, preferred_element_type=jnp.float32)


def locate(slot_table, wanted):
    slot_ids = jnp.arange(slot_table.shape[0], dtype=jnp.int32)
    hits = slot_table[None, :] == wanted[:, None]
    return jnp.sum(jnp.where(hits, slot_ids[None, :], 0), axis=1)


def on_device(acts, grads_out, weight_grad, slot_table, row_counts, old_cov):
    tok_rows = acts.shape[0]
    block = old_cov.shape[-1]
    in_blocks = acts.shape[1] // block
    out_blocks = grads_out.shape[1] // block
    owners = lax.axis_size("dp")
    owner_slots = slot_table.shape[0] // owners
    live = jnp.arange(tok_rows, dtype=jnp.int32) < row_counts[0]
    acts_live = jnp.where(live[:, None], acts, jnp.zeros_like(acts))
    grads_live = jnp.where(live[:, None], grads_out, jnp.zeros_like(grads_out))
    features = jnp.concatenate(
        (
            acts_live.reshape(tok_rows, in_blocks, block),
            grads_live.reshape(tok_rows, out_blocks, block),
        ),
        axis=1,
    )
    picked = jnp.take(features, jnp.maximum(slot_table, 0), axis=1)
    filled = (slot_table >= 0).astype(jnp.bfloat16)
    outgoing = (picked * filled[None, :, None]).reshape(tok_rows, owners, owner_slots, block)
    gram = slot_gram(lax.all_to_all(outgoing, "dp", split_axis=1, concat_axis=0, tiled=True))
    gram_share = lax.psum_scatter(gram, "pipe", scatter_dimension=0, tiled=True)
    total = lax.psum(row_counts.astype(jnp.float32)[0], ("pipe", "dp"))
    cov_share = 0.8 * old_cov[0] + 0.2 * gram_share / total
    slot_pos = jnp.arange(owners * owner_slots, dtype=jnp.int32)
    row_blocks = weight_grad.shape[0] // block
    col_blocks = weight_grad.shape[1] // block
    section = lax.axis_index("pipe")
    owner = lax.axis_index("dp")
    a_ids = section * row_blocks + jnp.arange(row_blocks, dtype=jnp.int32)
    g_ids = in_blocks + owner * col_blocks + jnp.arange(col_blocks, dtype=jnp.int32)
    owner_cov = lax.all_gather(cov_share, "pipe", axis=0, tiled=True)
    owner_all = invert_blocks(owner_cov).astype(jnp.bfloat16)
    inverses = lax.all_gather(owner_all, "dp", axis=0, tiled=True)
    a_inv = jnp.take(inverses, jnp.take(slot_pos, locate(slot_table, a_ids)), axis=0)
    g_inv = jnp.take(inverses, jnp.take(slot_pos, locate(slot_table, g_ids)), axis=0)
    grad_blocks = weight_grad.reshape(row_blocks, block, weight_grad.shape[1])
    left = jnp.einsum(
        "ixy,iyc->ixc", a_inv, grad_blocks, preferred_element_type=jnp.float32
    ).astype(jnp.bfloat16)
    left = left.reshape(weight_grad.shape[0], col_blocks, block)
    right = jnp.einsum("rjy,jyz->rjz", left, g_inv, preferred_element_type=jnp.float32)
    precond_grad = right.reshape(weight_grad.shape).astype(jnp.bfloat16)
    return (precond_grad, cov_share[None])


def solution(mesh):
    in_specs = (
        P(("pipe", "dp"), None),
        P(("pipe", "dp"), None),
        P("pipe", "dp"),
        P(),
        P(("pipe", "dp")),
        P("dp", "pipe", None, None),
    )
    out_specs = (P("pipe", "dp"), P("dp", "pipe", None, None))
    return jax.shard_map(
        on_device, mesh=mesh, in_specs=in_specs, out_specs=out_specs, check_vma=False
    )
```

profile of v0, /device:TPU:1, one launch (start us, length us, event | category | flops | bytes accessed | tf_op | source)
XLA Modules:
  0.0 571.2 jit_solution(6656117015598982059)
XLA Ops:
  9.3 8.6 %copy.60 = bf16[128,24576]{0,1:T(8,128)(2,1)} copy(bf16[128,24576]{1,0:T(8,128)(2,1)} %param.11) | data formatting | bytes 12582912 | tf_op args[1]
  18.0 6.4 %broadcast_select_fusion = bf16[128,24576]{0,1:T(8,128)(2,1)} fusion(bf16[128,24576]{0,1:T(8,128)(2,1)} %copy.60, pred[128]{0:T(512)(128)(4,1)S(1)} %iota_compare_fusion.2), kind=kLoop, calls=%fused_computation.10 | loop fusion | flops 3145728 | bytes 12583040 | tf_op jit(solution)/shard_map/jit(_where)/select_n | solution.py:33
  24.4 8.8 %copy.62 = bf16[128,192,128]{2,0,1:T(8,128)(2,1)} copy(bf16[128,192,128]{0,2,1:T(8,128)(2,1)} %bitcast.41) | data formatting | bytes 12582912 | tf_op jit(solution)/shard_map/reshape | solution.py:37
  33.2 1.6 copy.59
  34.7 1.5 broadcast_select_fusion.1
  36.2 1.6 copy.61
  38.0 7.0 %pad_maximum_fusion = bf16[128,240,128]{2,0,1:T(8,128)(2,1)} fusion(bf16[128,192,128]{2,0,1:T(8,128)(2,1)} %copy.62, bf16[128,48,128]{2,0,1:T(8,128)(2,1)} %copy.61), kind=kLoop, calls=%fused_computation.9 | loop fusion | flops 3932160 | bytes 15728640 | tf_op jit(solution)/shard_map/concatenate | solution.py:34
  45.0 12.0 %gather_fusion = bf16[256,128,128]{2,1,0:T(8,128)(2,1)} fusion(bf16[128,240,128]{2,0,1:T(8,128)(2,1)} %pad_maximum_fusion, s32[1024]{0:T(1024)S(1)} %pad_clamp_fusion.3), kind=kCustom, calls=%fused_computation.4 | custom fusion | bytes 16778240 | tf_op jit(solution)/shard_map/jit(_take)/gather | solution.py:41
  57.0 23.6 %fusion.2 = bf16[128,32,8,128]{3,2,1,0:T(8,128)(2,1)} fusion(bf16[128,256,128]{2,0,1:T(8,128)(2,1)} %bitcast.38, pred[32,8]{1,0:T(8,128)(4,1)S(1)} %broadcast_in_dim.87, bf16[32,8]{1,0:T(8,128)(2,1)S(1)} %reshape.101), kind=kLoop, calls=%fused_computation.8 | loop fusion | flops 8388608 | bytes 16777984 | tf_op jit(solution)/shard_map/mul | solution.py:43
  80.6 8.9 %copy.64 = bf16[128,32,8,128]{3,2,0,1:T(8,128)(2,1)} copy(bf16[128,32,8,128]{3,2,1,0:T(8,128)(2,1)} %fusion.2) | data formatting | bytes 16777216 | tf_op jit(solution)/shard_map/mul | solution.py:43
  89.5 104.5 %all_to_all.15 = bf16[128,32,8,128]{3,2,0,1:T(8,128)(2,1)} all-to-all(bf16[128,32,8,128]{3,2,0,1:T(8,128)(2,1)} %copy.64), channel_id=1, replica_groups=mesh['pipe'=8,'dp'=32] {'dp'}, dimensions={1} | all-to-all | bytes 16777216 | tf_op jit(solution)/shard_map/all_to_all | solution.py:44
  194.0 8.8 %copy.65 = bf16[32,128,1,8,128]{4,1,0,3,2:T(8,128)(2,1)} copy(bf16[32,128,1,8,128]{4,3,1,0,2:T(8,128)(2,1)} %bitcast.39) | data formatting | bytes 16777216 | tf_op jit(solution)/shard_map/all_to_all | solution.py:44
  202.9 9.4 %fusion = f32[8,128,128]{2,1,0:T(8,128)} fusion(bf16[4096,8,128]{2,0,1:T(8,128)(2,1)} %bitcast.42, bf16[4096,8,128]{2,1,0:T(8,128)(2,1)} %bitcast.40), kind=kOutput, calls=%fused_computation.5 | convolution fusion | flops 1073741824 | bytes 17301504 | tf_op jit(solution)/shard_map/tuxb,tuxc->xbc/dot_general | solution.py:15
  212.4 79.0 %psum.7 = f32[]{:T(128)} all-reduce(f32[]{:T(128)} %bitcast.10), channel_id=1, replica_groups=mesh['pipe'=8,'dp'=32] {'pipe','dp'}, use_global_device_ids=true, to_apply=%region_1.2 | all-reduce | flops 1 | bytes 8 | tf_op jit(solution)/shard_map/psum | solution.py:46
  293.1 19.8 %all_gather.6 = f32[8,128,128]{2,1,0:T(8,128)S(1)} all-gather(f32[1,128,128]{2,1,0:T(8,128)S(1)} %bitcast_add_fusion.1), channel_id=1, replica_groups=mesh['pipe'=8,'dp'=32] {'pipe'}, dimensions={0}, use_global_device_ids=true | all-gather | bytes 589824 | tf_op jit(solution)/shard_map/all_gather | solution.py:55
  313.5 93.8 %custom-call.11 = f32[8,128,128]{2,1,0:T(8,128)S(1)} custom-call(f32[8,128,128]{2,1,0:T(8,128)S(1)} %fusion.7), custom_call_target="Cholesky" | custom-call | tf_op jit(solution)/shard_map/jit(cholesky)/cholesky | solution.py:9
  407.6 78.6 %custom-call.12 = f32[8,1,128,128]{2,3,1,0:T(8,128)S(1)} custom-call(f32[8,1,128,128]{3,2,1,0:T(8,128)S(1)} %select_bitcast_fusion), custom_call_target="InvertDiagBlocksLowerTriangular" | custom-call | tf_op jit(solution)/shard_map/vmap(jit(_cho_solve))/triangular_solve | solution.py:10
  490.2 57.4 %all-gather.2.cloned.1.call-done = bf16[256,128,128]{2,1,0:T(8,128)(2,1)} async-done(((bf16[8,128,128]{2,1,0:T(8,128)(2,1)}), bf16[256,128,128]{2,1,0:T(8,128)(2,1)}) %all-gather.2.cloned.1.call-update) | async-done | bytes 8388624 | tf_op jit(solution)/shard_map/all_gather | solution.py:57
  547.6 4.0 gather_fusion.4
  551.6 1.5 convolution_convert_fusion.1
  553.1 2.8 reshape.100
  555.9 4.0 gather_fusion.2
  559.9 1.7 convolution_convert_fusion
  561.6 2.4 copy.73
  (50 shorter events, 8.2 us)
Async XLA Ops:
  7.2 544.4 %copy-start = (bf16[768,768]{1,0:T(8,128)(2,1)S(1)}, bf16[768,768]{1,0:T(8,128)(2,1)}, u32[]{:S(2)}) copy-start(bf16[768,768]{1,0:T(8,128)(2,1)} %param.12) | copy-start | bytes 3538948
  7.2 284.4 %reduce-scatter.2.cloned.1.call-start = ((), (), s32[]{:S(2)}) async-start(), calls=%async_computation.2 | async-start | bytes 589824 | tf_op jit(solution)/shard_map/reduce_scatter | solution.py:45
  24.4 8.8 %copy-start.1 = (bf16[128,6144]{1,0:T(8,128)(2,1)S(1)}, bf16[128,6144]{1,0:T(8,128)(2,1)}, u32[]{:S(2)}) copy-start(bf16[128,6144]{1,0:T(8,128)(2,1)} %param.10) | copy-start | bytes 4718596
  202.9 88.7 %copy-start.3 = (f32[1,1,128,128]{3,2,1,0:T(8,128)S(1)}, f32[1,1,128,128]{3,2,1,0:T(8,128)}, u32[]{:S(2)}) copy-start(f32[1,1,128,128]{3,2,1,0:T(8,128)} %param.15) | copy-start | bytes 196612
  212.3 276.3 %copy-start.4 = (s32[256]{0:T(256)S(1)}, s32[256]{0:T(256)}, u32[]{:S(2)}) copy-start(s32[256]{0:T(256)} %param.13) | copy-start | bytes 3076
  212.3 335.2 %all-gather.2.cloned.1.call-start = ((), (), s32[]{:S(2)}) async-start(), calls=%async_computation.3 | async-start | bytes 8650752 | tf_op jit(solution)/shard_map/all_gather | solution.py:57
  293.1 260.0 %copy-start.2 = (f32[1,128,128]{2,1,0:T(8,128)}, f32[1,128,128]{2,1,0:T(8,128)S(1)}, u32[]{:S(2)}) copy-start(f32[1,128,128]{2,1,0:T(8,128)S(1)} %bitcast_add_fusion.1) | copy-start | bytes 196612
Sparse Core Ops, SparseCore 0:
  212.5 32.6 reduce-scatter.1
  488.7 58.8 all-gather.1
where the time goes:
time: 576 us; the launch traced here: 571 us
  other arithmetic  215 us (37%)
  blocking collectives  203 us (35%)
  local copies, waits for them, and re-layouts  65.4 us (11%)
  waiting for transfers between devices  57.4 us (10%)
  between operations  15.4 us (3%)
  matrix products  15 us (3%)
    all_to_all x1, blocking collectives, on_device(): lax.all_to_all(outgoing, 'dp', split_axis=1, concat_axis=0, tiled=True)  105 us
    another operation x4, other arithmetic, invert_blocks(): chol = jnp.linalg.cholesky(cov + 0.1 * eye)  94 us
    psum x1, blocking collectives, on_device(): total = lax.psum(row_counts.astype(jnp.float32)[0], ('pipe', 'dp'))  79 us
    another operation x3, other arithmetic, invert_blocks(): solve_one = lambda factor: jax.scipy.linalg.cho_solve((factor, True), eye)  78.7 us
    all_gather x1, waiting for transfers between devices, on_device(): inverses = lax.all_gather(owner_all, 'dp', axis=0, tiled=True)  57.4 us
    mul x2, other arithmetic, on_device(): picked * filled[None, :, None]  24.2 us
    all_gather x1, blocking collectives, on_device(): owner_cov = lax.all_gather(cov_share, 'pipe', axis=0, tiled=True)  19.8 us
    unnamed x13, local copies, waits for them, and re-layouts  12.6 us
  transfers between devices with their start and end apart: 2, of which 1 were waited for; matrix products, arithmetic and copies ran while one was open for 0% of the time, Pallas kernels for 0%

commit v1 on v0

v1 whole, which is shorter than its diff:
```python
import functools

import jax
import jax.numpy as jnp
from jax import lax
from jax.experimental import pallas as pl
from jax.experimental.pallas import tpu as pltpu
from jax.sharding import Mesh, PartitionSpec as P

B = 128
H = B // 2
BF = jnp.bfloat16
F32 = jnp.float32
EXTRA = 16
VMEM_LIMIT = 50 * 1024 * 1024


def iota(shape, dim):
    return lax.broadcasted_iota(jnp.int32, shape, dim)


def pack(sym):
    top = sym[:H, :]
    low = pltpu.roll(sym[H:, :], H, 1)
    row, lane = iota((H, B), 0), iota((H, B), 1)
    half = jnp.where(lane < row, low, top)
    diag = jnp.sum(jnp.where(lane == row, low, 0.0), axis=0, keepdims=True)
    return half, diag


def unpack(half, diag):
    row, lane = iota((H, B), 0), iota((H, B), 1)
    upper = jnp.where(lane >= row, half, 0.0)
    lower = jnp.where(lane < row, half, 0.0)
    lower = jnp.where(lane == row, diag, lower)
    lower = pltpu.roll(lower, H, 1)
    part = jnp.concatenate((upper, lower), axis=0)
    brow, blane = iota((B, B), 0), iota((B, B), 1)
    return part + jnp.where(brow == blane, 0.0, part.T)


def invert(mat):
    rows = 8
    groups = [mat[g * rows : (g + 1) * rows, :] for g in range(B // rows)]
    lane, sub = iota((rows, B), 1), iota((rows, B), 0)
    for k in range(B):
        at, inside = k // rows, k % rows
        own = groups[at]
        scale = 1.0 / own[inside : inside + 1, k : k + 1]
        line = jnp.where(lane[:1] == k, scale, own[inside : inside + 1, :] * scale)
        line = jnp.broadcast_to(line, (rows, B))
        fresh = []
        for g in range(B // rows):
            col = jnp.broadcast_to(groups[g][:, k : k + 1], (rows, B))
            new = jnp.where(lane == k, 0.0, groups[g]) - col * line
            if g == at:
                new = jnp.where(sub == inside, line, new)
            fresh.append(new)
        groups = fresh
    return jnp.concatenate(groups, axis=0)


def gram_kernel(acts_steps, chunk, slot_ref, me_ref, acts_ref, grads_ref, own_ref, send_ref, diag_ref):
    step = pl.program_id(0)
    live = me_ref[0]
    core = me_ref[1]
    group_rows = own_ref.shape[0] // 16

    @pl.when(step == 0)
    def _():
        own_ref[...] = jnp.zeros_like(own_ref)
        send_ref[...] = jnp.zeros_like(send_ref)
        diag_ref[...] = jnp.zeros_like(diag_ref)

    def work(x_ref):
        x = x_ref[...]
        x = jnp.where(iota(x.shape, 0) < live, x, jnp.zeros_like(x))
        for b in range(chunk):
            xb = x[:, b * B : (b + 1) * B]
            gram = lax.dot_general(xb, xb, (((0,), (0,)), ((), ())), preferred_element_type=F32)
            half, diag = pack(gram)
            half = half.astype(BF)
            slot = slot_ref[step * chunk + b]
            owner, row = slot // 8, slot % 8
            other = (owner % 2) != core
            group = owner // 2
            at = pl.multiple_of(group * group_rows + row * H, 16)

            @pl.when(other)
            def _():
                send_ref[pl.ds(at, H), :] = half

            @pl.when(jnp.logical_not(other))
            def _():
                own_ref[pl.ds(at, H), :] = half

            diag_ref[pl.ds(other.astype(jnp.int32) * 128 + group * 8 + row, 1), :] = diag

    pl.when(step < acts_steps)(lambda: work(acts_ref))
    pl.when(step >= acts_steps)(lambda: work(grads_ref))

    @pl.when(step == pl.num_programs(0) - 1)
    def _():
        count = jnp.full((8, B), live, jnp.int32).astype(F32)
        for rel, ref in ((0, own_ref), (1, send_ref)):
            for group in range(16):
                rows = diag_ref[pl.ds(rel * 128 + group * 8, 8), :]
                ref[pl.ds(group * group_rows + 8 * H, EXTRA), :] = jnp.concatenate((rows, count), axis=0).astype(BF)


def grams(slot_of, me, acts, grads_out):
    chunk = 8
    width = chunk * B
    tok = acts.shape[0]
    acts_steps = acts.shape[1] // width
    grads_steps = grads_out.shape[1] // width
    group_rows = 8 * H + EXTRA
    out = jax.ShapeDtypeStruct((16 * group_rows, B), BF)
    whole = pl.BlockSpec((16 * group_rows, B), lambda i, *_: (0, 0))
    return pl.pallas_call(
        functools.partial(gram_kernel, acts_steps, chunk),
        out_shape=(out, out),
        grid_spec=pltpu.PrefetchScalarGridSpec(
            num_scalar_prefetch=2,
            grid=(acts_steps + grads_steps,),
            in_specs=[
                pl.BlockSpec((tok, width), lambda i, *_: (0, jnp.minimum(i, acts_steps - 1))),
                pl.BlockSpec((tok, width), lambda i, *_: (0, jnp.maximum(i - acts_steps, 0))),
            ],
            out_specs=[whole, whole],
            scratch_shapes=[pltpu.VMEM((256, B), F32)],
        ),
        compiler_params=pltpu.CompilerParams(vmem_limit_bytes=VMEM_LIMIT),
        name="grams",
    )(slot_of, me, acts, grads_out)


def section_kernel(parts_ref, out_ref):
    for row in range(8):
        total = parts_ref[0, row * H : (row + 1) * H, :].astype(F32)
        for g in range(1, 16):
            total += parts_ref[g, row * H : (row + 1) * H, :].astype(F32)
        out_ref[row, :H, :] = total.astype(BF)
    extra = parts_ref[0, 8 * H :, :].astype(F32)
    for g in range(1, 16):
        extra += parts_ref[g, 8 * H :, :].astype(F32)
    count = extra[8:, :]
    high = jnp.floor(count * (1.0 / 256.0))
    low = count - 256.0 * high
    sub = iota((8, B), 0)
    for row in range(8):
        first = jnp.where(sub == 0, jnp.broadcast_to(extra[row : row + 1, :], (8, B)), jnp.where(sub == 1, high, low))
        out_ref[row, H:, :] = jnp.concatenate((first, jnp.zeros_like(first)), axis=0).astype(BF)


def section_sum(parts):
    return pl.pallas_call(
        section_kernel,
        out_shape=jax.ShapeDtypeStruct((8, H + EXTRA, B), BF),
        compiler_params=pltpu.CompilerParams(vmem_limit_bytes=VMEM_LIMIT),
        name="section_sum",
    )(parts)


def inverse_kernel(parts_ref, old_ref, cov_ref, out_ref):
    half = parts_ref[0, :H, :].astype(F32)
    extra = parts_ref[0, H:, :].astype(F32)
    for s in range(1, 8):
        half += parts_ref[s, :H, :].astype(F32)
        extra += parts_ref[s, H:, :].astype(F32)
    total = extra[1:2, :] * 256.0 + extra[2:3, :]
    gram = unpack(half, extra[:1, :])
    cov = 0.8 * old_ref[0, 0] + 0.2 * gram / total
    cov_ref[0, 0] = cov
    eye = jnp.where(iota((B, B), 0) == iota((B, B), 1), 0.1, 0.0)
    inv_half, inv_diag = pack(invert(cov + eye))
    out_ref[:H, :] = inv_half.astype(BF)
    out_ref[H:, :] = jnp.broadcast_to(inv_diag, (EXTRA, B)).astype(BF)


def inverse(parts, old_cov):
    return pl.pallas_call(
        inverse_kernel,
        out_shape=(
            jax.ShapeDtypeStruct(old_cov.shape, F32),
            jax.ShapeDtypeStruct((H + EXTRA, B), BF),
        ),
        compiler_params=pltpu.CompilerParams(vmem_limit_bytes=VMEM_LIMIT),
        name="inverse",
    )(parts, old_cov)


def final_kernel(in_blocks, slot_ref, me_ref, inv_ref, weight_ref, out_ref, left_ref):
    section, owner = me_ref[2], me_ref[3]
    row_blocks = weight_ref.shape[0] // B
    col_blocks = weight_ref.shape[1] // B

    def block(which):
        slot = slot_ref[which]
        packed = inv_ref[slot].astype(F32)
        return unpack(packed[:H, :], packed[H : H + 1, :]).astype(BF)

    for i in range(row_blocks):
        rows = slice(i * B, (i + 1) * B)
        left = jnp.dot(block(section * row_blocks + i), weight_ref[rows, :], preferred_element_type=F32)
        left_ref[rows, :] = left.astype(BF)
    for j in range(col_blocks):
        cols = slice(j * B, (j + 1) * B)
        right = jnp.dot(left_ref[:, cols], block(in_blocks + owner * col_blocks + j), preferred_element_type=F32)
        out_ref[:, cols] = right.astype(BF)


def final(slot_of, me, inverses, weight_grad, in_blocks):
    smem = pl.BlockSpec(memory_space=pltpu.SMEM)
    vmem = pl.BlockSpec(memory_space=pltpu.VMEM)
    return pl.pallas_call(
        functools.partial(final_kernel, in_blocks),
        out_shape=jax.ShapeDtypeStruct(weight_grad.shape, BF),
        in_specs=[smem, smem, vmem, vmem],
        out_specs=vmem,
        scratch_shapes=[pltpu.VMEM(weight_grad.shape, BF)],
        compiler_params=pltpu.CompilerParams(vmem_limit_bytes=VMEM_LIMIT),
        name="final",
    )(slot_of, me, inverses, weight_grad)


def locate(slot_table, count):
    slot_ids = jnp.arange(slot_table.shape[0], dtype=jnp.int32)
    hits = slot_table[None, :] == jnp.arange(count, dtype=jnp.int32)[:, None]
    return jnp.sum(jnp.where(hits, slot_ids[None, :], 0), axis=1)


def on_device(acts, grads_out, weight_grad, slot_table, row_counts, old_cov):
    in_blocks = acts.shape[1] // B
    out_blocks = grads_out.shape[1] // B
    core = lax.axis_index("c")
    section = lax.axis_index("z")
    owner = (lax.axis_index("y") * 4 + lax.axis_index("x")) * 2 + core
    slot_of = locate(slot_table, in_blocks + out_blocks)
    me = jnp.stack((row_counts[0], core, section, owner)).astype(jnp.int32)
    own, send = grams(slot_of, me, acts, grads_out)
    got = lax.ppermute(send, "c", [(0, 1), (1, 0)])
    chip = (own.astype(F32) + got.astype(F32)).astype(BF)
    chip = chip.reshape(16, -1, B)
    plane = lax.all_to_all(chip, ("y", "x"), split_axis=0, concat_axis=0, tiled=True)
    share = lax.all_to_all(section_sum(plane), "z", split_axis=0, concat_axis=0, tiled=True)
    new_cov, inv = inverse(share, old_cov)
    column = lax.all_gather(inv, "z", axis=0)
    inverses = lax.all_gather(column, ("y", "x", "c"), axis=0, tiled=True)
    return final(slot_of, me, inverses, weight_grad, in_blocks), new_cov


def solution(mesh):
    wide = Mesh(mesh.devices.reshape(8, 4, 4, 2), ("z", "y", "x", "c"))
    dp = ("y", "x", "c")
    in_specs = (
        P(("z",) + dp, None),
        P(("z",) + dp, None),
        P("z", dp),
        P(),
        P(("z",) + dp),
        P(dp, "z", None, None),
    )
    out_specs = (P("z", dp), P(dp, "z", None, None))
    return jax.shard_map(
        on_device, mesh=wide, in_specs=in_specs, out_specs=out_specs, check_vma=False
    )
```

time: 576 us -> 237 us (0.41)
  other arithmetic: 215 us -> 1.46 us
  blocking collectives: 203 us -> 70.3 us
  Pallas kernels: 0 us -> 86.1 us
  local copies, waits for them, and re-layouts: 65.4 us -> 1.42 us
  matrix products: 15 us -> 0 us
    another operation x7 -> x1, other arithmetic: 173 us -> 0.08 us  [on_device(): me = jnp.stack((row_counts[0], core, section, owner)).astype(jnp.int32)]
    pallas_call x0 -> x4, Pallas kernels: none -> 86.1 us  [the longest x1 69.5 us: grams(): pl.pallas_call(functools.partial(gram_kernel, acts_steps, chunk), out_sha...]
    psum x1 -> x0, blocking collectives: 79 us -> none  [on_device(): total = lax.psum(row_counts.astype(jnp.float32)[0], ('pipe', 'dp'))]
    all_to_all x1 -> x2, blocking collectives: 105 us -> 49.6 us  [the longest x1 33.1 us: on_device(): lax.all_to_all(chip, ('y', 'x'), split_axis=0, concat_axis=0, tiled=True)]
    mul x3 -> x0, other arithmetic: 24.2 us -> none  [the longest x2 24.2 us: on_device(): picked * filled[None, :, None]]
    gather x5 -> x0, local copies, waits for them, and re-layouts: 21.2 us -> none  [the longest x1 12 us: on_device(): picked = jnp.take(features, jnp.maximum(slot_table, 0), axis=1)]
    reshape x3 -> x0, local copies, waits for them, and re-layouts: 13.2 us -> none  [the longest x1 8.79 us: on_device(): grads_live.reshape(tok_rows, out_blocks, block)]
    dot_general x3 -> x0, matrix products: 12.7 us -> none  [the longest x1 9.44 us: slot_gram(): jnp.einsum('tuxb,tuxc->xbc', piece, piece, preferred_element_type=jnp.flo...]
  transfers between devices with their start and end apart: 2 -> 2, of which waited for: 1 -> 2; matrix products, arithmetic and copies ran while one was open for 0% -> 0% of each run, Pallas kernels for 0% -> 0%
where the time goes in v1:
time: 237 us; the launch traced here: 236 us
  Pallas kernels  86.1 us (36%)
  blocking collectives  70.3 us (30%)
  waiting for transfers between devices  59.1 us (25%)
  between operations  14.7 us (6%)
  starting transfers between devices  3.27 us (1%)
    pallas_call x1, Pallas kernels, grams(): pl.pallas_call(functools.partial(gram_kernel, acts_steps, chunk), out_sha...  69.5 us
    all_gather x1, waiting for transfers between devices, on_device(): inverses = lax.all_gather(column, ('y', 'x', 'c'), axis=0, tiled=True)  55 us
    all_to_all x1, blocking collectives, on_device(): lax.all_to_all(chip, ('y', 'x'), split_axis=0, concat_axis=0, tiled=True)  33.1 us
    all_gather x1, blocking collectives, on_device(): column = lax.all_gather(inv, 'z', axis=0)  20.7 us
    all_to_all x1, blocking collectives, on_device(): lax.all_to_all(section_sum(plane), 'z', split_axis=0, concat_axis=0, tile...  16.5 us
    pallas_call x1, Pallas kernels, inverse(): pl.pallas_call(inverse_kernel, out_shape=(jax.ShapeDtypeStruct(old_cov.sh...  11.8 us
  transfers between devices with their start and end apart: 2, of which 2 were waited for; matrix products, arithmetic and copies ran while one was open for 0% of the time, Pallas kernels for 0%

profile of v1, /device:TPU:1, one launch (start us, length us, event | category | flops | bytes accessed | tf_op | source)
XLA Modules:
  0.0 236.3 jit_solution(14892086712439520079)
XLA Ops:
  7.2 0.0 all-gather.3.cloned.1.call-start
  7.9 0.8 select_reduce_fusion.slot_ref
  8.7 0.1 pad_add_fusion.me_ref
  8.7 0.0 copy-start
  8.7 1.4 copy-done
  10.2 69.5 %grams.1 = (bf16[8448,128]{1,0:T(8,128)(2,1)S(1)}, bf16[8448,128]{1,0:T(8,128)(2,1)}) custom-call(s32[240]{0:T(256)S(1)} %select_reduce_fusion.slot_ref, s32[4]{0:T(128)S(1)} %pad_add_fusion.me_ref, bf16[128,6144]{1,0:T(8,128)(2,1)S(1)} %copy-done, bf16[128,24576]{1,0:T(8,128)(2,1)} %grads_ref.1), custom_call_target="tpu_custom_call" | custom-call | tf_op jit(solution)/shard_map/grams/pallas_call | solution.py:120
  79.6 3.2 %collective-permute-start = (bf16[8448,128]{1,0:T(8,128)(2,1)}, bf16[8448,128]{1,0:T(8,128)(2,1)S(1)}, u32[]{:S(2)}, u32[]{:S(2)}) collective-permute-start(bf16[8448,128]{1,0:T(8,128)(2,1)} %get-tuple-element.7), channel_id=1, source_target_pairs={{0,1},{1,0},{2,3},{3,2},{4,5},{5,4},{6,7},{7,6},{8,9},{9,8},{10,11... | collective-permute-start | bytes 6488072 | tf_op jit(solution)/shard_map/ppermute | solution.py:242
  82.9 4.1 %collective-permute-done = bf16[8448,128]{1,0:T(8,128)(2,1)S(1)} collective-permute-done((bf16[8448,128]{1,0:T(8,128)(2,1)}, bf16[8448,128]{1,0:T(8,128)(2,1)S(1)}, u32[]{:S(2)}, u32[]{:S(2)}) %collective-permute-start) | collective-permute-done | bytes 2162720 | tf_op jit(solution)/shard_map/ppermute | solution.py:242
  87.0 0.6 add_convert_fusion
  87.5 33.1 %all_to_all.10.parts_ref = bf16[16,528,128]{2,1,0:T(8,128)(2,1)S(1)} all-to-all(bf16[16,528,128]{2,1,0:T(8,128)(2,1)S(1)} %bitcast.5), channel_id=1, replica_groups=mesh['z'=8,'y'=4,'x'=4,'c'=2] {'y','x'}, dimensions={0} | all-to-all | bytes 4325376 | tf_op jit(solution)/shard_map/all_to_all | solution.py:245
  120.6 0.0 copy-start.2
  120.6 0.0 copy-start.1
  120.6 0.3 section_sum.1
  120.9 16.5 %all_to_all.11.parts_ref = bf16[8,80,128]{2,1,0:T(8,128)(2,1)S(1)} all-to-all(bf16[8,80,128]{2,1,0:T(8,128)(2,1)S(1)} %section_sum.1), channel_id=1, replica_groups=mesh['z'=8,'y'=4,'x'=4,'c'=2] {'z'}, dimensions={0} | all-to-all | bytes 327680 | tf_op jit(solution)/shard_map/all_to_all | solution.py:246
  137.4 0.0 copy-done.2
  137.4 11.8 %inverse.1 = (f32[1,1,128,128]{3,2,1,0:T(8,128)}, bf16[80,128]{1,0:T(8,128)(2,1)S(1)}) custom-call(bf16[8,80,128]{2,1,0:T(8,128)(2,1)S(1)} %all_to_all.11.parts_ref, f32[1,1,128,128]{3,2,1,0:T(8,128)S(1)} %copy-done.2), custom_call_target="tpu_custom_call" | custom-call | tf_op jit(solution)/shard_map/inverse/pallas_call | solution.py:182
  149.2 20.7 %all-gather = bf16[640,128]{1,0:T(8,128)(2,1)} all-gather(bf16[80,128]{1,0:T(8,128)(2,1)S(1)} %get-tuple-element.8), channel_id=2, replica_groups=mesh['z'=8,'y'=4,'x'=4,'c'=2] {'z'}, dimensions={0}, use_global_device_ids=true | all-gather | bytes 184320 | tf_op jit(solution)/shard_map/all_gather | solution.py:248
  169.9 0.0 all-gather.3.cloned.1.call-update
  170.0 55.0 %all-gather.3.cloned.1.call-done.inv_ref = bf16[256,80,128]{2,1,0:T(8,128)(2,1)} async-done(((bf16[8,80,128]{2,1,0:T(8,128)(2,1)}), bf16[256,80,128]{2,1,0:T(8,128)(2,1)}) %all-gather.3.cloned.1.call-update) | async-done | bytes 5242896 | tf_op jit(solution)/shard_map/all_gather | solution.py:249
  224.9 0.0 copy-done.1
  224.9 4.5 %final.1 = bf16[768,768]{1,0:T(8,128)(2,1)} custom-call(s32[240]{0:T(256)S(1)} %select_reduce_fusion.slot_ref, s32[4]{0:T(128)S(1)} %pad_add_fusion.me_ref, bf16[256,80,128]{2,1,0:T(8,128)(2,1)} %all-gather.3.cloned.1.call-done.inv_ref, bf16[768,768]{1,0:T(8,128)(2,1)S(1)} %copy-done.1), custom_call_target="tpu_custom_call" | custom-call | tf_op jit(solution)/shard_map/final/pallas_call | solution.py:216
Async XLA Ops:
  7.2 217.8 %all-gather.3.cloned.1.call-start = ((), (), s32[]{:S(2)}) async-start(), calls=%async_computation.2 | async-start | bytes 5406720 | tf_op jit(solution)/shard_map/all_gather | solution.py:249
  8.7 1.4 copy-start
  79.6 7.3 %collective-permute-start = (bf16[8448,128]{1,0:T(8,128)(2,1)}, bf16[8448,128]{1,0:T(8,128)(2,1)S(1)}, u32[]{:S(2)}, u32[]{:S(2)}) collective-permute-start(bf16[8448,128]{1,0:T(8,128)(2,1)} %get-tuple-element.7), channel_id=1, source_target_pairs={{0,1},{1,0},{2,3},{3,2},{4,5},{5,4},{6,7},{7,6},{8,9},{9,8},{10,11... | collective-permute-start | bytes 6488072 | tf_op jit(solution)/shard_map/ppermute | solution.py:242
  120.6 16.8 %copy-start.2 = (f32[1,1,128,128]{3,2,1,0:T(8,128)S(1)}, f32[1,1,128,128]{3,2,1,0:T(8,128)}, u32[]{:S(2)}) copy-start(f32[1,1,128,128]{3,2,1,0:T(8,128)} %old_ref.1) | copy-start | bytes 196612
  120.6 104.3 %copy-start.1 = (bf16[768,768]{1,0:T(8,128)(2,1)S(1)}, bf16[768,768]{1,0:T(8,128)(2,1)}, u32[]{:S(2)}) copy-start(bf16[768,768]{1,0:T(8,128)(2,1)} %weight_ref.1) | copy-start | bytes 3538948
Sparse Core Ops, SparseCore 0:
  170.1 54.8 all-gather.2

commit v2 on v1

v2 whole, which is shorter than its diff:
```python
import functools

import jax
import jax.numpy as jnp
from jax import lax
from jax.experimental import pallas as pl
from jax.experimental.pallas import tpu as pltpu
from jax.sharding import Mesh, PartitionSpec as P

B = 128
H = B // 2
BF = jnp.bfloat16
F32 = jnp.float32
EXTRA = 16
VMEM_LIMIT = 24 * 1024 * 1024


def iota(shape, dim):
    return lax.broadcasted_iota(jnp.int32, shape, dim)


def pack(sym):
    top = sym[:H, :]
    low = pltpu.roll(sym[H:, :], H, 1)
    row, lane = iota((H, B), 0), iota((H, B), 1)
    half = jnp.where(lane < row, low, top)
    diag = jnp.sum(jnp.where(lane == row, low, 0.0), axis=0, keepdims=True)
    return half, diag


def unpack(half, diag):
    row, lane = iota((H, B), 0), iota((H, B), 1)
    upper = jnp.where(lane >= row, half, 0.0)
    lower = jnp.where(lane < row, half, 0.0)
    lower = jnp.where(lane == row, diag, lower)
    lower = pltpu.roll(lower, H, 1)
    part = jnp.concatenate((upper, lower), axis=0)
    brow, blane = iota((B, B), 0), iota((B, B), 1)
    return part + jnp.where(brow == blane, 0.0, part.T)


def invert(mat):
    rows = 8
    groups = [mat[g * rows : (g + 1) * rows, :] for g in range(B // rows)]
    lane, sub = iota((rows, B), 1), iota((rows, B), 0)
    for k in range(B):
        at, inside = k // rows, k % rows
        own = groups[at]
        scale = 1.0 / own[inside : inside + 1, k : k + 1]
        line = jnp.where(lane[:1] == k, scale, own[inside : inside + 1, :] * scale)
        line = jnp.broadcast_to(line, (rows, B))
        fresh = []
        for g in range(B // rows):
            col = jnp.broadcast_to(groups[g][:, k : k + 1], (rows, B))
            new = jnp.where(lane == k, 0.0, groups[g]) - col * line
            if g == at:
                new = jnp.where(sub == inside, line, new)
            fresh.append(new)
        groups = fresh
    return jnp.concatenate(groups, axis=0)


def gram_kernel(away, table_ref, me_ref, acts_ref, grads_ref, out_ref):
    live, core = me_ref[0], me_ref[1]
    want = 1 - core if away else core
    in_blocks = acts_ref.shape[1] // B
    out_blocks = grads_ref.shape[1] // B
    group_rows = 8 * H + EXTRA
    unroll = 2

    @pl.loop(0, 16 // unroll)
    def _(trip):
        for inner in range(unroll):
            group = trip * unroll + inner
            base = pl.multiple_of(group * group_rows, 16)
            diags = jnp.zeros((8, B), F32)
            for row in range(8):
                which = table_ref[(group * 2 + want) * 8 + row]
                filled = jnp.where(which >= 0, live, 0)
                first = pl.multiple_of(jnp.clip(which, 0, in_blocks - 1) * B, B)
                second = pl.multiple_of(jnp.clip(which - in_blocks, 0, out_blocks - 1) * B, B)
                x = jnp.where(which < in_blocks, acts_ref[:, pl.ds(first, B)], grads_ref[:, pl.ds(second, B)])
                x = jnp.where(iota(x.shape, 0) < filled, x, jnp.zeros_like(x))
                gram = lax.dot_general(x, x, (((0,), (0,)), ((), ())), preferred_element_type=F32)
                half, diag = pack(gram)
                out_ref[pl.ds(base + row * H, H), :] = half.astype(BF)
                diags = jnp.where(iota((8, B), 0) == row, diag, diags)
            count = jnp.full((8, B), live, jnp.int32).astype(F32)
            out_ref[pl.ds(base + 8 * H, EXTRA), :] = jnp.concatenate((diags, count), axis=0).astype(BF)


def grams(away, table, me, acts, grads_out):
    smem = pl.BlockSpec(memory_space=pltpu.SMEM)
    vmem = pl.BlockSpec(memory_space=pltpu.VMEM)
    return pl.pallas_call(
        functools.partial(gram_kernel, away),
        out_shape=jax.ShapeDtypeStruct((16 * (8 * H + EXTRA), B), BF),
        in_specs=[smem, smem, vmem, vmem],
        out_specs=vmem,
        compiler_params=pltpu.CompilerParams(vmem_limit_bytes=VMEM_LIMIT),
        cost_estimate=pl.CostEstimate(flops=2 * 128 * B**3, bytes_accessed=16 * 2**20, transcendentals=0),
        name="grams_away" if away else "grams_own",
    )(table, me, acts, grads_out)


def section_kernel(parts_ref, out_ref):
    for row in range(8):
        total = parts_ref[0, row * H : (row + 1) * H, :].astype(F32)
        for g in range(1, 16):
            total += parts_ref[g, row * H : (row + 1) * H, :].astype(F32)
        out_ref[row, :H, :] = total.astype(BF)
    extra = parts_ref[0, 8 * H :, :].astype(F32)
    for g in range(1, 16):
        extra += parts_ref[g, 8 * H :, :].astype(F32)
    count = extra[8:, :]
    high = jnp.floor(count * (1.0 / 256.0))
    low = count - 256.0 * high
    sub = iota((8, B), 0)
    for row in range(8):
        first = jnp.where(sub == 0, jnp.broadcast_to(extra[row : row + 1, :], (8, B)), jnp.where(sub == 1, high, low))
        out_ref[row, H:, :] = jnp.concatenate((first, jnp.zeros_like(first)), axis=0).astype(BF)


def section_sum(parts):
    return pl.pallas_call(
        section_kernel,
        out_shape=jax.ShapeDtypeStruct((8, H + EXTRA, B), BF),
        compiler_params=pltpu.CompilerParams(vmem_limit_bytes=VMEM_LIMIT),
        name="section_sum",
    )(parts)


def inverse_kernel(parts_ref, old_ref, cov_ref, out_ref):
    half = parts_ref[0, :H, :].astype(F32)
    extra = parts_ref[0, H:, :].astype(F32)
    for s in range(1, 8):
        half += parts_ref[s, :H, :].astype(F32)
        extra += parts_ref[s, H:, :].astype(F32)
    total = extra[1:2, :] * 256.0 + extra[2:3, :]
    gram = unpack(half, extra[:1, :])
    cov = 0.8 * old_ref[0, 0] + 0.2 * gram / total
    cov_ref[0, 0] = cov
    eye = jnp.where(iota((B, B), 0) == iota((B, B), 1), 0.1, 0.0)
    inv_half, inv_diag = pack(invert(cov + eye))
    packed = jnp.concatenate((inv_half, jnp.broadcast_to(inv_diag, (EXTRA, B))), axis=0).astype(BF)
    for g in range(16):
        out_ref[g] = packed


def inverse(parts, old_cov):
    return pl.pallas_call(
        inverse_kernel,
        out_shape=(
            jax.ShapeDtypeStruct(old_cov.shape, F32),
            jax.ShapeDtypeStruct((16, H + EXTRA, B), BF),
        ),
        compiler_params=pltpu.CompilerParams(vmem_limit_bytes=VMEM_LIMIT),
        name="inverse",
    )(parts, old_cov)


def route_kernel(in_blocks, row_blocks, col_blocks, slot_ref, me_ref, mine_ref, other_ref, out_ref):
    core, owner = me_ref[1], me_ref[3]
    share = row_blocks // 2
    sub = iota((EXTRA, B), 0)

    def packed(which):
        holder = slot_ref[which] // 8
        same = (holder % 2) == core
        return jnp.where(same, mine_ref[holder // 2], other_ref[holder // 2])

    cols = []
    col_diags = jnp.zeros((EXTRA, B), F32)
    for j in range(col_blocks):
        block = packed(in_blocks + owner * col_blocks + j)
        cols.append(block[:H, :])
        col_diags = jnp.where(sub == j, block[H:, :].astype(F32), col_diags)
    for section in range(8):
        diags = col_diags
        for j in range(col_blocks):
            out_ref[section, j * H : (j + 1) * H, :] = cols[j]
        for i in range(share):
            block = packed(section * row_blocks + core * share + i)
            at = (col_blocks + i) * H
            out_ref[section, at : at + H, :] = block[:H, :]
            diags = jnp.where(sub == col_blocks + i, block[H:, :].astype(F32), diags)
        out_ref[section, (col_blocks + share) * H :, :] = diags.astype(BF)


def route(slot_of, me, mine, other, in_blocks, row_blocks, col_blocks):
    smem = pl.BlockSpec(memory_space=pltpu.SMEM)
    vmem = pl.BlockSpec(memory_space=pltpu.VMEM)
    rows = (col_blocks + row_blocks // 2) * H + EXTRA
    return pl.pallas_call(
        functools.partial(route_kernel, in_blocks, row_blocks, col_blocks),
        out_shape=jax.ShapeDtypeStruct((8, rows, B), BF),
        in_specs=[smem, smem, vmem, vmem],
        out_specs=vmem,
        compiler_params=pltpu.CompilerParams(vmem_limit_bytes=VMEM_LIMIT),
        name="route",
    )(slot_of, me, mine, other)


def pick_kernel(row_blocks, col_blocks, slot_ref, me_ref, got_ref, out_ref):
    core, section = me_ref[1], me_ref[2]
    share = row_blocks // 2
    sub = iota((EXTRA, B), 0)
    for i in range(share):
        source = slot_ref[section * row_blocks + core * share + i] % 8
        at = (col_blocks + i) * H
        out_ref[i, :H, :] = got_ref[source, at : at + H, :]
        diags = got_ref[source, (col_blocks + share) * H :, :].astype(F32)
        diag = jnp.sum(jnp.where(sub == col_blocks + i, diags, 0.0), axis=0, keepdims=True)
        out_ref[i, H:, :] = jnp.broadcast_to(diag, (EXTRA, B)).astype(BF)


def pick(slot_of, me, got, row_blocks, col_blocks):
    smem = pl.BlockSpec(memory_space=pltpu.SMEM)
    vmem = pl.BlockSpec(memory_space=pltpu.VMEM)
    return pl.pallas_call(
        functools.partial(pick_kernel, row_blocks, col_blocks),
        out_shape=jax.ShapeDtypeStruct((row_blocks // 2, H + EXTRA, B), BF),
        in_specs=[smem, smem, vmem],
        out_specs=vmem,
        compiler_params=pltpu.CompilerParams(vmem_limit_bytes=VMEM_LIMIT),
        name="pick",
    )(slot_of, me, got)


def final_kernel(in_blocks, slot_ref, me_ref, got_ref, mine_ref, other_ref, weight_ref, out_ref, left_ref):
    core, owner = me_ref[1], me_ref[3]
    row_blocks = weight_ref.shape[0] // B
    col_blocks = weight_ref.shape[1] // B
    share = row_blocks // 2
    sub = iota((EXTRA, B), 0)
    for i in range(row_blocks):
        same = core == i // share
        packed = jnp.where(same, mine_ref[i % share], other_ref[i % share]).astype(F32)
        block = unpack(packed[:H, :], packed[H : H + 1, :]).astype(BF)
        rows = slice(i * B, (i + 1) * B)
        left = jnp.dot(block, weight_ref[rows, :], preferred_element_type=F32)
        left_ref[rows, :] = left.astype(BF)
    for j in range(col_blocks):
        source = slot_ref[in_blocks + owner * col_blocks + j] % 8
        half = got_ref[source, j * H : (j + 1) * H, :].astype(F32)
        diags = got_ref[source, (col_blocks + share) * H :, :].astype(F32)
        diag = jnp.sum(jnp.where(sub == j, diags, 0.0), axis=0, keepdims=True)
        block = unpack(half, diag).astype(BF)
        cols = slice(j * B, (j + 1) * B)
        right = jnp.dot(left_ref[:, cols], block, preferred_element_type=F32)
        out_ref[:, cols] = right.astype(BF)


def final(slot_of, me, got, mine, other, weight_grad, in_blocks):
    smem = pl.BlockSpec(memory_space=pltpu.SMEM)
    vmem = pl.BlockSpec(memory_space=pltpu.VMEM)
    return pl.pallas_call(
        functools.partial(final_kernel, in_blocks),
        out_shape=jax.ShapeDtypeStruct(weight_grad.shape, BF),
        in_specs=[smem, smem, vmem, vmem, vmem, vmem],
        out_specs=vmem,
        scratch_shapes=[pltpu.VMEM(weight_grad.shape, BF)],
        compiler_params=pltpu.CompilerParams(vmem_limit_bytes=VMEM_LIMIT),
        name="final",
    )(slot_of, me, got, mine, other, weight_grad)


def locate(slot_table, count):
    slot_ids = jnp.arange(slot_table.shape[0], dtype=jnp.int32)
    hits = slot_table[None, :] == jnp.arange(count, dtype=jnp.int32)[:, None]
    return jnp.sum(jnp.where(hits, slot_ids[None, :], 0), axis=1)


def on_device(acts, grads_out, weight_grad, slot_table, row_counts, old_cov):
    in_blocks = acts.shape[1] // B
    out_blocks = grads_out.shape[1] // B
    core = lax.axis_index("c")
    section = lax.axis_index("z")
    owner = (lax.axis_index("y") * 4 + lax.axis_index("x")) * 2 + core
    slot_of = locate(slot_table, in_blocks + out_blocks)
    me = jnp.stack((row_counts[0], core, section, owner)).astype(jnp.int32)
    swap = [(0, 1), (1, 0)]
    away = grams(True, slot_table, me, acts, grads_out)
    got = lax.ppermute(away, "c", swap)
    own = grams(False, slot_table, me, acts, grads_out)
    chip = (own.astype(F32) + got.astype(F32)).astype(BF)
    chip = chip.reshape(16, -1, B)
    plane = lax.all_to_all(chip, ("y", "x"), split_axis=0, concat_axis=0, tiled=True)
    share = lax.all_to_all(section_sum(plane), "z", split_axis=0, concat_axis=0, tiled=True)
    new_cov, inv = inverse(share, old_cov)
    mine = lax.all_to_all(inv, ("y", "x"), split_axis=0, concat_axis=0, tiled=True)
    other = lax.ppermute(mine, "c", swap)
    row_blocks = weight_grad.shape[0] // B
    col_blocks = weight_grad.shape[1] // B
    routed = route(slot_of, me, mine, other, in_blocks, row_blocks, col_blocks)
    got = lax.all_to_all(routed, "z", split_axis=0, concat_axis=0, tiled=True)
    mine = pick(slot_of, me, got, row_blocks, col_blocks)
    other = lax.ppermute(mine, "c", swap)
    return final(slot_of, me, got, mine, other, weight_grad, in_blocks), new_cov


def solution(mesh):
    wide = Mesh(mesh.devices.reshape(8, 4, 4, 2), ("z", "y", "x", "c"))
    dp = ("y", "x", "c")
    in_specs = (
        P(("z",) + dp, None),
        P(("z",) + dp, None),
        P("z", dp),
        P(),
        P(("z",) + dp),
        P(dp, "z", None, None),
    )
    out_specs = (P("z", dp), P(dp, "z", None, None))
    return jax.shard_map(
        on_device, mesh=wide, in_specs=in_specs, out_specs=out_specs, check_vma=False
    )
```

time: 237 us -> 140 us (0.59)
  Pallas kernels: 86.1 us -> 26.4 us
  waiting for transfers between devices: 59.1 us -> 2.04 us
  blocking collectives: 70.3 us -> 96.2 us
  between operations: 14.7 us -> 1.34 us
  starting transfers between devices: 3.27 us -> 7.79 us
  local copies, waits for them, and re-layouts: 1.42 us -> 4.89 us
    pallas_call x1 -> x4, Pallas kernels: 69.5 us -> 11.8 us  [the longest x2 10.2 us: grams(): pl.pallas_call(functools.partial(gram_kernel, away), out_shape=jax.ShapeD...]
    all_gather x1 -> x0, waiting for transfers between devices: 55 us -> none  [on_device(): inverses = lax.all_gather(column, ('y', 'x', 'c'), axis=0, tiled=True)]
    all_to_all x0 -> x2, blocking collectives: none -> 46.1 us  [the longest x1 35.3 us: on_device(): got = lax.all_to_all(routed, 'z', split_axis=0, concat_axis=0, tiled=True)]
    all_gather x1 -> x0, blocking collectives: 20.7 us -> none  [on_device(): column = lax.all_gather(inv, 'z', axis=0)]
    ppermute x1 -> x3, starting transfers between devices: 3.23 us -> 7.79 us  [the longest x2 4.46 us: on_device(): other = lax.ppermute(mine, 'c', swap)]
    unnamed x6 -> x12, local copies, waits for them, and re-layouts: 1.42 us -> 4.89 us
  transfers between devices with their start and end apart: 2 -> 3, of which waited for: 2 -> 2; matrix products, arithmetic and copies ran while one was open for 0% -> 0% of each run, Pallas kernels for 0% -> 4%
where the time goes in v2:
time: 140 us; the launch traced here: 139 us
  blocking collectives  96.2 us (69%)
  Pallas kernels  26.4 us (19%)
  starting transfers between devices  7.79 us (6%)
  local copies, waits for them, and re-layouts  4.89 us (3%)
  waiting for transfers between devices  2.04 us (1%)
    all_to_all x1, blocking collectives, on_device(): got = lax.all_to_all(routed, 'z', split_axis=0, concat_axis=0, tiled=True)  35.3 us
    all_to_all x1, blocking collectives, on_device(): lax.all_to_all(chip, ('y', 'x'), split_axis=0, concat_axis=0, tiled=True)  33.8 us
    all_to_all x1, blocking collectives, on_device(): lax.all_to_all(section_sum(plane), 'z', split_axis=0, concat_axis=0, tile...  16.4 us
    pallas_call x1, Pallas kernels, inverse(): pl.pallas_call(inverse_kernel, out_shape=(jax.ShapeDtypeStruct(old_cov.sh...  11.8 us
    all_to_all x1, blocking collectives, on_device(): lax.all_to_all(inv, ('y', 'x'), split_axis=0, concat_axis=0, tiled=True)  10.9 us
    pallas_call x2, Pallas kernels, grams(): pl.pallas_call(functools.partial(gram_kernel, away), out_shape=jax.ShapeD...  10.2 us
    unnamed x12, local copies, waits for them, and re-layouts  4.89 us
    ppermute x2, starting transfers between devices, on_device(): other = lax.ppermute(mine, 'c', swap)  4.46 us
  transfers between devices with their start and end apart: 3, of which 2 were waited for; matrix products, arithmetic and copies ran while one was open for 0% of the time, Pallas kernels for 4%

profile of v2, /device:TPU:1, one launch (start us, length us, event | category | flops | bytes accessed | tf_op | source)
XLA Modules:
  0.0 139.5 jit_solution(11600475849184501460)
XLA Ops:
  1.3 0.1 pad_add_fusion.me_ref
  1.4 2.8 %copy-done = bf16[128,24576]{1,0:T(8,128)(2,1)S(1)} copy-done((bf16[128,24576]{1,0:T(8,128)(2,1)S(1)}, bf16[128,24576]{1,0:T(8,128)(2,1)}, u32[]{:S(2)}) %copy-start) | copy-done | bytes 6291480
  4.2 1.4 %copy-done.1 = bf16[128,6144]{1,0:T(8,128)(2,1)S(1)} copy-done((bf16[128,6144]{1,0:T(8,128)(2,1)S(1)}, bf16[128,6144]{1,0:T(8,128)(2,1)}, u32[]{:S(2)}) %copy-start.1) | copy-done | bytes 1572888
  5.6 0.7 copy-done.4
  6.2 5.1 %grams_away.1 = bf16[8448,128]{1,0:T(8,128)(2,1)S(1)} custom-call(s32[256]{0:T(256)S(1)} %copy-done.4, s32[4]{0:T(128)S(1)} %pad_add_fusion.me_ref, bf16[128,6144]{1,0:T(8,128)(2,1)S(1)} %copy-done.1, bf16[128,24576]{1,0:T(8,128)(2,1)S(1)} %copy-done), custom_call_target="tpu_custom_call" | custom-call | flops 536870912 | bytes 16777216 | tf_op jit(solution)/shard_map/grams_away/pallas_call | solution.py:95
  11.3 3.3 %collective-permute-start = (bf16[8448,128]{1,0:T(8,128)(2,1)S(1)}, bf16[8448,128]{1,0:T(8,128)(2,1)S(1)}, u32[]{:S(2)}, u32[]{:S(2)}) collective-permute-start(bf16[8448,128]{1,0:T(8,128)(2,1)S(1)} %grams_away.1), channel_id=1, source_target_pairs={{0,1},{1,0},{2,3},{3,2},{4,5},{5,4},{6,7},{7,6},{8,9},{9,8},{10,11... | collective-permute-start | bytes 6488072 | tf_op jit(solution)/shard_map/ppermute | solution.py:284
  14.7 5.1 %grams_own.1 = bf16[8448,128]{1,0:T(8,128)(2,1)S(1)} custom-call(s32[256]{0:T(256)S(1)} %copy-done.4, s32[4]{0:T(128)S(1)} %pad_add_fusion.me_ref, bf16[128,6144]{1,0:T(8,128)(2,1)S(1)} %copy-done.1, bf16[128,24576]{1,0:T(8,128)(2,1)S(1)} %copy-done), custom_call_target="tpu_custom_call" | custom-call | flops 536870912 | bytes 16777216 | tf_op jit(solution)/shard_map/grams_own/pallas_call | solution.py:95
  19.7 0.0 collective-permute-done
  19.8 0.6 add_convert_fusion
  20.4 33.8 %all_to_all.20.parts_ref = bf16[16,528,128]{2,1,0:T(8,128)(2,1)S(1)} all-to-all(bf16[16,528,128]{2,1,0:T(8,128)(2,1)S(1)} %bitcast.4), channel_id=1, replica_groups=mesh['z'=8,'y'=4,'x'=4,'c'=2] {'y','x'}, dimensions={0} | all-to-all | bytes 4325376 | tf_op jit(solution)/shard_map/all_to_all | solution.py:288
  54.1 0.3 section_sum.1
  54.4 16.4 %all_to_all.21.parts_ref = bf16[8,80,128]{2,1,0:T(8,128)(2,1)S(1)} all-to-all(bf16[8,80,128]{2,1,0:T(8,128)(2,1)S(1)} %section_sum.1), channel_id=1, replica_groups=mesh['z'=8,'y'=4,'x'=4,'c'=2] {'z'}, dimensions={0} | all-to-all | bytes 327680 | tf_op jit(solution)/shard_map/all_to_all | solution.py:289
  70.8 11.8 %inverse.1 = (f32[1,1,128,128]{3,2,1,0:T(8,128)}, bf16[16,80,128]{2,1,0:T(8,128)(2,1)S(1)}) custom-call(bf16[8,80,128]{2,1,0:T(8,128)(2,1)S(1)} %all_to_all.21.parts_ref, f32[1,1,128,128]{3,2,1,0:T(8,128)S(1)} %copy-done.3), custom_call_target="tpu_custom_call" | custom-call | tf_op jit(solution)/shard_map/inverse/pallas_call | solution.py:151
  82.6 10.9 %all_to_all.22.mine_ref = bf16[16,80,128]{2,1,0:T(8,128)(2,1)S(1)} all-to-all(bf16[16,80,128]{2,1,0:T(8,128)(2,1)S(1)} %get-tuple-element.4), channel_id=1, replica_groups=mesh['z'=8,'y'=4,'x'=4,'c'=2] {'y','x'}, dimensions={0} | all-to-all | bytes 655360 | tf_op jit(solution)/shard_map/all_to_all | solution.py:291
  93.5 3.9 %collective-permute-start.1 = (bf16[16,80,128]{2,1,0:T(8,128)(2,1)S(1)}, bf16[16,80,128]{2,1,0:T(8,128)(2,1)S(1)}, u32[]{:S(2)}, u32[]{:S(2)}) collective-permute-start(bf16[16,80,128]{2,1,0:T(8,128)(2,1)S(1)} %all_to_all.22.mine_ref), channel_id=1, source_target_pairs={{0,1},{1,0},{2,3},{3,2},{4,5},{5,4},{6,7},{7,6},{8,9},{9,8},{10,11... | collective-permute-start | bytes 983048 | tf_op jit(solution)/shard_map/ppermute | solution.py:292
  97.4 0.1 select_reduce_fusion.slot_ref
  97.5 1.1 collective-permute-done.1.other_ref
  98.6 1.0 route.1
  99.7 0.0 copy-start.2
  99.7 35.3 %all_to_all.23.got_ref = bf16[8,592,128]{2,1,0:T(8,128)(2,1)S(1)} all-to-all(bf16[8,592,128]{2,1,0:T(8,128)(2,1)S(1)} %route.1), channel_id=1, replica_groups=mesh['z'=8,'y'=4,'x'=4,'c'=2] {'z'}, dimensions={0} | all-to-all | bytes 2424832 | tf_op jit(solution)/shard_map/all_to_all | solution.py:296
  134.9 0.6 pick.1.mine_ref
  135.5 0.6 collective-permute-start.2
  136.1 0.9 collective-permute-done.2.other_ref
  137.0 2.5 %final.1 = bf16[768,768]{1,0:T(8,128)(2,1)} custom-call(s32[240]{0:T(256)S(1)} %select_reduce_fusion.slot_ref, s32[4]{0:T(128)S(1)} %pad_add_fusion.me_ref, bf16[8,592,128]{2,1,0:T(8,128)(2,1)S(1)} %all_to_all.23.got_ref, bf16[3,80,128]{2,1,0:T(8,128)(2,1)S(1)} %pick.1.mine_ref, bf16[3,80,128]{2,1,0:T(8,128)(2,1)S(1)} %collective-permute-done.2.other_ref, ...), custom_call_target="tpu_custom_call" | custom-call | tf_op jit(solution)/shard_map/final/pallas_call | solution.py:257
  (8 shorter events, 0.0 us)
Async XLA Ops:
  1.4 2.8 %copy-start = (bf16[128,24576]{1,0:T(8,128)(2,1)S(1)}, bf16[128,24576]{1,0:T(8,128)(2,1)}, u32[]{:S(2)}) copy-start(bf16[128,24576]{1,0:T(8,128)(2,1)} %grads_ref.3) | copy-start | bytes 18874372
  4.1 1.4 %copy-start.1 = (bf16[128,6144]{1,0:T(8,128)(2,1)S(1)}, bf16[128,6144]{1,0:T(8,128)(2,1)}, u32[]{:S(2)}) copy-start(bf16[128,6144]{1,0:T(8,128)(2,1)} %acts_ref.3) | copy-start | bytes 4718596
  5.6 0.7 copy-start.4
  11.3 8.4 %collective-permute-start = (bf16[8448,128]{1,0:T(8,128)(2,1)S(1)}, bf16[8448,128]{1,0:T(8,128)(2,1)S(1)}, u32[]{:S(2)}, u32[]{:S(2)}) collective-permute-start(bf16[8448,128]{1,0:T(8,128)(2,1)S(1)} %grams_away.1), channel_id=1, source_target_pairs={{0,1},{1,0},{2,3},{3,2},{4,5},{5,4},{6,7},{7,6},{8,9},{9,8},{10,11... | collective-permute-start | bytes 6488072 | tf_op jit(solution)/shard_map/ppermute | solution.py:284
  54.1 16.7 %copy-start.3 = (f32[1,1,128,128]{3,2,1,0:T(8,128)S(1)}, f32[1,1,128,128]{3,2,1,0:T(8,128)}, u32[]{:S(2)}) copy-start(f32[1,1,128,128]{3,2,1,0:T(8,128)} %old_ref.1) | copy-start | bytes 196612
  54.1 43.2 %copy-start.5 = (s32[256]{0:T(256)S(1)}, s32[256]{0:T(256)}, u32[]{:S(2)}) copy-start(s32[256]{0:T(256)} %table_ref.3) | copy-start | bytes 3076
  93.5 5.2 %collective-permute-start.1 = (bf16[16,80,128]{2,1,0:T(8,128)(2,1)S(1)}, bf16[16,80,128]{2,1,0:T(8,128)(2,1)S(1)}, u32[]{:S(2)}, u32[]{:S(2)}) collective-permute-start(bf16[16,80,128]{2,1,0:T(8,128)(2,1)S(1)} %all_to_all.22.mine_ref), channel_id=1, source_target_pairs={{0,1},{1,0},{2,3},{3,2},{4,5},{5,4},{6,7},{7,6},{8,9},{9,8},{10,11... | collective-permute-start | bytes 983048 | tf_op jit(solution)/shard_map/ppermute | solution.py:292
  99.7 37.3 %copy-start.2 = (bf16[768,768]{1,0:T(8,128)(2,1)S(1)}, bf16[768,768]{1,0:T(8,128)(2,1)}, u32[]{:S(2)}) copy-start(bf16[768,768]{1,0:T(8,128)(2,1)} %weight_ref.1) | copy-start | bytes 3538948
  135.5 1.5 %collective-permute-start.2 = (bf16[3,80,128]{2,1,0:T(8,128)(2,1)S(1)}, bf16[3,80,128]{2,1,0:T(8,128)(2,1)S(1)}, u32[]{:S(2)}, u32[]{:S(2)}) collective-permute-start(bf16[3,80,128]{2,1,0:T(8,128)(2,1)S(1)} %pick.1.mine_ref), channel_id=1, source_target_pairs={{0,1},{1,0},{2,3},{3,2},{4,5},{5,4},{6,7},{7,6},{8,9},{9,8},{10,11... | collective-permute-start | bytes 184328 | tf_op jit(solution)/shard_map/ppermute | solution.py:298

commit v3 on v2

v3 whole, which is shorter than its diff:
```python
import functools

import jax
import jax.numpy as jnp
import numpy as np
from jax import lax
from jax.experimental import pallas as pl
from jax.experimental.pallas import tpu as pltpu
from jax.sharding import Mesh, PartitionSpec as P

B = 128
H = B // 2
BF = jnp.bfloat16
F32 = jnp.float32
EXTRA = 16
VMEM_LIMIT = 24 * 1024 * 1024


def iota(shape, dim):
    return lax.broadcasted_iota(jnp.int32, shape, dim)


def pack(sym):
    top = sym[:H, :]
    low = pltpu.roll(sym[H:, :], H, 1)
    row, lane = iota((H, B), 0), iota((H, B), 1)
    half = jnp.where(lane < row, low, top)
    diag = jnp.sum(jnp.where(lane == row, low, 0.0), axis=0, keepdims=True)
    return half, diag


def unpack(half, diag):
    row, lane = iota((H, B), 0), iota((H, B), 1)
    upper = jnp.where(lane >= row, half, 0.0)
    lower = jnp.where(lane < row, half, 0.0)
    lower = jnp.where(lane == row, diag, lower)
    lower = pltpu.roll(lower, H, 1)
    part = jnp.concatenate((upper, lower), axis=0)
    brow, blane = iota((B, B), 0), iota((B, B), 1)
    return part + jnp.where(brow == blane, 0.0, part.T)


def eliminate(groups, k, m, solve):
    rows = 8
    lane, sub = iota((rows, B), 1), iota((rows, B), 0)
    at, inside = k // rows, k % rows
    spread = lambda v: jnp.broadcast_to(v, (rows, B))
    cols = [[spread(g[:, k + i : k + i + 1]) for g in groups] for i in range(m)]
    pivot = [[spread(cols[j][at][inside + i : inside + i + 1, :]) for j in range(m)] for i in range(m)]
    inv = solve(pivot)
    lines = [spread(groups[at][inside + i : inside + i + 1, :]) for i in range(m)]
    fresh_lines = []
    for i in range(m):
        line = inv[i][0] * lines[0]
        for j in range(1, m):
            line = line + inv[i][j] * lines[j]
        for j in range(m):
            line = jnp.where(lane == k + j, inv[i][j], line)
        fresh_lines.append(line)
    out = []
    inner = (lane >= k) & (lane < k + m)
    for g in range(B // rows):
        new = jnp.where(inner, 0.0, groups[g])
        for i in range(m):
            new = new - cols[i][g] * fresh_lines[i]
        if g == at:
            for i in range(m):
                new = jnp.where(sub == inside + i, fresh_lines[i], new)
        out.append(new)
    return out


def solve2(p):
    a, b, c = p[0][0], p[0][1], p[1][1]
    scale = 1.0 / (a * c - b * b)
    off = -b * scale
    return [[c * scale, off], [off, a * scale]]


def solve4(p):
    e = solve2([p[0][:2], p[1][:2]])
    f = [row[2:] for row in p[:2]]
    m = [[e[i][0] * f[0][j] + e[i][1] * f[1][j] for j in range(2)] for i in range(2)]
    s = [[p[2 + i][2 + j] - (f[0][i] * m[0][j] + f[1][i] * m[1][j]) for j in range(2)] for i in range(2)]
    si = solve2(s)
    x = [[m[i][0] * si[0][j] + m[i][1] * si[1][j] for j in range(2)] for i in range(2)]
    top = [[e[i][j] + x[i][0] * m[j][0] + x[i][1] * m[j][1] for j in range(2)] + [-x[i][0], -x[i][1]] for i in range(2)]
    low = [[-x[0][i], -x[1][i]] + si[i] for i in range(2)]
    return top + low


def invert(mat):
    groups = [mat[g * 8 : (g + 1) * 8, :] for g in range(B // 8)]
    for k in range(0, B, 4):
        groups = eliminate(groups, k, 4, solve4)
    return jnp.concatenate(groups, axis=0)


def gram_kernel(away, table_ref, me_ref, acts_ref, grads_ref, out_ref):
    live, core = me_ref[0], me_ref[1]
    want = 1 - core if away else core
    in_blocks = acts_ref.shape[1] // B
    out_blocks = grads_ref.shape[1] // B
    group_rows = 8 * H + EXTRA
    unroll = 2

    @pl.loop(0, 16 // unroll)
    def _(trip):
        for inner in range(unroll):
            group = trip * unroll + inner
            base = pl.multiple_of(group * group_rows, 16)
            diags = jnp.zeros((8, B), F32)
            for row in range(8):
                which = table_ref[(group * 2 + want) * 8 + row]
                filled = jnp.where(which >= 0, live, 0)
                first = pl.multiple_of(jnp.clip(which, 0, in_blocks - 1) * B, B)
                second = pl.multiple_of(jnp.clip(which - in_blocks, 0, out_blocks - 1) * B, B)
                x = jnp.where(which < in_blocks, acts_ref[:, pl.ds(first, B)], grads_ref[:, pl.ds(second, B)])
                x = jnp.where(iota(x.shape, 0) < filled, x, jnp.zeros_like(x))
                gram = lax.dot_general(x, x, (((0,), (0,)), ((), ())), preferred_element_type=F32)
                half, diag = pack(gram)
                out_ref[pl.ds(base + row * H, H), :] = half.astype(BF)
                diags = jnp.where(iota((8, B), 0) == row, diag, diags)
            count = jnp.full((8, B), live, jnp.int32).astype(F32)
            out_ref[pl.ds(base + 8 * H, EXTRA), :] = jnp.concatenate((diags, count), axis=0).astype(BF)


def grams(away, table, me, acts, grads_out):
    smem = pl.BlockSpec(memory_space=pltpu.SMEM)
    vmem = pl.BlockSpec(memory_space=pltpu.VMEM)
    return pl.pallas_call(
        functools.partial(gram_kernel, away),
        out_shape=jax.ShapeDtypeStruct((16 * (8 * H + EXTRA), B), BF),
        in_specs=[smem, smem, vmem, vmem],
        out_specs=vmem,
        compiler_params=pltpu.CompilerParams(vmem_limit_bytes=VMEM_LIMIT),
        cost_estimate=pl.CostEstimate(flops=2 * 128 * B**3, bytes_accessed=16 * 2**20, transcendentals=0),
        name="grams_away" if away else "grams_own",
    )(table, me, acts, grads_out)


def home_table():
    table = np.full((16, 2, 8), -1, np.int32)
    for chip in range(16):
        y, x = divmod(chip, 4)
        for core in range(2):
            at = 48 + 6 * (chip * 2 + core)
            for section in range(8):
                if section % 4 != x:
                    table[chip, core, section] = at
                    at += 1
                elif y < 3:
                    table[chip, core, section] = 6 * section + 2 * y + core
    return table.reshape(-1)


def home_of(table, count):
    places = np.zeros((count,), np.int32)
    for place, block in enumerate(table):
        if block >= 0:
            places[block] = place
    return places


SMEM = pl.BlockSpec(memory_space=pltpu.SMEM)
VMEM = pl.BlockSpec(memory_space=pltpu.VMEM)
PARAMS = pltpu.CompilerParams(vmem_limit_bytes=VMEM_LIMIT)


def take_row(rows, at):
    return jnp.sum(jnp.where(iota((EXTRA, B), 0) == at, rows, 0.0), axis=0, keepdims=True)


def stack_rows(rows):
    out = jnp.zeros((EXTRA, B), F32)
    for at, row in enumerate(rows):
        out = jnp.where(iota((EXTRA, B), 0) == at, jnp.broadcast_to(row, (EXTRA, B)), out)
    return out


def split(value):
    high = value.astype(BF).astype(F32)
    return high, value - high


def section_kernel(home_ref, slot_ref, me_ref, parts_ref, old_ref, out_ref):
    owner = me_ref[3]
    extra = parts_ref[0, 8 * H :, :].astype(F32)
    for g in range(1, 16):
        extra += parts_ref[g, 8 * H :, :].astype(F32)
    count = extra[8:9, :]
    count_high = jnp.floor(count * (1.0 / 256.0))
    count_low = count - 256.0 * count_high
    for row in range(8):
        total = parts_ref[0, row * H : (row + 1) * H, :].astype(F32)
        for g in range(1, 16):
            total += parts_ref[g, row * H : (row + 1) * H, :].astype(F32)
        out_ref[row, :H, :] = total.astype(BF)
        block = jnp.maximum(home_ref[owner * 8 + row], 0)
        old_half, old_diag = pack(old_ref[slot_ref[block] // 8])
        high, low = split(old_half)
        out_ref[row, H : 2 * H, :] = high.astype(BF)
        out_ref[row, 2 * H : 3 * H, :] = low.astype(BF)
        high, low = split(old_diag)
        out_ref[row, 3 * H :, :] = stack_rows((extra[row : row + 1, :], count_high, count_low, high, low)).astype(BF)


def section_sum(home, slot_of, me, parts, old_row):
    return pl.pallas_call(
        section_kernel,
        out_shape=jax.ShapeDtypeStruct((8, 3 * H + EXTRA, B), BF),
        in_specs=[SMEM, SMEM, SMEM, VMEM, VMEM],
        out_specs=VMEM,
        compiler_params=PARAMS,
        name="section_sum",
    )(home, slot_of, me, parts, old_row)


def inverse_kernel(home_ref, slot_ref, me_ref, parts_ref, out_ref):
    section, owner = me_ref[2], me_ref[3]
    block = jnp.maximum(home_ref[owner * 8 + section], 0)
    source = slot_ref[block] % 8
    half = parts_ref[0, :H, :].astype(F32)
    extra = parts_ref[0, 3 * H :, :].astype(F32)
    for s in range(1, 8):
        half += parts_ref[s, :H, :].astype(F32)
        extra += parts_ref[s, 3 * H :, :].astype(F32)
    total = extra[1:2, :] * 256.0 + extra[2:3, :]
    gram_half = 0.2 * half / total
    gram_diag = 0.2 * extra[:1, :] / total
    old_half = parts_ref[source, H : 2 * H, :].astype(F32) + parts_ref[source, 2 * H : 3 * H, :].astype(F32)
    old_extra = parts_ref[source, 3 * H :, :].astype(F32)
    cov = unpack(0.8 * old_half + gram_half, 0.8 * (old_extra[3:4, :] + old_extra[4:5, :]) + gram_diag)
    eye = jnp.where(iota((B, B), 0) == iota((B, B), 1), 0.1, 0.0)
    inv_half, inv_diag = pack(invert(cov + eye))
    packed = jnp.concatenate((inv_half, gram_half, stack_rows((inv_diag, gram_diag))), axis=0).astype(BF)
    for s in range(8):
        out_ref[s] = packed


def inverse(home, slot_of, me, parts):
    return pl.pallas_call(
        inverse_kernel,
        out_shape=jax.ShapeDtypeStruct((8, 2 * H + EXTRA, B), BF),
        in_specs=[SMEM, SMEM, SMEM, VMEM],
        out_specs=VMEM,
        compiler_params=PARAMS,
        name="inverse",
    )(home, slot_of, me, parts)


def route_kernel(table_ref, place_ref, me_ref, mine_ref, other_ref, out_ref):
    core, section = me_ref[1], me_ref[2]
    halves, diags = [], []
    for c in range(2):
        packed = jnp.where(core == c, mine_ref[section], other_ref[section])
        halves.append(packed[:H, :])
        diags.append(take_row(packed[2 * H :, :].astype(F32), 0))
    for chip in range(16):
        block = jnp.maximum(table_ref[(chip * 2 + core) * 8 + section], 0)
        place = place_ref[block]
        same = (place // 8) % 2 == core
        at = place % 8
        half = jnp.where(same, mine_ref[at, H : 2 * H, :], other_ref[at, H : 2 * H, :])
        extra = jnp.where(same, mine_ref[at, 2 * H :, :], other_ref[at, 2 * H :, :]).astype(F32)
        out_ref[chip, :H, :] = halves[0]
        out_ref[chip, H : 2 * H, :] = halves[1]
        out_ref[chip, 2 * H : 3 * H, :] = half
        out_ref[chip, 3 * H :, :] = stack_rows((diags[0], diags[1], take_row(extra, 1))).astype(BF)


def route(table, places, me, mine, other):
    return pl.pallas_call(
        route_kernel,
        out_shape=jax.ShapeDtypeStruct((16, 3 * H + EXTRA, B), BF),
        in_specs=[SMEM, SMEM, SMEM, VMEM, VMEM],
        out_specs=VMEM,
        compiler_params=PARAMS,
        name="route",
    )(table, places, me, mine, other)


def final_kernel(table_ref, place_ref, me_ref, plane_ref, column_ref, old_ref, weight_ref, out_ref, cov_ref, left_ref):
    section, owner = me_ref[2], me_ref[3]
    row_blocks = weight_ref.shape[0] // B
    col_blocks = weight_ref.shape[1] // B
    for i in range(row_blocks):
        chip = i // 2 * 4 + section % 4
        half = plane_ref[chip, i % 2 * H : (i % 2 + 1) * H, :].astype(F32)
        diag = take_row(plane_ref[chip, 3 * H :, :].astype(F32), i % 2)
        rows = slice(i * B, (i + 1) * B)
        left = jnp.dot(unpack(half, diag).astype(BF), weight_ref[rows, :], preferred_element_type=F32)
        left_ref[rows, :] = left.astype(BF)
    skipped = (owner // 2) % 4
    for j in range(col_blocks):
        turn, at = j // 3 * 4, j % 3
        home = turn + at + jnp.where(skipped <= at, 1, 0)
        half = column_ref[home, :H, :].astype(F32)
        diag = take_row(column_ref[home, 2 * H :, :].astype(F32), 0)
        cols = slice(j * B, (j + 1) * B)
        right = jnp.dot(left_ref[:, cols], unpack(half, diag).astype(BF), preferred_element_type=F32)
        out_ref[:, cols] = right.astype(BF)
    block = table_ref[owner * 8 + section]
    chip = place_ref[jnp.maximum(block, 0)] // 16
    half = plane_ref[chip, 2 * H : 3 * H, :].astype(F32)
    diag = take_row(plane_ref[chip, 3 * H :, :].astype(F32), 2)
    cov_ref[0, 0] = 0.8 * old_ref[0, 0] + jnp.where(block >= 0, unpack(half, diag), 0.0)


def final(table, places, me, plane, column, old_cov, weight_grad):
    return pl.pallas_call(
        final_kernel,
        out_shape=(
            jax.ShapeDtypeStruct(weight_grad.shape, BF),
            jax.ShapeDtypeStruct(old_cov.shape, F32),
        ),
        in_specs=[SMEM, SMEM, SMEM, VMEM, VMEM, VMEM, VMEM],
        out_specs=(VMEM, VMEM),
        scratch_shapes=[pltpu.VMEM(weight_grad.shape, BF)],
        compiler_params=PARAMS,
        name="final",
    )(table, places, me, plane, column, old_cov, weight_grad)


def locate(slot_table, count):
    slot_ids = jnp.arange(slot_table.shape[0], dtype=jnp.int32)
    hits = slot_table[None, :] == jnp.arange(count, dtype=jnp.int32)[:, None]
    return jnp.sum(jnp.where(hits, slot_ids[None, :], 0), axis=1)


def on_device(acts, grads_out, weight_grad, slot_table, row_counts, old_cov):
    blocks = (acts.shape[1] + grads_out.shape[1]) // B
    plane, swap = ("y", "x"), [(0, 1), (1, 0)]
    exchange = functools.partial(lax.all_to_all, split_axis=0, concat_axis=0, tiled=True)
    old_row = lax.all_gather(old_cov[0, 0], plane + ("c",), axis=0)
    core = lax.axis_index("c")
    section = lax.axis_index("z")
    owner = (lax.axis_index("y") * 4 + lax.axis_index("x")) * 2 + core
    me = jnp.stack((row_counts[0], core, section, owner)).astype(jnp.int32)
    table = home_table()
    home, places = jnp.asarray(table), jnp.asarray(home_of(table, blocks))
    slot_of = locate(slot_table, blocks)
    away = grams(True, home, me, acts, grads_out)
    got = lax.ppermute(away, "c", swap)
    own = grams(False, home, me, acts, grads_out)
    chip = (own.astype(F32) + got.astype(F32)).astype(BF)
    parts = exchange(chip.reshape(16, -1, B), plane)
    share = exchange(section_sum(home, slot_of, me, parts, old_row), "z")
    mine = exchange(inverse(home, slot_of, me, share), "z")
    other = lax.ppermute(mine, "c", swap)
    row = exchange(route(slot_table, places, me, mine, other), plane)
    return final(slot_table, places, me, row, mine, old_cov, weight_grad)


def solution(mesh):
    wide = Mesh(mesh.devices.reshape(8, 4, 4, 2), ("z", "y", "x", "c"))
    dp = ("y", "x", "c")
    in_specs = (
        P(("z",) + dp, None),
        P(("z",) + dp, None),
        P("z", dp),
        P(),
        P(("z",) + dp),
        P(dp, "z", None, None),
    )
    out_specs = (P("z", dp), P(dp, "z", None, None))
    return jax.shard_map(
        on_device, mesh=wide, in_specs=in_specs, out_specs=out_specs, check_vma=False
    )
```

time: 140 us -> 170 us (1.21)
  waiting for transfers between devices: 2.04 us -> 53.8 us
  blocking collectives: 96.2 us -> 53.1 us
  between operations: 1.34 us -> 14.8 us
  local copies, waits for them, and re-layouts: 4.89 us -> 9.27 us
  starting transfers between devices: 7.79 us -> 11.5 us
  Pallas kernels: 26.4 us -> 23.5 us
  other arithmetic: 0.8 us -> 3.04 us
    all_gather x0 -> x1, waiting for transfers between devices: none -> 52.6 us  [on_device(): old_row = lax.all_gather(old_cov[0, 0], plane + ('c',), axis=0)]
    all_to_all x4 -> x3, blocking collectives: 96.2 us -> 53.1 us  [the longest x1 21.5 us: on_device(): share = exchange(section_sum(home, slot_of, me, parts, old_row), 'z')]
    all_to_all x0 -> x1, starting transfers between devices: none -> 5.15 us  [on_device(): parts = exchange(chip.reshape(16, -1, B), plane)]
    unnamed x12 -> x22, local copies, waits for them, and re-layouts: 4.89 us -> 9.27 us
    pallas_call x5 -> x4, Pallas kernels: 16.2 us -> 12 us  [the longest x1 7.7 us: inverse(): pl.pallas_call(inverse_kernel, out_shape=jax.ShapeDtypeStruct((8, 2 * H +...]
    convert_element_type x1, other arithmetic: 0.61 us -> 2.84 us  [on_device(): chip = (own.astype(F32) + got.astype(F32)).astype(BF)]
    ppermute x2 -> x1, starting transfers between devices: 4.46 us -> 3.11 us  [on_device(): other = lax.ppermute(mine, 'c', swap)]
  transfers between devices with their start and end apart: 3 -> 4, of which waited for: 2 -> 2; matrix products, arithmetic and copies ran while one was open for 0% -> 2% of each run, Pallas kernels for 4% -> 3%
where the time goes in v3:
time: 170 us; the launch traced here: 169 us
  waiting for transfers between devices  53.8 us (32%)
  blocking collectives  53.1 us (31%)
  Pallas kernels  23.5 us (14%)
  between operations  14.8 us (9%)
  starting transfers between devices  11.5 us (7%)
  local copies, waits for them, and re-layouts  9.27 us (5%)
  other arithmetic  3.04 us (2%)
    all_gather x1, waiting for transfers between devices, on_device(): old_row = lax.all_gather(old_cov[0, 0], plane + ('c',), axis=0)  52.6 us
    all_to_all x1, blocking collectives, on_device(): share = exchange(section_sum(home, slot_of, me, parts, old_row), 'z')  21.5 us
    all_to_all x1, blocking collectives, on_device(): row = exchange(route(slot_table, places, me, mine, other), plane)  18.9 us
    all_to_all x1, blocking collectives, on_device(): mine = exchange(inverse(home, slot_of, me, share), 'z')  12.8 us
    pallas_call x2, Pallas kernels, grams(): pl.pallas_call(functools.partial(gram_kernel, away), out_shape=jax.ShapeD...  11.5 us
    unnamed x22, local copies, waits for them, and re-layouts  9.27 us
    pallas_call x1, Pallas kernels, inverse(): pl.pallas_call(inverse_kernel, out_shape=jax.ShapeDtypeStruct((8, 2 * H +...  7.7 us
    all_to_all x1, starting transfers between devices, on_device(): parts = exchange(chip.reshape(16, -1, B), plane)  5.15 us
  transfers between devices with their start and end apart: 4, of which 2 were waited for; matrix products, arithmetic and copies ran while one was open for 2% of the time, Pallas kernels for 3%

profile of v3, /device:TPU:1, one launch (start us, length us, event | category | flops | bytes accessed | tf_op | source)
XLA Modules:
  0.0 169.1 jit_solution(13038985158125072181)
XLA Ops:
  7.2 0.0 all-gather.3.cloned.1.call-start
  7.9 0.1 pad_add_fusion.me_ref
  7.9 2.8 %copy-done = bf16[128,24576]{1,0:T(8,128)(2,1)S(1)} copy-done((bf16[128,24576]{1,0:T(8,128)(2,1)S(1)}, bf16[128,24576]{1,0:T(8,128)(2,1)}, u32[]{:S(2)}) %copy-start) | copy-done | bytes 6291480
  10.7 1.4 copy-done.2
  12.1 0.7 copy-done.7
  12.8 6.4 %grams_away.1 = bf16[8448,128]{1,0:T(8,128)(2,1)} custom-call(s32[256]{0:T(256)S(1)} %copy-done.7, s32[4]{0:T(128)S(1)} %pad_add_fusion.me_ref, bf16[128,6144]{1,0:T(8,128)(2,1)S(1)} %copy-done.2, bf16[128,24576]{1,0:T(8,128)(2,1)S(1)} %copy-done), custom_call_target="tpu_custom_call" | custom-call | flops 536870912 | bytes 16777216 | tf_op jit(solution)/shard_map/grams_away/pallas_call | solution.py:131
  19.2 3.2 %collective-permute-start = (bf16[8448,128]{1,0:T(8,128)(2,1)}, bf16[8448,128]{1,0:T(8,128)(2,1)}, u32[]{:S(2)}, u32[]{:S(2)}) collective-permute-start(bf16[8448,128]{1,0:T(8,128)(2,1)} %grams_away.1), channel_id=1, source_target_pairs={{0,1},{1,0},{2,3},{3,2},{4,5},{5,4},{6,7},{7,6},{8,9},{9,8},{10,11... | collective-permute-start | bytes 6488072 | tf_op jit(solution)/shard_map/ppermute | solution.py:344
  22.5 0.0 all-gather.3.cloned.1.call-update
  22.5 2.8 %copy-done.1 = bf16[128,24576]{1,0:T(8,128)(2,1)S(1)} copy-done((bf16[128,24576]{1,0:T(8,128)(2,1)S(1)}, bf16[128,24576]{1,0:T(8,128)(2,1)}, u32[]{:S(2)}) %copy-start.1) | copy-done | bytes 6291480
  25.3 5.1 %grams_own.1 = bf16[8448,128]{1,0:T(8,128)(2,1)S(1)} custom-call(s32[256]{0:T(256)S(1)} %copy-done.8, s32[4]{0:T(128)S(1)} %pad_add_fusion.me_ref, bf16[128,6144]{1,0:T(8,128)(2,1)S(1)} %copy-done.3, bf16[128,24576]{1,0:T(8,128)(2,1)S(1)} %copy-done.1), custom_call_target="tpu_custom_call" | custom-call | flops 536870912 | bytes 16777216 | tf_op jit(solution)/shard_map/grams_own/pallas_call | solution.py:131
  30.4 2.8 %add_convert_fusion = bf16[8448,128]{1,0:T(8,128)(2,1)} fusion(bf16[8448,128]{1,0:T(8,128)(2,1)} %collective-permute-done, bf16[8448,128]{1,0:T(8,128)(2,1)S(1)} %grams_own.1), kind=kLoop, calls=%fused_computation | loop fusion | flops 4325376 | bytes 6488064 | tf_op jit(solution)/shard_map/convert_element_type | solution.py:346
  33.3 5.1 %all-to-all-start = ((bf16[16,528,128]{2,1,0:T(8,128)(2,1)}), bf16[16,528,128]{2,1,0:T(8,128)(2,1)S(1)}, u32[]{:S(2)}, u32[]{:S(2)}) async-start(bf16[16,528,128]{2,1,0:T(8,128)(2,1)} %bitcast.6), calls=%async_computation | async-start | bytes 4325376 | tf_op jit(solution)/shard_map/all_to_all | solution.py:347
  38.4 0.1 select_reduce_fusion.slot_ref
  38.5 52.6 %all-gather.3.cloned.1.call-done = f32[32,1,128,128]{3,2,1,0:T(8,128)} async-done(((f32[1,1,128,128]{3,2,1,0:T(8,128)}), f32[32,1,128,128]{3,2,1,0:T(8,128)}) %all-gather.3.cloned.1.call-update) | async-done | bytes 2097168 | tf_op jit(solution)/shard_map/all_gather | solution.py:335
  91.1 1.6 copy-done.4
  92.7 1.0 section_sum.1
  93.7 21.5 %all_to_all.20.parts_ref = bf16[8,208,128]{2,1,0:T(8,128)(2,1)S(1)} all-to-all(bf16[8,208,128]{2,1,0:T(8,128)(2,1)S(1)} %section_sum.1), channel_id=1, replica_groups=mesh['z'=8,'y'=4,'x'=4,'c'=2] {'z'}, dimensions={0} | all-to-all | bytes 851968 | tf_op jit(solution)/shard_map/all_to_all | solution.py:348
  115.2 7.7 %inverse.1 = bf16[8,144,128]{2,1,0:T(8,128)(2,1)S(1)} custom-call(s32[256]{0:T(256)S(1)} %copy-done.8, s32[240]{0:T(256)S(1)} %select_reduce_fusion.slot_ref, s32[4]{0:T(128)S(1)} %pad_add_fusion.me_ref, bf16[8,208,128]{2,1,0:T(8,128)(2,1)S(1)} %all_to_all.20.parts_ref), custom_call_target="tpu_custom_call" | custom-call | tf_op jit(solution)/shard_map/inverse/pallas_call | solution.py:242
  122.9 12.8 %all_to_all.21.mine_ref.column_ref = bf16[8,144,128]{2,1,0:T(8,128)(2,1)S(1)} all-to-all(bf16[8,144,128]{2,1,0:T(8,128)(2,1)S(1)} %inverse.1), channel_id=1, replica_groups=mesh['z'=8,'y'=4,'x'=4,'c'=2] {'z'}, dimensions={0} | all-to-all | bytes 589824 | tf_op jit(solution)/shard_map/all_to_all | solution.py:349
  135.7 3.1 %collective-permute-start.1 = (bf16[8,144,128]{2,1,0:T(8,128)(2,1)S(1)}, bf16[8,144,128]{2,1,0:T(8,128)(2,1)S(1)}, u32[]{:S(2)}, u32[]{:S(2)}) collective-permute-start(bf16[8,144,128]{2,1,0:T(8,128)(2,1)S(1)} %all_to_all.21.mine_ref.column_ref), channel_id=1, source_target_pairs={{0,1},{1,0},{2,3},{3,2},{4,5},{5,4},{6,7},{7,6},{8,9},{9,8},{10,11... | collective-permute-start | bytes 884744 | tf_op jit(solution)/shard_map/ppermute | solution.py:350
  138.8 1.2 collective-permute-done.1.other_ref
  140.0 0.8 route.1
  140.8 18.9 %all_to_all.22.plane_ref = bf16[16,208,128]{2,1,0:T(8,128)(2,1)S(1)} all-to-all(bf16[16,208,128]{2,1,0:T(8,128)(2,1)S(1)} %route.1), channel_id=1, replica_groups=mesh['z'=8,'y'=4,'x'=4,'c'=2] {'y','x'}, dimensions={0} | all-to-all | bytes 1703936 | tf_op jit(solution)/shard_map/all_to_all | solution.py:351
  159.7 2.6 %final.1 = (bf16[768,768]{1,0:T(8,128)(2,1)}, f32[1,1,128,128]{3,2,1,0:T(8,128)}) custom-call(s32[256]{0:T(256)S(1)} %copy-done.9, s32[240]{0:T(256)S(1)} %copy-done.10, s32[4]{0:T(128)S(1)} %pad_add_fusion.me_ref, bf16[16,208,128]{2,1,0:T(8,128)(2,1)S(1)} %all_to_all.22.plane_ref, bf16[8,144,128]{2,1,0:T(8,128)(2,1)S(1)} %all_to_all.21.mine_ref.column_ref, ...), custom_call_target="tpu_custom_call" | custom-call | tf_op jit(solution)/shard_map/final/pallas_call | solution.py:311
  (19 shorter events, 0.0 us)
Async XLA Ops:
  7.2 84.0 %all-gather.3.cloned.1.call-start = ((), (), s32[]{:S(2)}) async-start(), calls=%async_computation.4 | async-start | bytes 2162688 | tf_op jit(solution)/shard_map/all_gather | solution.py:335
  7.9 2.8 %copy-start = (bf16[128,24576]{1,0:T(8,128)(2,1)S(1)}, bf16[128,24576]{1,0:T(8,128)(2,1)}, u32[]{:S(2)}) copy-start(bf16[128,24576]{1,0:T(8,128)(2,1)} %grads_ref.3) | copy-start | bytes 18874372
  10.7 1.4 copy-start.2
  12.1 0.7 copy-start.7
  12.8 9.7 %copy-start.3 = (bf16[128,6144]{1,0:T(8,128)(2,1)S(1)}, bf16[128,6144]{1,0:T(8,128)(2,1)}, u32[]{:S(2)}) copy-start(bf16[128,6144]{1,0:T(8,128)(2,1)} %acts_ref.3) | copy-start | bytes 4718596
  12.8 9.7 %copy-start.8 = (s32[256]{0:T(256)S(1)}, s32[256]{0:T(256)}, u32[]{:S(2)}) copy-start(s32[256]{0:T(256)} %constant.26.clone.table_ref.home_ref) | copy-start | bytes 3076
  19.2 11.2 %collective-permute-start = (bf16[8448,128]{1,0:T(8,128)(2,1)}, bf16[8448,128]{1,0:T(8,128)(2,1)}, u32[]{:S(2)}, u32[]{:S(2)}) collective-permute-start(bf16[8448,128]{1,0:T(8,128)(2,1)} %grams_away.1), channel_id=1, source_target_pairs={{0,1},{1,0},{2,3},{3,2},{4,5},{5,4},{6,7},{7,6},{8,9},{9,8},{10,11... | collective-permute-start | bytes 6488072 | tf_op jit(solution)/shard_map/ppermute | solution.py:344
  22.5 2.8 %copy-start.1 = (bf16[128,24576]{1,0:T(8,128)(2,1)S(1)}, bf16[128,24576]{1,0:T(8,128)(2,1)}, u32[]{:S(2)}) copy-start(bf16[128,24576]{1,0:T(8,128)(2,1)} %grads_ref.3) | copy-start | bytes 18874372
  33.3 5.2 %copy-start.9 = (s32[256]{0:T(256)S(1)}, s32[256]{0:T(256)}, u32[]{:S(2)}) copy-start(s32[256]{0:T(256)} %table_ref.5) | copy-start | bytes 3076
  33.3 57.9 %all-to-all-start = ((bf16[16,528,128]{2,1,0:T(8,128)(2,1)}), bf16[16,528,128]{2,1,0:T(8,128)(2,1)S(1)}, u32[]{:S(2)}, u32[]{:S(2)}) async-start(bf16[16,528,128]{2,1,0:T(8,128)(2,1)} %bitcast.6), calls=%async_computation | async-start | bytes 4325376 | tf_op jit(solution)/shard_map/all_to_all | solution.py:347
  91.1 1.6 copy-start.4
  93.7 46.3 %copy-start.10 = (s32[240]{0:T(256)S(1)}, s32[240]{0:T(256)}, u32[]{:S(2)}) copy-start(s32[240]{0:T(256)} %constant.27.clone.place_ref) | copy-start | bytes 2884
  115.2 44.5 %copy-start.5 = (bf16[768,768]{1,0:T(8,128)(2,1)S(1)}, bf16[768,768]{1,0:T(8,128)(2,1)}, u32[]{:S(2)}) copy-start(bf16[768,768]{1,0:T(8,128)(2,1)} %weight_ref.1) | copy-start | bytes 3538948
  115.2 44.5 %copy-start.6 = (f32[1,1,128,128]{3,2,1,0:T(8,128)S(1)}, f32[1,1,128,128]{3,2,1,0:T(8,128)}, u32[]{:S(2)}) copy-start(f32[1,1,128,128]{3,2,1,0:T(8,128)} %old_ref.1) | copy-start | bytes 196612
  135.7 4.3 %collective-permute-start.1 = (bf16[8,144,128]{2,1,0:T(8,128)(2,1)S(1)}, bf16[8,144,128]{2,1,0:T(8,128)(2,1)S(1)}, u32[]{:S(2)}, u32[]{:S(2)}) collective-permute-start(bf16[8,144,128]{2,1,0:T(8,128)(2,1)S(1)} %all_to_all.21.mine_ref.column_ref), channel_id=1, source_target_pairs={{0,1},{1,0},{2,3},{3,2},{4,5},{5,4},{6,7},{7,6},{8,9},{9,8},{10,11... | collective-permute-start | bytes 884744 | tf_op jit(solution)/shard_map/ppermute | solution.py:350
Sparse Core Ops, SparseCore 0:
  22.6 68.4 all-gather.2

commit v4 on v2

v4 whole, which is shorter than its diff:
```python
import functools

import jax
import jax.numpy as jnp
import numpy as np
from jax import lax
from jax.experimental import pallas as pl
from jax.experimental.pallas import tpu as pltpu
from jax.sharding import Mesh, PartitionSpec as P

B = 128
H = B // 2
BF = jnp.bfloat16
F32 = jnp.float32
EXTRA = 16
ROOMS = (3, 4)
VMEM_LIMIT = 24 * 1024 * 1024


SMEM = pl.BlockSpec(memory_space=pltpu.SMEM)
VMEM = pl.BlockSpec(memory_space=pltpu.VMEM)
HBM = pl.BlockSpec(memory_space=pltpu.HBM)
PARAMS = pltpu.CompilerParams(vmem_limit_bytes=VMEM_LIMIT)


def iota(shape, dim):
    return lax.broadcasted_iota(jnp.int32, shape, dim)


def pack(sym):
    top = sym[:H, :]
    low = pltpu.roll(sym[H:, :], H, 1)
    row, lane = iota((H, B), 0), iota((H, B), 1)
    half = jnp.where(lane < row, low, top)
    diag = jnp.sum(jnp.where(lane == row, low, 0.0), axis=0, keepdims=True)
    return half, diag


def unpack(half, diag):
    row, lane = iota((H, B), 0), iota((H, B), 1)
    upper = jnp.where(lane >= row, half, 0.0)
    lower = jnp.where(lane < row, half, 0.0)
    lower = jnp.where(lane == row, diag, lower)
    lower = pltpu.roll(lower, H, 1)
    part = jnp.concatenate((upper, lower), axis=0)
    brow, blane = iota((B, B), 0), iota((B, B), 1)
    return part + jnp.where(brow == blane, 0.0, part.T)


def eliminate(groups, k, m, solve):
    rows = 8
    lane, sub = iota((rows, B), 1), iota((rows, B), 0)
    at, inside = k // rows, k % rows
    spread = lambda v: jnp.broadcast_to(v, (rows, B))
    cols = [[spread(g[:, k + i : k + i + 1]) for g in groups] for i in range(m)]
    pivot = [[spread(cols[j][at][inside + i : inside + i + 1, :]) for j in range(m)] for i in range(m)]
    inv = solve(pivot)
    lines = [spread(groups[at][inside + i : inside + i + 1, :]) for i in range(m)]
    fresh_lines = []
    for i in range(m):
        line = inv[i][0] * lines[0]
        for j in range(1, m):
            line = line + inv[i][j] * lines[j]
        for j in range(m):
            line = jnp.where(lane == k + j, inv[i][j], line)
        fresh_lines.append(line)
    out = []
    inner = (lane >= k) & (lane < k + m)
    for g in range(B // rows):
        new = jnp.where(inner, 0.0, groups[g])
        for i in range(m):
            new = new - cols[i][g] * fresh_lines[i]
        if g == at:
            for i in range(m):
                new = jnp.where(sub == inside + i, fresh_lines[i], new)
        out.append(new)
    return out


def solve2(p):
    a, b, c = p[0][0], p[0][1], p[1][1]
    scale = 1.0 / (a * c - b * b)
    off = -b * scale
    return [[c * scale, off], [off, a * scale]]


def solve4(p):
    e = solve2([p[0][:2], p[1][:2]])
    f = [row[2:] for row in p[:2]]
    m = [[e[i][0] * f[0][j] + e[i][1] * f[1][j] for j in range(2)] for i in range(2)]
    s = [[p[2 + i][2 + j] - (f[0][i] * m[0][j] + f[1][i] * m[1][j]) for j in range(2)] for i in range(2)]
    si = solve2(s)
    x = [[m[i][0] * si[0][j] + m[i][1] * si[1][j] for j in range(2)] for i in range(2)]
    top = [[e[i][j] + x[i][0] * m[j][0] + x[i][1] * m[j][1] for j in range(2)] + [-x[i][0], -x[i][1]] for i in range(2)]
    low = [[-x[0][i], -x[1][i]] + si[i] for i in range(2)]
    return top + low


def invert(mat):
    groups = [mat[g * 8 : (g + 1) * 8, :] for g in range(B // 8)]
    for k in range(0, B, 4):
        groups = eliminate(groups, k, 4, solve4)
    return jnp.concatenate(groups, axis=0)


def slot_grams(live, want, table_ref, acts_ref, grads_ref, out_ref):
    in_blocks = acts_ref.shape[1] // B
    out_blocks = grads_ref.shape[1] // B
    group_rows = 8 * H + EXTRA
    unroll = 2

    @pl.loop(0, 16 // unroll)
    def _(trip):
        for inner in range(unroll):
            group = trip * unroll + inner
            base = pl.multiple_of(group * group_rows, 16)
            diags = jnp.zeros((8, B), F32)
            for row in range(8):
                which = table_ref[(group * 2 + want) * 8 + row]
                filled = jnp.where(which >= 0, live, 0)
                first = pl.multiple_of(jnp.clip(which, 0, in_blocks - 1) * B, B)
                second = pl.multiple_of(jnp.clip(which - in_blocks, 0, out_blocks - 1) * B, B)
                x = jnp.where(which < in_blocks, acts_ref[:, pl.ds(first, B)], grads_ref[:, pl.ds(second, B)])
                x = jnp.where(iota(x.shape, 0) < filled, x, jnp.zeros_like(x))
                gram = lax.dot_general(x, x, (((0,), (0,)), ((), ())), preferred_element_type=F32)
                half, diag = pack(gram)
                out_ref[pl.ds(base + row * H, H), :] = half.astype(BF)
                diags = jnp.where(iota((8, B), 0) == row, diag, diags)
            count = jnp.full((8, B), live, jnp.int32).astype(F32)
            out_ref[pl.ds(base + 8 * H, EXTRA), :] = jnp.concatenate((diags, count), axis=0).astype(BF)


def make_plan(in_blocks, row_blocks, col_blocks, table_ref, crowd_ref, plan_ref):
    core, chip = lax.axis_index("c"), lax.axis_index("y") * 4 + lax.axis_index("x")
    wide = 2 * col_blocks
    count = wide + row_blocks
    which, lane = iota((24, B), 0), iota((24, B), 1)
    wanted = jnp.where(
        which < wide,
        in_blocks + (lane % 16) * wide + which,
        jnp.where(which < count, (lane // 16) * row_blocks + which - wide, -2),
    )
    slots = jnp.zeros_like(wanted)
    for slot in range(table_ref.shape[0]):
        slots = jnp.where(wanted == table_ref[slot], slot, slots)
    holder = slots // 16
    ranks = jnp.zeros_like(wanted)
    for at in range(count - 1):
        same = holder == jnp.broadcast_to(holder[at : at + 1, :], holder.shape)
        ranks += jnp.where(same & (which > at), 1, 0)
    crowd_ref[0] = jnp.max(jnp.where(which < count, ranks, 0))
    sends = jnp.zeros((8, B), jnp.int32)
    for at in range(max(ROOMS)):
        chosen = (holder == chip) & (ranks == 2 * at + core) & (which < count)
        row = jnp.sum(jnp.where(chosen, slots % 16, 0), axis=0, keepdims=True)
        sends = jnp.where(iota((8, B), 0) == at, jnp.broadcast_to(row, (8, B)), sends)
    plan_ref[:8, :] = sends
    plan_ref[8:32, :] = (holder * 2 + ranks % 2) * 8 + ranks // 2
    plan_ref[32:, :] = slots


def away_kernel(
    row_blocks, col_blocks, table_ref, live_ref, acts_ref, grads_ref, out_ref, crowd_ref, plan_ref, x_ref, y_ref, sems
):
    first = pltpu.make_async_copy(acts_ref, x_ref, sems.at[0])
    second = pltpu.make_async_copy(grads_ref, y_ref, sems.at[1])
    first.start()
    second.start()
    make_plan(acts_ref.shape[1] // B, row_blocks, col_blocks, table_ref, crowd_ref, plan_ref)
    first.wait()
    second.wait()
    slot_grams(live_ref[0], 1 - lax.axis_index("c"), table_ref, x_ref, y_ref, out_ref)


def own_kernel(table_ref, live_ref, acts_ref, grads_ref, out_ref):
    slot_grams(live_ref[0], lax.axis_index("c"), table_ref, acts_ref, grads_ref, out_ref)


GRAMS = jax.ShapeDtypeStruct((16 * (8 * H + EXTRA), B), BF)


def away_grams(table, live, acts, grads_out, row_blocks, col_blocks):
    return pl.pallas_call(
        functools.partial(away_kernel, row_blocks, col_blocks),
        out_shape=(
            GRAMS,
            jax.ShapeDtypeStruct((1,), jnp.int32),
            jax.ShapeDtypeStruct((56, B), jnp.int32),
            jax.ShapeDtypeStruct(acts.shape, acts.dtype),
            jax.ShapeDtypeStruct(grads_out.shape, grads_out.dtype),
        ),
        in_specs=[SMEM, SMEM, HBM, HBM],
        out_specs=(VMEM, SMEM, VMEM, VMEM, VMEM),
        scratch_shapes=[pltpu.SemaphoreType.DMA((2,))],
        compiler_params=PARAMS,
        cost_estimate=pl.CostEstimate(flops=0, bytes_accessed=36 * 2**20, transcendentals=0),
        name="grams_away",
    )(table, live, acts, grads_out)


def own_grams(table, live, acts, grads_out):
    return pl.pallas_call(
        own_kernel,
        out_shape=GRAMS,
        in_specs=[SMEM, SMEM, VMEM, VMEM],
        out_specs=VMEM,
        compiler_params=PARAMS,
        cost_estimate=pl.CostEstimate(flops=0, bytes_accessed=18 * 2**20, transcendentals=0),
        name="grams_own",
    )(table, live, acts, grads_out)


def section_kernel(parts_ref, out_ref):
    for row in range(8):
        total = parts_ref[0, row * H : (row + 1) * H, :].astype(F32)
        for g in range(1, 16):
            total += parts_ref[g, row * H : (row + 1) * H, :].astype(F32)
        out_ref[row, :H, :] = total.astype(BF)
    extra = parts_ref[0, 8 * H :, :].astype(F32)
    for g in range(1, 16):
        extra += parts_ref[g, 8 * H :, :].astype(F32)
    count = extra[8:, :]
    high = jnp.floor(count * (1.0 / 256.0))
    low = count - 256.0 * high
    sub = iota((8, B), 0)
    for row in range(8):
        first = jnp.where(sub == 0, jnp.broadcast_to(extra[row : row + 1, :], (8, B)), jnp.where(sub == 1, high, low))
        out_ref[row, H:, :] = jnp.concatenate((first, jnp.zeros_like(first)), axis=0).astype(BF)


def section_sum(parts):
    return pl.pallas_call(
        section_kernel,
        out_shape=jax.ShapeDtypeStruct((8, H + EXTRA, B), BF),
        compiler_params=pltpu.CompilerParams(vmem_limit_bytes=VMEM_LIMIT),
        name="section_sum",
    )(parts)


def take_row(rows, at):
    return jnp.sum(jnp.where(iota((EXTRA, B), 0) == at, rows, 0.0), axis=0, keepdims=True)


def inverse_kernel(parts_ref, old_ref, cov_ref, out_ref, new_ref, sem):
    half = parts_ref[0, :H, :].astype(F32)
    extra = parts_ref[0, H:, :].astype(F32)
    for s in range(1, 8):
        half += parts_ref[s, :H, :].astype(F32)
        extra += parts_ref[s, H:, :].astype(F32)
    total = extra[1:2, :] * 256.0 + extra[2:3, :]
    gram = unpack(half, extra[:1, :])
    cov = 0.8 * old_ref[0, 0] + 0.2 * gram / total
    new_ref[0, 0] = cov
    copy = pltpu.make_async_copy(new_ref, cov_ref, sem)
    copy.start()
    eye = jnp.where(iota((B, B), 0) == iota((B, B), 1), 0.1, 0.0)
    inv_half, inv_diag = pack(invert(cov + eye))
    packed = jnp.concatenate((inv_half, jnp.broadcast_to(inv_diag, (EXTRA, B))), axis=0).astype(BF)
    for section in range(8):
        out_ref[section] = packed
    copy.wait()


def inverse(parts, old_cov):
    return pl.pallas_call(
        inverse_kernel,
        out_shape=(
            jax.ShapeDtypeStruct(old_cov.shape, F32),
            jax.ShapeDtypeStruct((8, H + EXTRA, B), BF),
        ),
        in_specs=[VMEM, VMEM],
        out_specs=(HBM, VMEM),
        scratch_shapes=[pltpu.VMEM(old_cov.shape, F32), pltpu.SemaphoreType.DMA],
        compiler_params=PARAMS,
        name="inverse",
    )(parts, old_cov)


def route_kernel(room, plan_ref, mine_ref, other_ref, out_ref):
    core, lane = lax.axis_index("c"), lax.axis_index("z") * 16
    for chip in range(16):
        diags = jnp.zeros((EXTRA, B), F32)
        for at in range(room):
            if room in ROOMS:
                index = plan_ref[at, lane + chip]
                block = jnp.where(index // 8 == core, mine_ref[index % 8], other_ref[index % 8])
            else:
                block = mine_ref[at]
            out_ref[chip, at * H : (at + 1) * H, :] = block[:H, :]
            diags = jnp.where(iota((EXTRA, B), 0) == at, block[H:, :].astype(F32), diags)
        out_ref[chip, room * H :, :] = diags.astype(BF)


def route(room, plans, mine, other):
    return pl.pallas_call(
        functools.partial(route_kernel, room),
        out_shape=jax.ShapeDtypeStruct((16, room * H + EXTRA, B), BF),
        in_specs=[SMEM, VMEM, VMEM],
        out_specs=VMEM,
        compiler_params=PARAMS,
        name="route",
    )(plans, mine, other)


def final_kernel(room, plan_ref, mine_ref, other_ref, weight_ref, out_ref, left_ref, right_ref, sems):
    core = lax.axis_index("c")
    lane = lax.axis_index("z") * 16 + lax.axis_index("y") * 4 + lax.axis_index("x")
    row_blocks = weight_ref.shape[0] // B
    col_blocks = weight_ref.shape[1] // B

    def block(index):
        found = plan_ref[(8 if room in ROOMS else 32) + index, lane]
        holder, at = found // 8, found % 8
        same = holder % 2 == core
        chip = holder // 2
        rows = pl.ds(pl.multiple_of(at * H, H), H)
        half = jnp.where(same, mine_ref[chip, rows, :], other_ref[chip, rows, :]).astype(F32)
        diags = jnp.where(same, mine_ref[chip, room * H :, :], other_ref[chip, room * H :, :]).astype(F32)
        return unpack(half, take_row(diags, at)).astype(BF)

    col_invs = [block(core * col_blocks + j) for j in range(col_blocks)]
    copies = []
    strips = 2
    for strip in range(strips):
        span = row_blocks // strips
        for i in range(strip * span, (strip + 1) * span):
            rows = slice(i * B, (i + 1) * B)
            left = jnp.dot(block(2 * col_blocks + i), weight_ref[rows, :], preferred_element_type=F32)
            left_ref[rows, :] = left.astype(BF)
        rows = slice(strip * span * B, (strip + 1) * span * B)
        for j in range(col_blocks):
            cols = slice(j * B, (j + 1) * B)
            right = jnp.dot(left_ref[rows, cols], col_invs[j], preferred_element_type=F32)
            right_ref[rows, cols] = right.astype(BF)
        copies.append(pltpu.make_async_copy(right_ref.at[rows, :], out_ref.at[rows, :], sems.at[strip]))
        copies[-1].start()
    for copy in copies:
        copy.wait()


def final(room, plans, mine, other, weight_grad):
    return pl.pallas_call(
        functools.partial(final_kernel, room),
        out_shape=jax.ShapeDtypeStruct(weight_grad.shape, BF),
        in_specs=[SMEM, VMEM, VMEM, VMEM],
        out_specs=HBM,
        scratch_shapes=[
            pltpu.VMEM(weight_grad.shape, BF),
            pltpu.VMEM(weight_grad.shape, BF),
            pltpu.SemaphoreType.DMA((2,)),
        ],
        compiler_params=PARAMS,
        name="final",
    )(plans, mine, other, weight_grad)


def on_device(acts, grads_out, weight_grad, slot_table, row_counts, old_cov):
    row_blocks = weight_grad.shape[0] // B
    col_blocks = weight_grad.shape[1] // B
    plane = ("y", "x")
    exchange = functools.partial(lax.all_to_all, split_axis=0, concat_axis=0, tiled=True)
    swap = functools.partial(lax.ppermute, axis_name="c", perm=[(0, 1), (1, 0)])

    away, crowd, plans, acts_held, grads_held = away_grams(
        slot_table, row_counts, acts, grads_out, row_blocks, col_blocks
    )
    got = swap(away)
    own = own_grams(slot_table, row_counts, acts_held, grads_held)
    sums = (own.astype(F32) + got.astype(F32)).astype(BF)
    branch = sum((crowd[0] >= 2 * room).astype(jnp.int32) for room in ROOMS)
    sums, branch = lax.optimization_barrier((sums, branch))
    parts = exchange(sums.reshape(16, -1, B), plane)
    parts = exchange(section_sum(parts), "z")
    new_cov, inv = inverse(parts, old_cov)
    mine = exchange(inv, "z")

    def compact(room, plans, mine, weight_grad):
        got = exchange(route(room, plans, mine, swap(mine)), plane)
        return final(room, plans, got, swap(got), weight_grad)

    def full(plans, mine, weight_grad):
        got = exchange(route(8, plans, mine, mine), plane)
        return final(8, plans, got, swap(got), weight_grad)

    branches = [functools.partial(compact, room) for room in ROOMS] + [full]
    return lax.switch(branch, branches, plans, mine, weight_grad), new_cov


def solution(mesh):
    wide = Mesh(mesh.devices.reshape(8, 4, 4, 2), ("z", "y", "x", "c"))
    dp = ("y", "x", "c")
    in_specs = (
        P(("z",) + dp, None),
        P(("z",) + dp, None),
        P("z", dp),
        P(),
        P(("z",) + dp),
        P(dp, "z", None, None),
    )
    out_specs = (P("z", dp), P(dp, "z", None, None))
    return jax.shard_map(
        on_device, mesh=wide, in_specs=in_specs, out_specs=out_specs, check_vma=False
    )
```

time: 140 us -> 125 us (0.89)
  blocking collectives: 96.2 us -> 67.7 us
  waiting for transfers between devices: 2.04 us -> 11.3 us
  starting transfers between devices: 7.79 us -> 11.8 us
  Pallas kernels: 26.4 us -> 24.2 us
    all_to_all x4 -> x3, blocking collectives: 96.2 us -> 67.7 us  [the longest x1 33.8 us: on_device(): parts = exchange(sums.reshape(16, -1, B), plane)]
    all_to_all x0 -> x1, waiting for transfers between devices: none -> 8.28 us  [on_device(): mine = exchange(inv, 'z')]
    pallas_call x1, Pallas kernels: 11.8 us -> 8.05 us  [inverse(): pl.pallas_call(inverse_kernel, out_shape=(jax.ShapeDtypeStruct(old_cov.sh...]
    all_to_all x0 -> x1, starting transfers between devices: none -> 3.39 us  [on_device(): mine = exchange(inv, 'z')]
    pallas_call x5 -> x4, Pallas kernels: 14.3 us -> 15.8 us  [the longest x1 6.51 us: away_grams(): pl.pallas_call(functools.partial(away_kernel, row_blocks, col_blocks), ou...]
  transfers between devices with their start and end apart: 3 -> 4, of which waited for: 2 -> 3; matrix products, arithmetic and copies ran while one was open for 0% -> 0% of each run, Pallas kernels for 4% -> 4%
where the time goes in v4:
time: 125 us; the launch traced here: 124 us
  blocking collectives  67.7 us (54%)
  Pallas kernels  24.2 us (19%)
  starting transfers between devices  11.8 us (9%)
  waiting for transfers between devices  11.3 us (9%)
  local copies, waits for them, and re-layouts  5.88 us (5%)
  between operations  2.66 us (2%)
    all_to_all x1, blocking collectives, on_device(): parts = exchange(sums.reshape(16, -1, B), plane)  33.8 us
    all_to_all x1, blocking collectives, compact(): got = exchange(route(room, plans, mine, swap(mine)), plane)  17.4 us
    all_to_all x1, blocking collectives, on_device(): parts = exchange(section_sum(parts), 'z')  16.5 us
    all_to_all x1, waiting for transfers between devices, on_device(): mine = exchange(inv, 'z')  8.28 us
    pallas_call x1, Pallas kernels, inverse(): pl.pallas_call(inverse_kernel, out_shape=(jax.ShapeDtypeStruct(old_cov.sh...  8.05 us
    pallas_call x1, Pallas kernels, away_grams(): pl.pallas_call(functools.partial(away_kernel, row_blocks, col_blocks), ou...  6.51 us
    unnamed x12, local copies, waits for them, and re-layouts  5.88 us
    pallas_call x1, Pallas kernels, own_grams(): pl.pallas_call(own_kernel, out_shape=GRAMS, in_specs=[SMEM, SMEM, VMEM, V...  5.09 us
  transfers between devices with their start and end apart: 4, of which 3 were waited for; matrix products, arithmetic and copies ran while one was open for 0% of the time, Pallas kernels for 4%

profile of v4, /device:TPU:1, one launch (start us, length us, event | category | flops | bytes accessed | tf_op | source)
XLA Modules:
  0.0 124.3 jit_solution(9671766806474708531)
XLA Ops:
  1.3 2.8 %copy-done = bf16[128,24576]{1,0:T(8,128)(2,1)S(1)} copy-done((bf16[128,24576]{1,0:T(8,128)(2,1)S(1)}, bf16[128,24576]{1,0:T(8,128)(2,1)}, u32[]{:S(2)}) %copy-start) | copy-done | bytes 6291480
  4.1 1.4 %copy-done.1 = bf16[128,6144]{1,0:T(8,128)(2,1)S(1)} copy-done((bf16[128,6144]{1,0:T(8,128)(2,1)S(1)}, bf16[128,6144]{1,0:T(8,128)(2,1)}, u32[]{:S(2)}) %copy-start.1) | copy-done | bytes 1572888
  5.5 0.7 copy-done.3
  6.2 6.5 %grams_away.1 = (bf16[8448,128]{1,0:T(8,128)(2,1)S(1)}, s32[1]{0:T(128)}, s32[56,128]{1,0:T(8,128)S(1)}, bf16[128,6144]{1,0:T(8,128)(2,1)S(1)}, bf16[128,24576]{1,0:T(8,128)(2,1)S(1)}) custom-call(s32[256]{0:T(256)S(1)} %copy-done.3, s32[1]{0:T(128)S(6)} %copy.11.live_ref, bf16[128,6144]{1,0:T(8,128)(2,1)S(1)} %copy-done.1, bf16[128,24576]{1,0:T(8,128)(2,1)S(1)} %copy-done), custom_call_target="tpu_custom_call" | custom-call | bytes 37748736 | tf_op jit(solution)/shard_map/grams_away/pallas_call | solution.py:183
  12.7 3.3 %collective-permute-start.5 = (bf16[8448,128]{1,0:T(8,128)(2,1)S(1)}, bf16[8448,128]{1,0:T(8,128)(2,1)S(1)}, u32[]{:S(2)}, u32[]{:S(2)}) collective-permute-start(bf16[8448,128]{1,0:T(8,128)(2,1)S(1)} %get-tuple-element.44), channel_id=1, source_target_pairs={{0,1},{1,0},{2,3},{3,2},{4,5},{5,4},{6,7},{7,6},{8,9},{9,8},{10,11... | collective-permute-start | bytes 6488072 | tf_op jit(solution)/shard_map/ppermute | solution.py:367
  17.3 5.1 %grams_own.1 = bf16[8448,128]{1,0:T(8,128)(2,1)S(1)} custom-call(s32[256]{0:T(256)S(1)} %copy-done.3, s32[1]{0:T(128)S(6)} %copy.11.live_ref, bf16[128,6144]{1,0:T(8,128)(2,1)S(1)} %get-tuple-element.42.acts_ref, bf16[128,24576]{1,0:T(8,128)(2,1)S(1)} %get-tuple-element.43.grads_ref), custom_call_target="tpu_custom_call" | custom-call | bytes 18874368 | tf_op jit(solution)/shard_map/grams_own/pallas_call | solution.py:202
  22.4 0.0 collective-permute-done.5
  22.4 0.6 add_convert_fusion
  23.0 33.8 %all_to_all.30.parts_ref = bf16[16,528,128]{2,1,0:T(8,128)(2,1)S(1)} all-to-all(bf16[16,528,128]{2,1,0:T(8,128)(2,1)S(1)} %bitcast.2), channel_id=1, replica_groups=mesh['z'=8,'y'=4,'x'=4,'c'=2] {'y','x'}, dimensions={0} | all-to-all | bytes 4325376 | tf_op jit(solution)/shard_map/all_to_all | solution.py:372
  56.8 0.3 section_sum.1
  57.1 16.5 %all_to_all.31.parts_ref = bf16[8,80,128]{2,1,0:T(8,128)(2,1)S(1)} all-to-all(bf16[8,80,128]{2,1,0:T(8,128)(2,1)S(1)} %section_sum.1), channel_id=1, replica_groups=mesh['z'=8,'y'=4,'x'=4,'c'=2] {'z'}, dimensions={0} | all-to-all | bytes 327680 | tf_op jit(solution)/shard_map/all_to_all | solution.py:373
  73.6 8.0 %inverse.1 = (f32[1,1,128,128]{3,2,1,0:T(8,128)}, bf16[8,80,128]{2,1,0:T(8,128)(2,1)}) custom-call(bf16[8,80,128]{2,1,0:T(8,128)(2,1)S(1)} %all_to_all.31.parts_ref, f32[1,1,128,128]{3,2,1,0:T(8,128)S(1)} %copy-done.2), custom_call_target="tpu_custom_call" | custom-call | tf_op jit(solution)/shard_map/inverse/pallas_call | solution.py:265
  81.6 3.4 %all-to-all-start.5 = ((bf16[8,80,128]{2,1,0:T(8,128)(2,1)}), bf16[8,80,128]{2,1,0:T(8,128)(2,1)S(1)}, u32[]{:S(2)}, u32[]{:S(2)}) async-start(bf16[8,80,128]{2,1,0:T(8,128)(2,1)} %get-tuple-element.48), calls=%async_computation.5 | async-start | bytes 327680 | tf_op jit(solution)/shard_map/all_to_all | solution.py:375
  85.0 8.3 %all-to-all-done.5 = bf16[8,80,128]{2,1,0:T(8,128)(2,1)S(1)} async-done(((bf16[8,80,128]{2,1,0:T(8,128)(2,1)}), bf16[8,80,128]{2,1,0:T(8,128)(2,1)S(1)}, u32[]{:S(2)}, u32[]{:S(2)}) %all-to-all-start.5) | async-done | bytes 163872 | tf_op jit(solution)/shard_map/all_to_all | solution.py:375
  93.3 30.0 %conditional.1 = (bf16[768,768]{1,0:T(8,128)(2,1)S(1)}) conditional(s32[]{:T(128)} %clamp.3, (bf16[8,80,128]{2,1,0:T(8,128)(2,1)S(1)}, s32[56,128]{1,0:T(8,128)S(1)}, bf16[768,768]{1,0:T(8,128)(2,1)S(1)}) %tuple.25, (bf16[8,80,128]{2,1,0:T(8,128)(2,1)S(1)}, s32[56,128]{1,0:T(8,128)S(1)}, bf16[768,768]{1,0:T(8,128)(2,1)S(1)}) %tuple.26, ...), branch_computations={%region_0.0_spmd, %region_1.0_spmd, %region_2.0_spmd} | conditional | bytes 12976176 | solution.py:386
  93.3 3.6 %collective-permute-start = (bf16[8,80,128]{2,1,0:T(8,128)(2,1)S(1)}, bf16[8,80,128]{2,1,0:T(8,128)(2,1)S(1)}, u32[]{:S(2)}, u32[]{:S(2)}) collective-permute-start(bf16[8,80,128]{2,1,0:T(8,128)(2,1)S(1)} %get-tuple-element.19.mine_ref), channel_id=1, source_target_pairs={{0,1},{1,0},{2,3},{3,2},{4,5},{5,4},{6,7},{7,6},{8,9},{9,8},{10,11... | collective-permute-start | bytes 491528 | tf_op jit(solution)/shard_map/cond/branch_0_fun/ppermute | solution.py:378
  97.0 1.0 collective-permute-done.other_ref
  98.0 1.5 %route.3 = bf16[16,208,128]{2,1,0:T(8,128)(2,1)S(1)} custom-call(s32[56,128]{1,0:T(8,128)S(1)} %get-tuple-element.18.plan_ref, bf16[8,80,128]{2,1,0:T(8,128)(2,1)S(1)} %get-tuple-element.19.mine_ref, bf16[8,80,128]{2,1,0:T(8,128)(2,1)S(1)} %collective-permute-done.other_ref), custom_call_target="tpu_custom_call" | custom-call | tf_op jit(solution)/shard_map/cond/branch_0_fun/route/pallas_call | solution.py:295
  99.5 17.4 %all_to_all.27.mine_ref = bf16[16,208,128]{2,1,0:T(8,128)(2,1)S(1)} all-to-all(bf16[16,208,128]{2,1,0:T(8,128)(2,1)S(1)} %route.3), channel_id=1, replica_groups=mesh['z'=8,'y'=4,'x'=4,'c'=2] {'y','x'}, dimensions={0} | all-to-all | bytes 1703936 | tf_op jit(solution)/shard_map/cond/branch_0_fun/all_to_all | solution.py:378
  116.9 1.5 %collective-permute-start.1 = (bf16[16,208,128]{2,1,0:T(8,128)(2,1)S(1)}, bf16[16,208,128]{2,1,0:T(8,128)(2,1)S(1)}, u32[]{:S(2)}, u32[]{:S(2)}) collective-permute-start(bf16[16,208,128]{2,1,0:T(8,128)(2,1)S(1)} %all_to_all.27.mine_ref), channel_id=1, source_target_pairs={{0,1},{1,0},{2,3},{3,2},{4,5},{5,4},{6,7},{7,6},{8,9},{9,8},{10,11... | collective-permute-start | bytes 2555912 | tf_op jit(solution)/shard_map/cond/branch_0_fun/ppermute | solution.py:379
  118.4 2.0 %collective-permute-done.1.other_ref = bf16[16,208,128]{2,1,0:T(8,128)(2,1)S(1)} collective-permute-done((bf16[16,208,128]{2,1,0:T(8,128)(2,1)S(1)}, bf16[16,208,128]{2,1,0:T(8,128)(2,1)S(1)}, u32[]{:S(2)}, u32[]{:S(2)}) %collective-permute-start.1) | collective-permute-done | bytes 852000 | tf_op jit(solution)/shard_map/cond/branch_0_fun/ppermute | solution.py:379
  120.4 2.7 %final.3 = bf16[768,768]{1,0:T(8,128)(2,1)S(1)} custom-call(s32[56,128]{1,0:T(8,128)S(1)} %get-tuple-element.18.plan_ref, bf16[16,208,128]{2,1,0:T(8,128)(2,1)S(1)} %all_to_all.27.mine_ref, bf16[16,208,128]{2,1,0:T(8,128)(2,1)S(1)} %collective-permute-done.1.other_ref, bf16[768,768]{1,0:T(8,128)(2,1)S(1)} %get-tuple-element.24.weight_ref), custom_call_target="tpu_custom_call" | custom-call | tf_op jit(solution)/shard_map/cond/branch_0_fun/final/pallas_call | solution.py:342
  123.3 0.0 copy-start.5
  123.3 1.0 copy-done.5
  (7 shorter events, 0.0 us)
Async XLA Ops:
  1.3 2.8 %copy-start = (bf16[128,24576]{1,0:T(8,128)(2,1)S(1)}, bf16[128,24576]{1,0:T(8,128)(2,1)}, u32[]{:S(2)}) copy-start(bf16[128,24576]{1,0:T(8,128)(2,1)} %grads_ref.1) | copy-start | bytes 18874372
  4.1 1.4 %copy-start.1 = (bf16[128,6144]{1,0:T(8,128)(2,1)S(1)}, bf16[128,6144]{1,0:T(8,128)(2,1)}, u32[]{:S(2)}) copy-start(bf16[128,6144]{1,0:T(8,128)(2,1)} %acts_ref.1) | copy-start | bytes 4718596
  5.5 0.7 copy-start.3
  12.7 9.7 %collective-permute-start.5 = (bf16[8448,128]{1,0:T(8,128)(2,1)S(1)}, bf16[8448,128]{1,0:T(8,128)(2,1)S(1)}, u32[]{:S(2)}, u32[]{:S(2)}) collective-permute-start(bf16[8448,128]{1,0:T(8,128)(2,1)S(1)} %get-tuple-element.44), channel_id=1, source_target_pairs={{0,1},{1,0},{2,3},{3,2},{4,5},{5,4},{6,7},{7,6},{8,9},{9,8},{10,11... | collective-permute-start | bytes 6488072 | tf_op jit(solution)/shard_map/ppermute | solution.py:367
  56.8 16.8 %copy-start.2 = (f32[1,1,128,128]{3,2,1,0:T(8,128)S(1)}, f32[1,1,128,128]{3,2,1,0:T(8,128)}, u32[]{:S(2)}) copy-start(f32[1,1,128,128]{3,2,1,0:T(8,128)} %old_ref.1) | copy-start | bytes 196612
  56.8 36.5 %copy-start.4 = (bf16[768,768]{1,0:T(8,128)(2,1)S(1)}, bf16[768,768]{1,0:T(8,128)(2,1)}, u32[]{:S(2)}) copy-start(bf16[768,768]{1,0:T(8,128)(2,1)} %param.11) | copy-start | bytes 3538948
  81.6 11.7 %all-to-all-start.5 = ((bf16[8,80,128]{2,1,0:T(8,128)(2,1)}), bf16[8,80,128]{2,1,0:T(8,128)(2,1)S(1)}, u32[]{:S(2)}, u32[]{:S(2)}) async-start(bf16[8,80,128]{2,1,0:T(8,128)(2,1)} %get-tuple-element.48), calls=%async_computation.5 | async-start | bytes 327680 | tf_op jit(solution)/shard_map/all_to_all | solution.py:375
  93.3 4.7 %collective-permute-start = (bf16[8,80,128]{2,1,0:T(8,128)(2,1)S(1)}, bf16[8,80,128]{2,1,0:T(8,128)(2,1)S(1)}, u32[]{:S(2)}, u32[]{:S(2)}) collective-permute-start(bf16[8,80,128]{2,1,0:T(8,128)(2,1)S(1)} %get-tuple-element.19.mine_ref), channel_id=1, source_target_pairs={{0,1},{1,0},{2,3},{3,2},{4,5},{5,4},{6,7},{7,6},{8,9},{9,8},{10,11... | collective-permute-start | bytes 491528 | tf_op jit(solution)/shard_map/cond/branch_0_fun/ppermute | solution.py:378
  116.9 3.5 %collective-permute-start.1 = (bf16[16,208,128]{2,1,0:T(8,128)(2,1)S(1)}, bf16[16,208,128]{2,1,0:T(8,128)(2,1)S(1)}, u32[]{:S(2)}, u32[]{:S(2)}) collective-permute-start(bf16[16,208,128]{2,1,0:T(8,128)(2,1)S(1)} %all_to_all.27.mine_ref), channel_id=1, source_target_pairs={{0,1},{1,0},{2,3},{3,2},{4,5},{5,4},{6,7},{7,6},{8,9},{9,8},{10,11... | collective-permute-start | bytes 2555912 | tf_op jit(solution)/shard_map/cond/branch_0_fun/ppermute | solution.py:379
  123.3 1.0 copy-start.5

commit v5 on v4

--- a/solution.py
+++ b/solution.py
@@ -14,6 +14,8 @@
 F32 = jnp.float32
 EXTRA = 16
 ROOMS = (3, 4)
+PARTS = 3
+STRIPS = 2
 VMEM_LIMIT = 24 * 1024 * 1024
 
 
@@ -47,32 +49,32 @@
     return part + jnp.where(brow == blane, 0.0, part.T)
 
 
-def eliminate(groups, k, m, solve):
+def eliminate(strips, first, k, m, solve):
     rows = 8
     lane, sub = iota((rows, B), 1), iota((rows, B), 0)
-    at, inside = k // rows, k % rows
+    at, inside = (k - first) // rows, k % rows
     spread = lambda v: jnp.broadcast_to(v, (rows, B))
-    cols = [[spread(g[:, k + i : k + i + 1]) for g in groups] for i in range(m)]
+    cols = [[spread(s[:, k + i : k + i + 1]) for s in strips] for i in range(m)]
     pivot = [[spread(cols[j][at][inside + i : inside + i + 1, :]) for j in range(m)] for i in range(m)]
     inv = solve(pivot)
-    lines = [spread(groups[at][inside + i : inside + i + 1, :]) for i in range(m)]
-    fresh_lines = []
+    lines = [spread(strips[at][inside + i : inside + i + 1, :]) for i in range(m)]
+    fresh = []
     for i in range(m):
         line = inv[i][0] * lines[0]
         for j in range(1, m):
             line = line + inv[i][j] * lines[j]
         for j in range(m):
             line = jnp.where(lane == k + j, inv[i][j], line)
-        fresh_lines.append(line)
+        fresh.append(line)
     out = []
-    inner = (lane >= k) & (lane < k + m)
-    for g in range(B // rows):
-        new = jnp.where(inner, 0.0, groups[g])
+    pivots = (lane >= k) & (lane < k + m)
+    for g, strip in enumerate(strips):
+        new = jnp.where(pivots, 0.0, strip)
         for i in range(m):
-            new = new - cols[i][g] * fresh_lines[i]
+            new = new - cols[i][g] * fresh[i]
         if g == at:
             for i in range(m):
-                new = jnp.where(sub == inside + i, fresh_lines[i], new)
+                new = jnp.where(sub == inside + i, fresh[i], new)
         out.append(new)
     return out
 
@@ -96,18 +98,51 @@
     return top + low
 
 
+def product(a, b):
+    return [[sum(a[i][t] * b[t][j] for t in range(1, len(b))) + a[i][0] * b[0][j] for j in range(len(b[0]))] for i in range(len(a))]
+
+
+def turned(a):
+    return [list(row) for row in zip(*a)]
+
+
+def solve8(p):
+    e = solve4([row[:4] for row in p[:4]])
+    f = [row[4:] for row in p[:4]]
+    m = product(e, f)
+    fm = product(turned(f), m)
+    si = solve4([[p[4 + i][4 + j] - fm[i][j] for j in range(4)] for i in range(4)])
+    x = product(m, si)
+    xm = product(x, turned(m))
+    top = [[e[i][j] + xm[i][j] for j in range(4)] + [-x[i][j] for j in range(4)] for i in range(4)]
+    low = [[-x[j][i] for j in range(4)] + si[i] for i in range(4)]
+    return top + low
+
+
 def invert(mat):
-    groups = [mat[g * 8 : (g + 1) * 8, :] for g in range(B // 8)]
-    for k in range(0, B, 4):
-        groups = eliminate(groups, k, 4, solve4)
-    return jnp.concatenate(groups, axis=0)
+    size = 32
+    dot = functools.partial(jnp.dot, precision=lax.Precision.HIGHEST, preferred_element_type=F32)
+    row, lane = iota((B, B), 0), iota((B, B), 1)
+    for first in range(0, B, size):
+        across = (lane >= first) & (lane < first + size)
+        down = (row >= first) & (row < first + size)
+        own = jnp.where(across, mat, 0.0)
+        strips = [own[first + g : first + g + 8, :] for g in range(0, size, 8)]
+        for k in range(first, first + size, 8):
+            strips = eliminate(strips, first, k, 8, solve8)
+        block = jnp.concatenate(strips, axis=0)
+        lines = jnp.where(across[:size], block, dot(block, mat))
+        edges = [jnp.zeros((rows, B), F32) for rows in (first, B - first - size)]
+        lines = jnp.concatenate([part for part in (edges[0], lines, edges[1]) if part.shape[0]], axis=0)
+        mat = jnp.where(down, lines, jnp.where(across, 0.0, mat) - dot(own, lines))
+    return mat
 
 
 def slot_grams(live, want, table_ref, acts_ref, grads_ref, out_ref):
     in_blocks = acts_ref.shape[1] // B
     out_blocks = grads_ref.shape[1] // B
     group_rows = 8 * H + EXTRA
-    unroll = 2
+    unroll = 4
 
     @pl.loop(0, 16 // unroll)
     def _(trip):
@@ -130,7 +165,7 @@
             out_ref[pl.ds(base + 8 * H, EXTRA), :] = jnp.concatenate((diags, count), axis=0).astype(BF)
 
 
-def make_plan(in_blocks, row_blocks, col_blocks, table_ref, crowd_ref, plan_ref):
+def make_plan(in_blocks, row_blocks, col_blocks, table_ref, branch_ref, send_ref, find_ref, turned_ref):
     core, chip = lax.axis_index("c"), lax.axis_index("y") * 4 + lax.axis_index("x")
     wide = 2 * col_blocks
     count = wide + row_blocks
@@ -148,28 +183,40 @@
     for at in range(count - 1):
         same = holder == jnp.broadcast_to(holder[at : at + 1, :], holder.shape)
         ranks += jnp.where(same & (which > at), 1, 0)
-    crowd_ref[0] = jnp.max(jnp.where(which < count, ranks, 0))
+    most = jnp.max(jnp.where(which < count, ranks, 0))
+    branch_ref[0] = sum((most >= 2 * room).astype(jnp.int32) for room in ROOMS)
     sends = jnp.zeros((8, B), jnp.int32)
     for at in range(max(ROOMS)):
         chosen = (holder == chip) & (ranks == 2 * at + core) & (which < count)
         row = jnp.sum(jnp.where(chosen, slots % 16, 0), axis=0, keepdims=True)
         sends = jnp.where(iota((8, B), 0) == at, jnp.broadcast_to(row, (8, B)), sends)
-    plan_ref[:8, :] = sends
-    plan_ref[8:32, :] = (holder * 2 + ranks % 2) * 8 + ranks // 2
-    plan_ref[32:, :] = slots
+    finds = (holder * 2 + ranks % 2) * 8 + ranks // 2
+    rest = jnp.zeros((B - 56, B), jnp.int32)
+    turned_ref[...] = jnp.concatenate((sends, finds, slots, rest), axis=0).T
+    section = lax.axis_index("z") * 16
+    send_ref[...] = turned_ref[pl.ds(pl.multiple_of(section, 16), 16), :]
+    find_ref[...] = jnp.broadcast_to(turned_ref[pl.ds(section + chip, 1), :], find_ref.shape)
 
 
 def away_kernel(
-    row_blocks, col_blocks, table_ref, live_ref, acts_ref, grads_ref, out_ref, crowd_ref, plan_ref, x_ref, y_ref, sems
+    row_blocks, col_blocks, table_ref, live_ref, acts_ref, grads_ref,
+    out_ref, branch_ref, send_ref, find_ref, x_ref, y_ref,
+    held_ref, turned_ref, sems,
 ):
-    first = pltpu.make_async_copy(acts_ref, x_ref, sems.at[0])
-    second = pltpu.make_async_copy(grads_ref, y_ref, sems.at[1])
-    first.start()
-    second.start()
-    make_plan(acts_ref.shape[1] // B, row_blocks, col_blocks, table_ref, crowd_ref, plan_ref)
-    first.wait()
-    second.wait()
-    slot_grams(live_ref[0], 1 - lax.axis_index("c"), table_ref, x_ref, y_ref, out_ref)
+    lookup = pltpu.make_async_copy(table_ref, held_ref, sems.at[PARTS + 1])
+    lookup.start()
+    copies = [pltpu.make_async_copy(acts_ref, x_ref, sems.at[0])]
+    width = grads_ref.shape[1] // PARTS
+    for part in range(PARTS):
+        cols = slice(part * width, (part + 1) * width)
+        copies.append(pltpu.make_async_copy(grads_ref.at[:, cols], y_ref.at[:, cols], sems.at[part + 1]))
+    for copy in copies:
+        copy.start()
+    lookup.wait()
+    make_plan(acts_ref.shape[1] // B, row_blocks, col_blocks, held_ref, branch_ref, send_ref, find_ref, turned_ref)
+    for copy in copies:
+        copy.wait()
+    slot_grams(live_ref[0], 1 - lax.axis_index("c"), held_ref, x_ref, y_ref, out_ref)
 
 
 def own_kernel(table_ref, live_ref, acts_ref, grads_ref, out_ref):
@@ -185,17 +232,27 @@
         out_shape=(
             GRAMS,
             jax.ShapeDtypeStruct((1,), jnp.int32),
-            jax.ShapeDtypeStruct((56, B), jnp.int32),
+            jax.ShapeDtypeStruct((16, B), jnp.int32),
+            jax.ShapeDtypeStruct((8, B), jnp.int32),
             jax.ShapeDtypeStruct(acts.shape, acts.dtype),
             jax.ShapeDtypeStruct(grads_out.shape, grads_out.dtype),
         ),
-        in_specs=[SMEM, SMEM, HBM, HBM],
-        out_specs=(VMEM, SMEM, VMEM, VMEM, VMEM),
-        scratch_shapes=[pltpu.SemaphoreType.DMA((2,))],
+        in_specs=[HBM, SMEM, HBM, HBM],
+        out_specs=(VMEM, SMEM, VMEM, VMEM, VMEM, VMEM),
+        scratch_shapes=[
+            pltpu.SMEM(table.shape, jnp.int32),
+            pltpu.VMEM((B, B), jnp.int32),
+            pltpu.SemaphoreType.DMA((PARTS + 2,)),
+        ],
         compiler_params=PARAMS,
         cost_estimate=pl.CostEstimate(flops=0, bytes_accessed=36 * 2**20, transcendentals=0),
         name="grams_away",
-    )(table, live, acts, grads_out)
+    )(
+        pltpu.with_memory_space_constraint(table, pltpu.HBM),
+        live,
+        pltpu.with_memory_space_constraint(acts, pltpu.HBM),
+        pltpu.with_memory_space_constraint(grads_out, pltpu.HBM),
+    )
 
 
 def own_grams(table, live, acts, grads_out):
@@ -241,7 +298,7 @@
     return jnp.sum(jnp.where(iota((EXTRA, B), 0) == at, rows, 0.0), axis=0, keepdims=True)
 
 
-def inverse_kernel(parts_ref, old_ref, cov_ref, out_ref, new_ref, sem):
+def inverse_kernel(parts_ref, old_ref, cov_ref, out_ref):
     half = parts_ref[0, :H, :].astype(F32)
     extra = parts_ref[0, H:, :].astype(F32)
     for s in range(1, 8):
@@ -250,15 +307,12 @@
     total = extra[1:2, :] * 256.0 + extra[2:3, :]
     gram = unpack(half, extra[:1, :])
     cov = 0.8 * old_ref[0, 0] + 0.2 * gram / total
-    new_ref[0, 0] = cov
-    copy = pltpu.make_async_copy(new_ref, cov_ref, sem)
-    copy.start()
+    cov_ref[0, 0] = cov
     eye = jnp.where(iota((B, B), 0) == iota((B, B), 1), 0.1, 0.0)
     inv_half, inv_diag = pack(invert(cov + eye))
     packed = jnp.concatenate((inv_half, jnp.broadcast_to(inv_diag, (EXTRA, B))), axis=0).astype(BF)
     for section in range(8):
         out_ref[section] = packed
-    copy.wait()
 
 
 def inverse(parts, old_cov):
@@ -269,20 +323,19 @@
             jax.ShapeDtypeStruct((8, H + EXTRA, B), BF),
         ),
         in_specs=[VMEM, VMEM],
-        out_specs=(HBM, VMEM),
-        scratch_shapes=[pltpu.VMEM(old_cov.shape, F32), pltpu.SemaphoreType.DMA],
+        out_specs=(VMEM, VMEM),
         compiler_params=PARAMS,
         name="inverse",
     )(parts, old_cov)
 
 
-def route_kernel(room, plan_ref, mine_ref, other_ref, out_ref):
-    core, lane = lax.axis_index("c"), lax.axis_index("z") * 16
+def route_kernel(room, send_ref, mine_ref, other_ref, out_ref):
+    core = lax.axis_index("c")
     for chip in range(16):
         diags = jnp.zeros((EXTRA, B), F32)
         for at in range(room):
             if room in ROOMS:
-                index = plan_ref[at, lane + chip]
+                index = send_ref[chip, at]
                 block = jnp.where(index // 8 == core, mine_ref[index % 8], other_ref[index % 8])
             else:
                 block = mine_ref[at]
@@ -291,7 +344,7 @@
         out_ref[chip, room * H :, :] = diags.astype(BF)
 
 
-def route(room, plans, mine, other):
+def route(room, sends, mine, other):
     return pl.pallas_call(
         functools.partial(route_kernel, room),
         out_shape=jax.ShapeDtypeStruct((16, room * H + EXTRA, B), BF),
@@ -299,33 +352,53 @@
         out_specs=VMEM,
         compiler_params=PARAMS,
         name="route",
-    )(plans, mine, other)
-
-
-def final_kernel(room, plan_ref, mine_ref, other_ref, weight_ref, out_ref, left_ref, right_ref, sems):
+    )(sends, mine, other)
+
+
+def pick_kernel(room, col_blocks, find_ref, got_ref, keep_ref, give_ref):
     core = lax.axis_index("c")
-    lane = lax.axis_index("z") * 16 + lax.axis_index("y") * 4 + lax.axis_index("x")
+    for ref, column in ((keep_ref, core), (give_ref, 1 - core)):
+        for want in range(ref.shape[0]):
+            index = column * col_blocks + want if want < col_blocks else col_blocks + want
+            found = find_ref[0, (8 if room in ROOMS else 32) + index]
+            chip, at = found // 16, found % 8
+            rows = pl.ds(pl.multiple_of(at * H, H), H)
+            ref[want, :H, :] = got_ref[chip, rows, :]
+            diag = take_row(got_ref[chip, room * H :, :].astype(F32), at)
+            ref[want, H:, :] = jnp.broadcast_to(diag, (EXTRA, B)).astype(BF)
+
+
+def pick(room, finds, got, row_blocks, col_blocks):
+    out = jax.ShapeDtypeStruct((col_blocks + row_blocks, H + EXTRA, B), BF)
+    return pl.pallas_call(
+        functools.partial(pick_kernel, room, col_blocks),
+        out_shape=(out, out),
+        in_specs=[SMEM, VMEM],
+        out_specs=(VMEM, VMEM),
+        compiler_params=PARAMS,
+        name="pick",
+    )(finds, got)
+
+
+def final_kernel(find_ref, branch_ref, mine_ref, other_ref, weight_ref, out_ref, left_ref, right_ref, sems):
+    core = lax.axis_index("c")
     row_blocks = weight_ref.shape[0] // B
     col_blocks = weight_ref.shape[1] // B
-
-    def block(index):
-        found = plan_ref[(8 if room in ROOMS else 32) + index, lane]
-        holder, at = found // 8, found % 8
-        same = holder % 2 == core
-        chip = holder // 2
-        rows = pl.ds(pl.multiple_of(at * H, H), H)
-        half = jnp.where(same, mine_ref[chip, rows, :], other_ref[chip, rows, :]).astype(F32)
-        diags = jnp.where(same, mine_ref[chip, room * H :, :], other_ref[chip, room * H :, :]).astype(F32)
-        return unpack(half, take_row(diags, at)).astype(BF)
-
-    col_invs = [block(core * col_blocks + j) for j in range(col_blocks)]
+    base = jnp.where(branch_ref[0] < len(ROOMS), 8, 32)
+
+    def block(want, index):
+        same = (find_ref[0, base + index] // 8) % 2 == core
+        packed = jnp.where(same, mine_ref[want], other_ref[want]).astype(F32)
+        return unpack(packed[:H, :], packed[H : H + 1, :]).astype(BF)
+
+    col_invs = [block(j, core * col_blocks + j) for j in range(col_blocks)]
     copies = []
-    strips = 2
-    for strip in range(strips):
-        span = row_blocks // strips
+    span = row_blocks // STRIPS
+    for strip in range(STRIPS):
         for i in range(strip * span, (strip + 1) * span):
             rows = slice(i * B, (i + 1) * B)
-            left = jnp.dot(block(2 * col_blocks + i), weight_ref[rows, :], preferred_element_type=F32)
+            inv = block(col_blocks + i, 2 * col_blocks + i)
+            left = jnp.dot(inv, weight_ref[rows, :], preferred_element_type=F32)
             left_ref[rows, :] = left.astype(BF)
         rows = slice(strip * span * B, (strip + 1) * span * B)
         for j in range(col_blocks):
@@ -338,20 +411,20 @@
         copy.wait()
 
 
-def final(room, plans, mine, other, weight_grad):
-    return pl.pallas_call(
-        functools.partial(final_kernel, room),
+def final(finds, branch, mine, other, weight_grad):
+    return pl.pallas_call(
+        final_kernel,
         out_shape=jax.ShapeDtypeStruct(weight_grad.shape, BF),
-        in_specs=[SMEM, VMEM, VMEM, VMEM],
+        in_specs=[SMEM, SMEM, VMEM, VMEM, VMEM],
         out_specs=HBM,
         scratch_shapes=[
             pltpu.VMEM(weight_grad.shape, BF),
             pltpu.VMEM(weight_grad.shape, BF),
-            pltpu.SemaphoreType.DMA((2,)),
+            pltpu.SemaphoreType.DMA((STRIPS,)),
         ],
         compiler_params=PARAMS,
         name="final",
-    )(plans, mine, other, weight_grad)
+    )(finds, branch, mine, other, weight_grad)
 
 
 def on_device(acts, grads_out, weight_grad, slot_table, row_counts, old_cov):
@@ -361,29 +434,28 @@
     exchange = functools.partial(lax.all_to_all, split_axis=0, concat_axis=0, tiled=True)
     swap = functools.partial(lax.ppermute, axis_name="c", perm=[(0, 1), (1, 0)])
 
-    away, crowd, plans, acts_held, grads_held = away_grams(
+    away, branch, sends, finds, acts_held, grads_held = away_grams(
         slot_table, row_counts, acts, grads_out, row_blocks, col_blocks
     )
     got = swap(away)
     own = own_grams(slot_table, row_counts, acts_held, grads_held)
     sums = (own.astype(F32) + got.astype(F32)).astype(BF)
-    branch = sum((crowd[0] >= 2 * room).astype(jnp.int32) for room in ROOMS)
-    sums, branch = lax.optimization_barrier((sums, branch))
     parts = exchange(sums.reshape(16, -1, B), plane)
     parts = exchange(section_sum(parts), "z")
     new_cov, inv = inverse(parts, old_cov)
     mine = exchange(inv, "z")
 
-    def compact(room, plans, mine, weight_grad):
-        got = exchange(route(room, plans, mine, swap(mine)), plane)
-        return final(room, plans, got, swap(got), weight_grad)
-
-    def full(plans, mine, weight_grad):
-        got = exchange(route(8, plans, mine, mine), plane)
-        return final(8, plans, got, swap(got), weight_grad)
+    def compact(room, sends, finds, mine):
+        got = exchange(route(room, sends, mine, swap(mine)), plane)
+        return pick(room, finds, got, row_blocks, col_blocks)
+
+    def full(sends, finds, mine):
+        got = exchange(route(8, sends, mine, mine), plane)
+        return pick(8, finds, got, row_blocks, col_blocks)
 
     branches = [functools.partial(compact, room) for room in ROOMS] + [full]
-    return lax.switch(branch, branches, plans, mine, weight_grad), new_cov
+    keep, give = lax.switch(branch[0], branches, sends, finds, mine)
+    return final(finds, branch, keep, swap(give), weight_grad), new_cov
 
 
 def solution(mesh):

time: 125 us -> 116 us (0.928)
  local copies, waits for them, and re-layouts: 5.88 us -> 0.01 us
  waiting for transfers between devices: 11.3 us -> 9.72 us
    unnamed x12 -> x6, local copies, waits for them, and re-layouts: 5.88 us -> 0.01 us
    pallas_call x1 -> x2, Pallas kernels: 2.72 us -> 4 us  [the longest x1 3.18 us: final(): pl.pallas_call(final_kernel, out_shape=jax.ShapeDtypeStruct(weight_grad.s...]
  transfers between devices with their start and end apart: 4 -> 4, of which waited for: 3 -> 3; matrix products, arithmetic and copies ran while one was open for 0% -> 0% of each run, Pallas kernels for 4% -> 3%
where the time goes in v5:
time: 116 us
  blocking collectives  67.1 us (58%)
  Pallas kernels  23.9 us (21%)
  starting transfers between devices  12.4 us (11%)
  waiting for transfers between devices  9.72 us (8%)
  between operations  1.97 us (2%)
    all_to_all x1, blocking collectives, on_device(): parts = exchange(sums.reshape(16, -1, B), plane)  33.3 us
    all_to_all x1, blocking collectives, compact(): got = exchange(route(room, sends, mine, swap(mine)), plane)  17.5 us
    all_to_all x1, blocking collectives, on_device(): parts = exchange(section_sum(parts), 'z')  16.3 us
    all_to_all x1, waiting for transfers between devices, on_device(): mine = exchange(inv, 'z')  7.55 us
    pallas_call x1, Pallas kernels, away_grams(): pl.pallas_call(functools.partial(away_kernel, row_blocks, col_blocks), ou...  7.32 us
    pallas_call x1, Pallas kernels, inverse(): pl.pallas_call(inverse_kernel, out_shape=(jax.ShapeDtypeStruct(old_cov.sh...  7.14 us
    ppermute x1, starting transfers between devices, compact(): got = exchange(route(room, sends, mine, swap(mine)), plane)  4.17 us
    pallas_call x1, Pallas kernels, own_grams(): pl.pallas_call(own_kernel, out_shape=GRAMS, in_specs=[SMEM, SMEM, VMEM, V...  4.04 us
  transfers between devices with their start and end apart: 4, of which 3 were waited for; matrix products, arithmetic and copies ran while one was open for 0% of the time, Pallas kernels for 3%

profile of v5, /device:TPU:1, one launch (start us, length us, event | category | flops | bytes accessed | tf_op | source)
XLA Modules:
  0.0 115.7 jit_solution(11759926323067640008)
XLA Ops:
  1.3 0.0 copy-start.2
  1.3 7.3 %grams_away.1 = (bf16[8448,128]{1,0:T(8,128)(2,1)S(1)}, s32[1]{0:T(128)}, s32[16,128]{1,0:T(8,128)S(1)}, s32[8,128]{1,0:T(8,128)S(1)}, bf16[128,6144]{1,0:T(8,128)(2,1)S(1)}, /*index=5*/bf16[128,24576]{1,0:T(8,128)(2,1)S(1)}) custom-call(s32[256]{0:T(256)} %table_ref.3, s32[1]{0:T(128)S(6)} %copy.14.live_ref, bf16[128,6144]{1,0:T(8,128)(2,1)} %acts_ref.1, ...), custom_call_target="tpu_custom_call" | custom-call | bytes 37748736 | tf_op jit(solution)/shard_map/grams_away/pallas_call | solution.py:230
  8.6 3.3 %collective-permute-start.2 = (bf16[8448,128]{1,0:T(8,128)(2,1)S(1)}, bf16[8448,128]{1,0:T(8,128)(2,1)S(1)}, u32[]{:S(2)}, u32[]{:S(2)}) collective-permute-start(bf16[8448,128]{1,0:T(8,128)(2,1)S(1)} %get-tuple-element.43), channel_id=1, source_target_pairs={{0,1},{1,0},{2,3},{3,2},{4,5},{5,4},{6,7},{7,6},{8,9},{9,8},{10,11... | collective-permute-start | bytes 6488072 | tf_op jit(solution)/shard_map/ppermute | solution.py:440
  11.9 0.0 copy-done.2
  11.9 4.0 %grams_own.1 = bf16[8448,128]{1,0:T(8,128)(2,1)S(1)} custom-call(s32[256]{0:T(256)S(1)} %copy-done.2, s32[1]{0:T(128)S(6)} %copy.14.live_ref, bf16[128,6144]{1,0:T(8,128)(2,1)S(1)} %get-tuple-element.41.acts_ref, bf16[128,24576]{1,0:T(8,128)(2,1)S(1)} %get-tuple-element.42.grads_ref), custom_call_target="tpu_custom_call" | custom-call | bytes 18874368 | tf_op jit(solution)/shard_map/grams_own/pallas_call | solution.py:259
  16.0 0.0 collective-permute-done.2
  16.0 0.6 add_convert_fusion
  16.6 33.3 %all_to_all.30.parts_ref = bf16[16,528,128]{2,1,0:T(8,128)(2,1)S(1)} all-to-all(bf16[16,528,128]{2,1,0:T(8,128)(2,1)S(1)} %bitcast.2), channel_id=1, replica_groups=mesh['z'=8,'y'=4,'x'=4,'c'=2] {'y','x'}, dimensions={0} | all-to-all | bytes 4325376 | tf_op jit(solution)/shard_map/all_to_all | solution.py:443
  49.9 0.3 section_sum.1
  50.2 16.3 %all_to_all.31.parts_ref = bf16[8,80,128]{2,1,0:T(8,128)(2,1)S(1)} all-to-all(bf16[8,80,128]{2,1,0:T(8,128)(2,1)S(1)} %section_sum.1), channel_id=1, replica_groups=mesh['z'=8,'y'=4,'x'=4,'c'=2] {'z'}, dimensions={0} | all-to-all | bytes 327680 | tf_op jit(solution)/shard_map/all_to_all | solution.py:444
  66.5 0.0 copy-done.1
  66.5 7.1 %inverse.1 = (f32[1,1,128,128]{3,2,1,0:T(8,128)}, bf16[8,80,128]{2,1,0:T(8,128)(2,1)}) custom-call(bf16[8,80,128]{2,1,0:T(8,128)(2,1)S(1)} %all_to_all.31.parts_ref, f32[1,1,128,128]{3,2,1,0:T(8,128)S(1)} %copy-done.1), custom_call_target="tpu_custom_call" | custom-call | tf_op jit(solution)/shard_map/inverse/pallas_call | solution.py:319
  73.6 3.4 %all-to-all-start.5 = ((bf16[8,80,128]{2,1,0:T(8,128)(2,1)}), bf16[8,80,128]{2,1,0:T(8,128)(2,1)S(1)}, u32[]{:S(2)}, u32[]{:S(2)}) async-start(bf16[8,80,128]{2,1,0:T(8,128)(2,1)} %get-tuple-element.44), calls=%async_computation.5 | async-start | bytes 327680 | tf_op jit(solution)/shard_map/all_to_all | solution.py:446
  77.6 7.6 %all-to-all-done.5 = bf16[8,80,128]{2,1,0:T(8,128)(2,1)S(1)} async-done(((bf16[8,80,128]{2,1,0:T(8,128)(2,1)}), bf16[8,80,128]{2,1,0:T(8,128)(2,1)S(1)}, u32[]{:S(2)}, u32[]{:S(2)}) %all-to-all-start.5) | async-done | bytes 163872 | tf_op jit(solution)/shard_map/all_to_all | solution.py:446
  85.2 24.7 %conditional.1 = ((bf16[12,80,128]{2,1,0:T(8,128)(2,1)S(1)}, bf16[12,80,128]{2,1,0:T(8,128)(2,1)S(1)})) conditional(s32[]{:T(128)} %bitcast, (bf16[8,80,128]{2,1,0:T(8,128)(2,1)S(1)}, s32[16,128]{1,0:T(8,128)S(1)}, s32[8,128]{1,0:T(8,128)S(1)}) %tuple.17, (bf16[8,80,128]{2,1,0:T(8,128)(2,1)S(1)}, s32[16,128]{1,0:T(8,128)S(1)}, ...), branch_computations={%region_0.0_spmd, %region_1.0_spmd, %region_2.0_spmd} | conditional | bytes 4325384 | solution.py:457
  85.2 4.2 %collective-permute-start = (bf16[8,80,128]{2,1,0:T(8,128)(2,1)S(1)}, bf16[8,80,128]{2,1,0:T(8,128)(2,1)S(1)}, u32[]{:S(2)}, u32[]{:S(2)}) collective-permute-start(bf16[8,80,128]{2,1,0:T(8,128)(2,1)S(1)} %get-tuple-element.20.mine_ref), channel_id=1, source_target_pairs={{0,1},{1,0},{2,3},{3,2},{4,5},{5,4},{6,7},{7,6},{8,9},{9,8},{10,11... | collective-permute-start | bytes 491528 | tf_op jit(solution)/shard_map/cond/branch_0_fun/ppermute | solution.py:449
  89.4 1.0 collective-permute-done.other_ref
  90.4 1.1 route.3
  91.5 17.5 %all_to_all.27.got_ref = bf16[16,208,128]{2,1,0:T(8,128)(2,1)S(1)} all-to-all(bf16[16,208,128]{2,1,0:T(8,128)(2,1)S(1)} %route.3), channel_id=1, replica_groups=mesh['z'=8,'y'=4,'x'=4,'c'=2] {'y','x'}, dimensions={0} | all-to-all | bytes 1703936 | tf_op jit(solution)/shard_map/cond/branch_0_fun/all_to_all | solution.py:449
  109.0 0.8 pick.3
  109.9 1.6 %collective-permute-start.3 = (bf16[12,80,128]{2,1,0:T(8,128)(2,1)S(1)}, bf16[12,80,128]{2,1,0:T(8,128)(2,1)S(1)}, u32[]{:S(2)}, u32[]{:S(2)}) collective-permute-start(bf16[12,80,128]{2,1,0:T(8,128)(2,1)S(1)} %get-tuple-element.47), channel_id=1, source_target_pairs={{0,1},{1,0},{2,3},{3,2},{4,5},{5,4},{6,7},{7,6},{8,9},{9,8},{10,11... | collective-permute-start | bytes 737288 | tf_op jit(solution)/shard_map/ppermute | solution.py:458
  111.4 1.1 collective-permute-done.3.other_ref
  112.6 0.0 copy-done
  112.6 3.2 %final.1 = bf16[768,768]{1,0:T(8,128)(2,1)} custom-call(s32[8,128]{1,0:T(8,128)S(1)} %get-tuple-element.39.find_ref, s32[1]{0:T(128)} %get-tuple-element.40.branch_ref, bf16[12,80,128]{2,1,0:T(8,128)(2,1)S(1)} %get-tuple-element.46.mine_ref, bf16[12,80,128]{2,1,0:T(8,128)(2,1)S(1)} %collective-permute-done.3.other_ref, bf16[768,768]{1,0:T(8,128)(2,1)S(1)} %copy-done), custom_call_target="tpu_custom_call" | custom-call | tf_op jit(solution)/shard_map/final/pallas_call | solution.py:415
  (2 shorter events, 0.0 us)
Async XLA Ops:
  1.3 10.7 %copy-start.2 = (s32[256]{0:T(256)S(1)}, s32[256]{0:T(256)}, u32[]{:S(2)}) copy-start(s32[256]{0:T(256)} %table_ref.3) | copy-start | bytes 3076
  8.6 7.4 %collective-permute-start.2 = (bf16[8448,128]{1,0:T(8,128)(2,1)S(1)}, bf16[8448,128]{1,0:T(8,128)(2,1)S(1)}, u32[]{:S(2)}, u32[]{:S(2)}) collective-permute-start(bf16[8448,128]{1,0:T(8,128)(2,1)S(1)} %get-tuple-element.43), channel_id=1, source_target_pairs={{0,1},{1,0},{2,3},{3,2},{4,5},{5,4},{6,7},{7,6},{8,9},{9,8},{10,11... | collective-permute-start | bytes 6488072 | tf_op jit(solution)/shard_map/ppermute | solution.py:440
  49.9 16.6 %copy-start.1 = (f32[1,1,128,128]{3,2,1,0:T(8,128)S(1)}, f32[1,1,128,128]{3,2,1,0:T(8,128)}, u32[]{:S(2)}) copy-start(f32[1,1,128,128]{3,2,1,0:T(8,128)} %old_ref.1) | copy-start | bytes 196612
  73.6 11.6 %all-to-all-start.5 = ((bf16[8,80,128]{2,1,0:T(8,128)(2,1)}), bf16[8,80,128]{2,1,0:T(8,128)(2,1)S(1)}, u32[]{:S(2)}, u32[]{:S(2)}) async-start(bf16[8,80,128]{2,1,0:T(8,128)(2,1)} %get-tuple-element.44), calls=%async_computation.5 | async-start | bytes 327680 | tf_op jit(solution)/shard_map/all_to_all | solution.py:446
  85.2 27.4 %copy-start = (bf16[768,768]{1,0:T(8,128)(2,1)S(1)}, bf16[768,768]{1,0:T(8,128)(2,1)}, u32[]{:S(2)}) copy-start(bf16[768,768]{1,0:T(8,128)(2,1)} %weight_ref.1) | copy-start | bytes 3538948
  85.2 5.2 %collective-permute-start = (bf16[8,80,128]{2,1,0:T(8,128)(2,1)S(1)}, bf16[8,80,128]{2,1,0:T(8,128)(2,1)S(1)}, u32[]{:S(2)}, u32[]{:S(2)}) collective-permute-start(bf16[8,80,128]{2,1,0:T(8,128)(2,1)S(1)} %get-tuple-element.20.mine_ref), channel_id=1, source_target_pairs={{0,1},{1,0},{2,3},{3,2},{4,5},{5,4},{6,7},{7,6},{8,9},{9,8},{10,11... | collective-permute-start | bytes 491528 | tf_op jit(solution)/shard_map/cond/branch_0_fun/ppermute | solution.py:449
  109.9 2.7 %collective-permute-start.3 = (bf16[12,80,128]{2,1,0:T(8,128)(2,1)S(1)}, bf16[12,80,128]{2,1,0:T(8,128)(2,1)S(1)}, u32[]{:S(2)}, u32[]{:S(2)}) collective-permute-start(bf16[12,80,128]{2,1,0:T(8,128)(2,1)S(1)} %get-tuple-element.47), channel_id=1, source_target_pairs={{0,1},{1,0},{2,3},{3,2},{4,5},{5,4},{6,7},{7,6},{8,9},{9,8},{10,11... | collective-permute-start | bytes 737288 | tf_op jit(solution)/shard_map/ppermute | solution.py:458

commit v6 on v5

--- a/solution.py
+++ b/solution.py
@@ -14,7 +14,7 @@
 F32 = jnp.float32
 EXTRA = 16
 ROOMS = (3, 4)
-PARTS = 3
+PARTS = 6
 STRIPS = 2
 VMEM_LIMIT = 24 * 1024 * 1024
 
@@ -138,11 +138,10 @@
     return mat
 
 
-def slot_grams(live, want, table_ref, acts_ref, grads_ref, out_ref):
-    in_blocks = acts_ref.shape[1] // B
-    out_blocks = grads_ref.shape[1] // B
+def slot_grams(live, want, table_ref, x_ref, out_ref):
+    blocks = x_ref.shape[1] // B
     group_rows = 8 * H + EXTRA
-    unroll = 4
+    unroll = 8
 
     @pl.loop(0, 16 // unroll)
     def _(trip):
@@ -153,9 +152,8 @@
             for row in range(8):
                 which = table_ref[(group * 2 + want) * 8 + row]
                 filled = jnp.where(which >= 0, live, 0)
-                first = pl.multiple_of(jnp.clip(which, 0, in_blocks - 1) * B, B)
-                second = pl.multiple_of(jnp.clip(which - in_blocks, 0, out_blocks - 1) * B, B)
-                x = jnp.where(which < in_blocks, acts_ref[:, pl.ds(first, B)], grads_ref[:, pl.ds(second, B)])
+                first = pl.multiple_of(jnp.clip(which, 0, blocks - 1) * B, B)
+                x = x_ref[:, pl.ds(first, B)]
                 x = jnp.where(iota(x.shape, 0) < filled, x, jnp.zeros_like(x))
                 gram = lax.dot_general(x, x, (((0,), (0,)), ((), ())), preferred_element_type=F32)
                 half, diag = pack(gram)
@@ -184,15 +182,17 @@
         same = holder == jnp.broadcast_to(holder[at : at + 1, :], holder.shape)
         ranks += jnp.where(same & (which > at), 1, 0)
     most = jnp.max(jnp.where(which < count, ranks, 0))
-    branch_ref[0] = sum((most >= 2 * room).astype(jnp.int32) for room in ROOMS)
     sends = jnp.zeros((8, B), jnp.int32)
     for at in range(max(ROOMS)):
         chosen = (holder == chip) & (ranks == 2 * at + core) & (which < count)
         row = jnp.sum(jnp.where(chosen, slots % 16, 0), axis=0, keepdims=True)
         sends = jnp.where(iota((8, B), 0) == at, jnp.broadcast_to(row, (8, B)), sends)
     finds = (holder * 2 + ranks % 2) * 8 + ranks // 2
-    rest = jnp.zeros((B - 56, B), jnp.int32)
-    turned_ref[...] = jnp.concatenate((sends, finds, slots, rest), axis=0).T
+    branch = sum((most >= 2 * room).astype(jnp.int32) for room in ROOMS)
+    branch_ref[0] = branch
+    cores = jnp.where(branch < len(ROOMS), ranks, slots // 8) % 2
+    rest = jnp.zeros((B - 80, B), jnp.int32)
+    turned_ref[...] = jnp.concatenate((sends, finds, slots, cores, rest), axis=0).T
     section = lax.axis_index("z") * 16
     send_ref[...] = turned_ref[pl.ds(pl.multiple_of(section, 16), 16), :]
     find_ref[...] = jnp.broadcast_to(turned_ref[pl.ds(section + chip, 1), :], find_ref.shape)
@@ -200,27 +200,29 @@
 
 def away_kernel(
     row_blocks, col_blocks, table_ref, live_ref, acts_ref, grads_ref,
-    out_ref, branch_ref, send_ref, find_ref, x_ref, y_ref,
+    out_ref, branch_ref, send_ref, find_ref, x_ref,
     held_ref, turned_ref, sems,
 ):
     lookup = pltpu.make_async_copy(table_ref, held_ref, sems.at[PARTS + 1])
     lookup.start()
-    copies = [pltpu.make_async_copy(acts_ref, x_ref, sems.at[0])]
+    inner = acts_ref.shape[1]
+    copies = [pltpu.make_async_copy(acts_ref, x_ref.at[:, :inner], sems.at[0])]
     width = grads_ref.shape[1] // PARTS
     for part in range(PARTS):
-        cols = slice(part * width, (part + 1) * width)
-        copies.append(pltpu.make_async_copy(grads_ref.at[:, cols], y_ref.at[:, cols], sems.at[part + 1]))
+        source = grads_ref.at[:, part * width : (part + 1) * width]
+        target = x_ref.at[:, inner + part * width : inner + (part + 1) * width]
+        copies.append(pltpu.make_async_copy(source, target, sems.at[part + 1]))
     for copy in copies:
         copy.start()
     lookup.wait()
     make_plan(acts_ref.shape[1] // B, row_blocks, col_blocks, held_ref, branch_ref, send_ref, find_ref, turned_ref)
     for copy in copies:
         copy.wait()
-    slot_grams(live_ref[0], 1 - lax.axis_index("c"), held_ref, x_ref, y_ref, out_ref)
-
-
-def own_kernel(table_ref, live_ref, acts_ref, grads_ref, out_ref):
-    slot_grams(live_ref[0], lax.axis_index("c"), table_ref, acts_ref, grads_ref, out_ref)
+    slot_grams(live_ref[0], 1 - lax.axis_index("c"), held_ref, x_ref, out_ref)
+
+
+def own_kernel(table_ref, live_ref, x_ref, out_ref):
+    slot_grams(live_ref[0], lax.axis_index("c"), table_ref, x_ref, out_ref)
 
 
 GRAMS = jax.ShapeDtypeStruct((16 * (8 * H + EXTRA), B), BF)
@@ -234,11 +236,10 @@
             jax.ShapeDtypeStruct((1,), jnp.int32),
             jax.ShapeDtypeStruct((16, B), jnp.int32),
             jax.ShapeDtypeStruct((8, B), jnp.int32),
-            jax.ShapeDtypeStruct(acts.shape, acts.dtype),
-            jax.ShapeDtypeStruct(grads_out.shape, grads_out.dtype),
+            jax.ShapeDtypeStruct((acts.shape[0], acts.shape[1] + grads_out.shape[1]), BF),
         ),
         in_specs=[HBM, SMEM, HBM, HBM],
-        out_specs=(VMEM, SMEM, VMEM, VMEM, VMEM, VMEM),
+        out_specs=(VMEM, SMEM, VMEM, VMEM, VMEM),
         scratch_shapes=[
             pltpu.SMEM(table.shape, jnp.int32),
             pltpu.VMEM((B, B), jnp.int32),
@@ -255,16 +256,16 @@
     )
 
 
-def own_grams(table, live, acts, grads_out):
+def own_grams(table, live, held):
     return pl.pallas_call(
         own_kernel,
         out_shape=GRAMS,
-        in_specs=[SMEM, SMEM, VMEM, VMEM],
+        in_specs=[SMEM, SMEM, VMEM],
         out_specs=VMEM,
         compiler_params=PARAMS,
         cost_estimate=pl.CostEstimate(flops=0, bytes_accessed=18 * 2**20, transcendentals=0),
         name="grams_own",
-    )(table, live, acts, grads_out)
+    )(table, live, held)
 
 
 def section_kernel(parts_ref, out_ref):
@@ -380,14 +381,13 @@
     )(finds, got)
 
 
-def final_kernel(find_ref, branch_ref, mine_ref, other_ref, weight_ref, out_ref, left_ref, right_ref, sems):
+def final_kernel(find_ref, mine_ref, other_ref, weight_ref, out_ref, left_ref, right_ref, sems):
     core = lax.axis_index("c")
     row_blocks = weight_ref.shape[0] // B
     col_blocks = weight_ref.shape[1] // B
-    base = jnp.where(branch_ref[0] < len(ROOMS), 8, 32)
 
     def block(want, index):
-        same = (find_ref[0, base + index] // 8) % 2 == core
+        same = find_ref[0, 56 + index] == core
         packed = jnp.where(same, mine_ref[want], other_ref[want]).astype(F32)
         return unpack(packed[:H, :], packed[H : H + 1, :]).astype(BF)
 
@@ -411,11 +411,11 @@
         copy.wait()
 
 
-def final(finds, branch, mine, other, weight_grad):
+def final(finds, mine, other, weight_grad):
     return pl.pallas_call(
         final_kernel,
         out_shape=jax.ShapeDtypeStruct(weight_grad.shape, BF),
-        in_specs=[SMEM, SMEM, VMEM, VMEM, VMEM],
+        in_specs=[SMEM, VMEM, VMEM, VMEM],
         out_specs=HBM,
         scratch_shapes=[
             pltpu.VMEM(weight_grad.shape, BF),
@@ -424,7 +424,7 @@
         ],
         compiler_params=PARAMS,
         name="final",
-    )(finds, branch, mine, other, weight_grad)
+    )(finds, mine, other, weight_grad)
 
 
 def on_device(acts, grads_out, weight_grad, slot_table, row_counts, old_cov):
@@ -434,11 +434,11 @@
     exchange = functools.partial(lax.all_to_all, split_axis=0, concat_axis=0, tiled=True)
     swap = functools.partial(lax.ppermute, axis_name="c", perm=[(0, 1), (1, 0)])
 
-    away, branch, sends, finds, acts_held, grads_held = away_grams(
+    away, branch, sends, finds, held = away_grams(
         slot_table, row_counts, acts, grads_out, row_blocks, col_blocks
     )
     got = swap(away)
-    own = own_grams(slot_table, row_counts, acts_held, grads_held)
+    own = own_grams(slot_table, row_counts, held)
     sums = (own.astype(F32) + got.astype(F32)).astype(BF)
     parts = exchange(sums.reshape(16, -1, B), plane)
     parts = exchange(section_sum(parts), "z")
@@ -455,7 +455,7 @@
 
     branches = [functools.partial(compact, room) for room in ROOMS] + [full]
     keep, give = lax.switch(branch[0], branches, sends, finds, mine)
-    return final(finds, branch, keep, swap(give), weight_grad), new_cov
+    return final(finds, keep, swap(give), weight_grad), new_cov
 
 
 def solution(mesh):

time: 116 us -> 114 us (0.983)
  Pallas kernels: 23.9 us -> 21.9 us
  transfers between devices with their start and end apart: 4 -> 4, of which waited for: 3 -> 4; matrix products, arithmetic and copies ran while one was open for 0% -> 0% of each run, Pallas kernels for 3% -> 3%
where the time goes in v6:
time: 114 us
  blocking collectives  66.9 us (59%)
  Pallas kernels  21.9 us (19%)
  starting transfers between devices  12.5 us (11%)
  waiting for transfers between devices  10.3 us (9%)
  between operations  1.96 us (2%)
    all_to_all x1, blocking collectives, on_device(): parts = exchange(sums.reshape(16, -1, B), plane)  33.1 us
    all_to_all x1, blocking collectives, compact(): got = exchange(route(room, sends, mine, swap(mine)), plane)  17.4 us
    all_to_all x1, blocking collectives, on_device(): parts = exchange(section_sum(parts), 'z')  16.4 us
    all_to_all x1, waiting for transfers between devices, on_device(): mine = exchange(inv, 'z')  7.61 us
    pallas_call x1, Pallas kernels, inverse(): pl.pallas_call(inverse_kernel, out_shape=(jax.ShapeDtypeStruct(old_cov.sh...  7.13 us
    pallas_call x1, Pallas kernels, away_grams(): pl.pallas_call(functools.partial(away_kernel, row_blocks, col_blocks), ou...  6.62 us
    ppermute x1, starting transfers between devices, compact(): got = exchange(route(room, sends, mine, swap(mine)), plane)  4.23 us
    all_to_all x1, starting transfers between devices, on_device(): mine = exchange(inv, 'z')  3.38 us
  transfers between devices with their start and end apart: 4, of which 4 were waited for; matrix products, arithmetic and copies ran while one was open for 0% of the time, Pallas kernels for 3%

profile of v6, /device:TPU:1, one launch (start us, length us, event | category | flops | bytes accessed | tf_op | source)
XLA Modules:
  0.0 114.1 jit_solution(7983414829863395575)
XLA Ops:
  1.3 0.0 copy-start.2
  1.3 6.6 %grams_away.1 = (bf16[8448,128]{1,0:T(8,128)(2,1)S(1)}, s32[1]{0:T(128)}, s32[16,128]{1,0:T(8,128)S(1)}, s32[8,128]{1,0:T(8,128)S(1)}, bf16[128,30720]{1,0:T(8,128)(2,1)S(1)}) custom-call(s32[256]{0:T(256)} %table_ref.3, s32[1]{0:T(128)S(6)} %copy.14.live_ref, bf16[128,6144]{1,0:T(8,128)(2,1)} %acts_ref.1, bf16[128,24576]{1,0:T(8,128)(2,1)} %grads_ref.1), custom_call_target="tpu_custom_call" | custom-call | bytes 37748736 | tf_op jit(solution)/shard_map/grams_away/pallas_call | solution.py:232
  7.9 3.3 %collective-permute-start.2 = (bf16[8448,128]{1,0:T(8,128)(2,1)S(1)}, bf16[8448,128]{1,0:T(8,128)(2,1)S(1)}, u32[]{:S(2)}, u32[]{:S(2)}) collective-permute-start(bf16[8448,128]{1,0:T(8,128)(2,1)S(1)} %get-tuple-element.41), channel_id=1, source_target_pairs={{0,1},{1,0},{2,3},{3,2},{4,5},{5,4},{6,7},{7,6},{8,9},{9,8},{10,11... | collective-permute-start | bytes 6488072 | tf_op jit(solution)/shard_map/ppermute | solution.py:440
  11.2 0.0 copy-done.2
  11.2 3.4 %grams_own.1 = bf16[8448,128]{1,0:T(8,128)(2,1)S(1)} custom-call(s32[256]{0:T(256)S(1)} %copy-done.2, s32[1]{0:T(128)S(6)} %copy.14.live_ref, bf16[128,30720]{1,0:T(8,128)(2,1)S(1)} %get-tuple-element.40.x_ref), custom_call_target="tpu_custom_call" | custom-call | bytes 18874368 | tf_op jit(solution)/shard_map/grams_own/pallas_call | solution.py:260
  14.6 0.5 collective-permute-done.2
  15.1 0.6 add_convert_fusion
  15.7 33.1 %all_to_all.30.parts_ref = bf16[16,528,128]{2,1,0:T(8,128)(2,1)S(1)} all-to-all(bf16[16,528,128]{2,1,0:T(8,128)(2,1)S(1)} %bitcast.2), channel_id=1, replica_groups=mesh['z'=8,'y'=4,'x'=4,'c'=2] {'y','x'}, dimensions={0} | all-to-all | bytes 4325376 | tf_op jit(solution)/shard_map/all_to_all | solution.py:443
  48.8 0.3 section_sum.1
  49.1 16.4 %all_to_all.31.parts_ref = bf16[8,80,128]{2,1,0:T(8,128)(2,1)S(1)} all-to-all(bf16[8,80,128]{2,1,0:T(8,128)(2,1)S(1)} %section_sum.1), channel_id=1, replica_groups=mesh['z'=8,'y'=4,'x'=4,'c'=2] {'z'}, dimensions={0} | all-to-all | bytes 327680 | tf_op jit(solution)/shard_map/all_to_all | solution.py:444
  65.5 0.0 copy-done.1
  65.5 7.1 %inverse.1 = (f32[1,1,128,128]{3,2,1,0:T(8,128)}, bf16[8,80,128]{2,1,0:T(8,128)(2,1)}) custom-call(bf16[8,80,128]{2,1,0:T(8,128)(2,1)S(1)} %all_to_all.31.parts_ref, f32[1,1,128,128]{3,2,1,0:T(8,128)S(1)} %copy-done.1), custom_call_target="tpu_custom_call" | custom-call | tf_op jit(solution)/shard_map/inverse/pallas_call | solution.py:320
  72.6 3.4 %all-to-all-start.5 = ((bf16[8,80,128]{2,1,0:T(8,128)(2,1)}), bf16[8,80,128]{2,1,0:T(8,128)(2,1)S(1)}, u32[]{:S(2)}, u32[]{:S(2)}) async-start(bf16[8,80,128]{2,1,0:T(8,128)(2,1)} %get-tuple-element.42), calls=%async_computation.5 | async-start | bytes 327680 | tf_op jit(solution)/shard_map/all_to_all | solution.py:446
  76.6 7.6 %all-to-all-done.5 = bf16[8,80,128]{2,1,0:T(8,128)(2,1)S(1)} async-done(((bf16[8,80,128]{2,1,0:T(8,128)(2,1)}), bf16[8,80,128]{2,1,0:T(8,128)(2,1)S(1)}, u32[]{:S(2)}, u32[]{:S(2)}) %all-to-all-start.5) | async-done | bytes 163872 | tf_op jit(solution)/shard_map/all_to_all | solution.py:446
  84.2 24.6 %conditional.1 = ((bf16[12,80,128]{2,1,0:T(8,128)(2,1)S(1)}, bf16[12,80,128]{2,1,0:T(8,128)(2,1)S(1)})) conditional(s32[]{:T(128)} %bitcast, (bf16[8,80,128]{2,1,0:T(8,128)(2,1)S(1)}, s32[16,128]{1,0:T(8,128)S(1)}, s32[8,128]{1,0:T(8,128)S(1)}) %tuple.17, (bf16[8,80,128]{2,1,0:T(8,128)(2,1)S(1)}, s32[16,128]{1,0:T(8,128)S(1)}, ...), branch_computations={%region_0.0_spmd, %region_1.0_spmd, %region_2.0_spmd} | conditional | bytes 4325384 | solution.py:457
  84.2 4.2 %collective-permute-start = (bf16[8,80,128]{2,1,0:T(8,128)(2,1)S(1)}, bf16[8,80,128]{2,1,0:T(8,128)(2,1)S(1)}, u32[]{:S(2)}, u32[]{:S(2)}) collective-permute-start(bf16[8,80,128]{2,1,0:T(8,128)(2,1)S(1)} %get-tuple-element.20.mine_ref), channel_id=1, source_target_pairs={{0,1},{1,0},{2,3},{3,2},{4,5},{5,4},{6,7},{7,6},{8,9},{9,8},{10,11... | collective-permute-start | bytes 491528 | tf_op jit(solution)/shard_map/cond/branch_0_fun/ppermute | solution.py:449
  88.5 1.0 collective-permute-done.other_ref
  89.5 1.1 route.3
  90.6 17.4 %all_to_all.27.got_ref = bf16[16,208,128]{2,1,0:T(8,128)(2,1)S(1)} all-to-all(bf16[16,208,128]{2,1,0:T(8,128)(2,1)S(1)} %route.3), channel_id=1, replica_groups=mesh['z'=8,'y'=4,'x'=4,'c'=2] {'y','x'}, dimensions={0} | all-to-all | bytes 1703936 | tf_op jit(solution)/shard_map/cond/branch_0_fun/all_to_all | solution.py:449
  108.0 0.8 pick.3
  108.8 1.6 %collective-permute-start.3 = (bf16[12,80,128]{2,1,0:T(8,128)(2,1)S(1)}, bf16[12,80,128]{2,1,0:T(8,128)(2,1)S(1)}, u32[]{:S(2)}, u32[]{:S(2)}) collective-permute-start(bf16[12,80,128]{2,1,0:T(8,128)(2,1)S(1)} %get-tuple-element.45), channel_id=1, source_target_pairs={{0,1},{1,0},{2,3},{3,2},{4,5},{5,4},{6,7},{7,6},{8,9},{9,8},{10,11... | collective-permute-start | bytes 737288 | tf_op jit(solution)/shard_map/ppermute | solution.py:458
  110.4 1.1 collective-permute-done.3.other_ref
  111.5 0.0 copy-done
  111.5 2.5 %final.1 = bf16[768,768]{1,0:T(8,128)(2,1)} custom-call(s32[8,128]{1,0:T(8,128)S(1)} %get-tuple-element.38.find_ref, bf16[12,80,128]{2,1,0:T(8,128)(2,1)S(1)} %get-tuple-element.44.mine_ref, bf16[12,80,128]{2,1,0:T(8,128)(2,1)S(1)} %collective-permute-done.3.other_ref, bf16[768,768]{1,0:T(8,128)(2,1)S(1)} %copy-done), custom_call_target="tpu_custom_call" | custom-call | tf_op jit(solution)/shard_map/final/pallas_call | solution.py:415
  (2 shorter events, 0.0 us)
Async XLA Ops:
  1.3 10.0 %copy-start.2 = (s32[256]{0:T(256)S(1)}, s32[256]{0:T(256)}, u32[]{:S(2)}) copy-start(s32[256]{0:T(256)} %table_ref.3) | copy-start | bytes 3076
  7.9 7.2 %collective-permute-start.2 = (bf16[8448,128]{1,0:T(8,128)(2,1)S(1)}, bf16[8448,128]{1,0:T(8,128)(2,1)S(1)}, u32[]{:S(2)}, u32[]{:S(2)}) collective-permute-start(bf16[8448,128]{1,0:T(8,128)(2,1)S(1)} %get-tuple-element.41), channel_id=1, source_target_pairs={{0,1},{1,0},{2,3},{3,2},{4,5},{5,4},{6,7},{7,6},{8,9},{9,8},{10,11... | collective-permute-start | bytes 6488072 | tf_op jit(solution)/shard_map/ppermute | solution.py:440
  48.8 16.7 %copy-start.1 = (f32[1,1,128,128]{3,2,1,0:T(8,128)S(1)}, f32[1,1,128,128]{3,2,1,0:T(8,128)}, u32[]{:S(2)}) copy-start(f32[1,1,128,128]{3,2,1,0:T(8,128)} %old_ref.1) | copy-start | bytes 196612
  72.6 11.6 %all-to-all-start.5 = ((bf16[8,80,128]{2,1,0:T(8,128)(2,1)}), bf16[8,80,128]{2,1,0:T(8,128)(2,1)S(1)}, u32[]{:S(2)}, u32[]{:S(2)}) async-start(bf16[8,80,128]{2,1,0:T(8,128)(2,1)} %get-tuple-element.42), calls=%async_computation.5 | async-start | bytes 327680 | tf_op jit(solution)/shard_map/all_to_all | solution.py:446
  84.2 27.3 %copy-start = (bf16[768,768]{1,0:T(8,128)(2,1)S(1)}, bf16[768,768]{1,0:T(8,128)(2,1)}, u32[]{:S(2)}) copy-start(bf16[768,768]{1,0:T(8,128)(2,1)} %weight_ref.1) | copy-start | bytes 3538948
  84.2 5.3 %collective-permute-start = (bf16[8,80,128]{2,1,0:T(8,128)(2,1)S(1)}, bf16[8,80,128]{2,1,0:T(8,128)(2,1)S(1)}, u32[]{:S(2)}, u32[]{:S(2)}) collective-permute-start(bf16[8,80,128]{2,1,0:T(8,128)(2,1)S(1)} %get-tuple-element.20.mine_ref), channel_id=1, source_target_pairs={{0,1},{1,0},{2,3},{3,2},{4,5},{5,4},{6,7},{7,6},{8,9},{9,8},{10,11... | collective-permute-start | bytes 491528 | tf_op jit(solution)/shard_map/cond/branch_0_fun/ppermute | solution.py:449
  108.8 2.7 %collective-permute-start.3 = (bf16[12,80,128]{2,1,0:T(8,128)(2,1)S(1)}, bf16[12,80,128]{2,1,0:T(8,128)(2,1)S(1)}, u32[]{:S(2)}, u32[]{:S(2)}) collective-permute-start(bf16[12,80,128]{2,1,0:T(8,128)(2,1)S(1)} %get-tuple-element.45), channel_id=1, source_target_pairs={{0,1},{1,0},{2,3},{3,2},{4,5},{5,4},{6,7},{7,6},{8,9},{9,8},{10,11... | collective-permute-start | bytes 737288 | tf_op jit(solution)/shard_map/ppermute | solution.py:458

commit v7 on v6

--- a/solution.py
+++ b/solution.py
@@ -13,7 +13,8 @@
 BF = jnp.bfloat16
 F32 = jnp.float32
 EXTRA = 16
-ROOMS = (3, 4)
+ROOMS = (5, 6, 8)
+Q = H // 2
 PARTS = 6
 STRIPS = 2
 VMEM_LIMIT = 24 * 1024 * 1024
@@ -164,7 +165,7 @@
 
 
 def make_plan(in_blocks, row_blocks, col_blocks, table_ref, branch_ref, send_ref, find_ref, turned_ref):
-    core, chip = lax.axis_index("c"), lax.axis_index("y") * 4 + lax.axis_index("x")
+    chip = lax.axis_index("y") * 4 + lax.axis_index("x")
     wide = 2 * col_blocks
     count = wide + row_blocks
     which, lane = iota((24, B), 0), iota((24, B), 1)
@@ -184,15 +185,14 @@
     most = jnp.max(jnp.where(which < count, ranks, 0))
     sends = jnp.zeros((8, B), jnp.int32)
     for at in range(max(ROOMS)):
-        chosen = (holder == chip) & (ranks == 2 * at + core) & (which < count)
+        chosen = (holder == chip) & (ranks == at) & (which < count)
         row = jnp.sum(jnp.where(chosen, slots % 16, 0), axis=0, keepdims=True)
         sends = jnp.where(iota((8, B), 0) == at, jnp.broadcast_to(row, (8, B)), sends)
-    finds = (holder * 2 + ranks % 2) * 8 + ranks // 2
-    branch = sum((most >= 2 * room).astype(jnp.int32) for room in ROOMS)
+    finds = holder * 8 + ranks
+    branch = sum((most >= room).astype(jnp.int32) for room in ROOMS)
     branch_ref[0] = branch
-    cores = jnp.where(branch < len(ROOMS), ranks, slots // 8) % 2
-    rest = jnp.zeros((B - 80, B), jnp.int32)
-    turned_ref[...] = jnp.concatenate((sends, finds, slots, cores, rest), axis=0).T
+    rest = jnp.zeros((B - 56, B), jnp.int32)
+    turned_ref[...] = jnp.concatenate((sends, finds, slots, rest), axis=0).T
     section = lax.axis_index("z") * 16
     send_ref[...] = turned_ref[pl.ds(pl.multiple_of(section, 16), 16), :]
     find_ref[...] = jnp.broadcast_to(turned_ref[pl.ds(section + chip, 1), :], find_ref.shape)
@@ -332,23 +332,23 @@
 
 def route_kernel(room, send_ref, mine_ref, other_ref, out_ref):
     core = lax.axis_index("c")
+    rows = pl.ds(pl.multiple_of(core * Q, Q), Q)
     for chip in range(16):
         diags = jnp.zeros((EXTRA, B), F32)
         for at in range(room):
-            if room in ROOMS:
-                index = send_ref[chip, at]
-                block = jnp.where(index // 8 == core, mine_ref[index % 8], other_ref[index % 8])
-            else:
-                block = mine_ref[at]
-            out_ref[chip, at * H : (at + 1) * H, :] = block[:H, :]
-            diags = jnp.where(iota((EXTRA, B), 0) == at, block[H:, :].astype(F32), diags)
-        out_ref[chip, room * H :, :] = diags.astype(BF)
+            index = send_ref[chip, at]
+            same = index // 8 == core
+            half = jnp.where(same, mine_ref[index % 8, rows, :], other_ref[index % 8, rows, :])
+            diag = jnp.where(same, mine_ref[index % 8, H:, :], other_ref[index % 8, H:, :])
+            out_ref[chip, at * Q : (at + 1) * Q, :] = half
+            diags = jnp.where(iota((EXTRA, B), 0) == at, diag.astype(F32), diags)
+        out_ref[chip, room * Q :, :] = diags.astype(BF)
 
 
 def route(room, sends, mine, other):
     return pl.pallas_call(
         functools.partial(route_kernel, room),
-        out_shape=jax.ShapeDtypeStruct((16, room * H + EXTRA, B), BF),
+        out_shape=jax.ShapeDtypeStruct((16, room * Q + EXTRA, B), BF),
         in_specs=[SMEM, VMEM, VMEM],
         out_specs=VMEM,
         compiler_params=PARAMS,
@@ -361,43 +361,55 @@
     for ref, column in ((keep_ref, core), (give_ref, 1 - core)):
         for want in range(ref.shape[0]):
             index = column * col_blocks + want if want < col_blocks else col_blocks + want
-            found = find_ref[0, (8 if room in ROOMS else 32) + index]
-            chip, at = found // 16, found % 8
-            rows = pl.ds(pl.multiple_of(at * H, H), H)
-            ref[want, :H, :] = got_ref[chip, rows, :]
-            diag = take_row(got_ref[chip, room * H :, :].astype(F32), at)
-            ref[want, H:, :] = jnp.broadcast_to(diag, (EXTRA, B)).astype(BF)
-
-
-def pick(room, finds, got, row_blocks, col_blocks):
-    out = jax.ShapeDtypeStruct((col_blocks + row_blocks, H + EXTRA, B), BF)
-    return pl.pallas_call(
-        functools.partial(pick_kernel, room, col_blocks),
+            found = find_ref[0, 8 + index]
+            chip, at = found // 8, found % 8
+            ref[want, :Q, :] = got_ref[chip, pl.ds(pl.multiple_of(at * Q, Q), Q), :]
+            diag = take_row(got_ref[chip, room * Q :, :].astype(F32), at)
+            ref[want, Q:, :] = jnp.broadcast_to(diag, (EXTRA, B)).astype(BF)
+
+
+def pick_any_kernel(col_blocks, find_ref, mine_ref, other_ref, keep_ref, give_ref):
+    core = lax.axis_index("c")
+    rows = pl.ds(pl.multiple_of(core * Q, Q), Q)
+    for ref, column in ((keep_ref, core), (give_ref, 1 - core)):
+        for want in range(ref.shape[0]):
+            index = column * col_blocks + want if want < col_blocks else col_blocks + want
+            slot = find_ref[0, 32 + index]
+            chip, same, at = slot // 16, (slot // 8) % 2 == core, slot % 8
+            ref[want, :Q, :] = jnp.where(same, mine_ref[chip, at, rows, :], other_ref[chip, at, rows, :])
+            ref[want, Q:, :] = jnp.where(same, mine_ref[chip, at, H:, :], other_ref[chip, at, H:, :])
+
+
+def pick(kernel, finds, got, row_blocks, col_blocks):
+    out = jax.ShapeDtypeStruct((col_blocks + row_blocks, Q + EXTRA, B), BF)
+    return pl.pallas_call(
+        kernel,
         out_shape=(out, out),
-        in_specs=[SMEM, VMEM],
+        in_specs=[SMEM] + [VMEM] * len(got),
         out_specs=(VMEM, VMEM),
         compiler_params=PARAMS,
         name="pick",
-    )(finds, got)
-
-
-def final_kernel(find_ref, mine_ref, other_ref, weight_ref, out_ref, left_ref, right_ref, sems):
+    )(finds, *got)
+
+
+def final_kernel(mine_ref, other_ref, weight_ref, out_ref, left_ref, right_ref, sems):
     core = lax.axis_index("c")
     row_blocks = weight_ref.shape[0] // B
     col_blocks = weight_ref.shape[1] // B
 
-    def block(want, index):
-        same = find_ref[0, 56 + index] == core
-        packed = jnp.where(same, mine_ref[want], other_ref[want]).astype(F32)
-        return unpack(packed[:H, :], packed[H : H + 1, :]).astype(BF)
-
-    col_invs = [block(j, core * col_blocks + j) for j in range(col_blocks)]
+    def block(want):
+        mine, other = mine_ref[want].astype(F32), other_ref[want].astype(F32)
+        first = jnp.where(core == 0, mine[:Q, :], other[:Q, :])
+        second = jnp.where(core == 0, other[:Q, :], mine[:Q, :])
+        return unpack(jnp.concatenate((first, second), axis=0), mine[Q : Q + 1, :]).astype(BF)
+
+    col_invs = [block(j) for j in range(col_blocks)]
     copies = []
     span = row_blocks // STRIPS
     for strip in range(STRIPS):
         for i in range(strip * span, (strip + 1) * span):
             rows = slice(i * B, (i + 1) * B)
-            inv = block(col_blocks + i, 2 * col_blocks + i)
+            inv = block(col_blocks + i)
             left = jnp.dot(inv, weight_ref[rows, :], preferred_element_type=F32)
             left_ref[rows, :] = left.astype(BF)
         rows = slice(strip * span * B, (strip + 1) * span * B)
@@ -411,11 +423,11 @@
         copy.wait()
 
 
-def final(finds, mine, other, weight_grad):
+def final(mine, other, weight_grad):
     return pl.pallas_call(
         final_kernel,
         out_shape=jax.ShapeDtypeStruct(weight_grad.shape, BF),
-        in_specs=[SMEM, VMEM, VMEM, VMEM],
+        in_specs=[VMEM, VMEM, VMEM],
         out_specs=HBM,
         scratch_shapes=[
             pltpu.VMEM(weight_grad.shape, BF),
@@ -424,7 +436,7 @@
         ],
         compiler_params=PARAMS,
         name="final",
-    )(finds, mine, other, weight_grad)
+    )(mine, other, weight_grad)
 
 
 def on_device(acts, grads_out, weight_grad, slot_table, row_counts, old_cov):
@@ -447,15 +459,15 @@
 
     def compact(room, sends, finds, mine):
         got = exchange(route(room, sends, mine, swap(mine)), plane)
-        return pick(room, finds, got, row_blocks, col_blocks)
+        return pick(functools.partial(pick_kernel, room, col_blocks), finds, (got,), row_blocks, col_blocks)
 
     def full(sends, finds, mine):
-        got = exchange(route(8, sends, mine, mine), plane)
-        return pick(8, finds, got, row_blocks, col_blocks)
+        got = exchange(jnp.broadcast_to(mine[None], (16,) + mine.shape), plane)
+        return pick(functools.partial(pick_any_kernel, col_blocks), finds, (got, swap(got)), row_blocks, col_blocks)
 
     branches = [functools.partial(compact, room) for room in ROOMS] + [full]
     keep, give = lax.switch(branch[0], branches, sends, finds, mine)
-    return final(finds, keep, swap(give), weight_grad), new_cov
+    return final(keep, swap(give), weight_grad), new_cov
 
 
 def solution(mesh):

time: 114 us -> 113 us (level)
  blocking collectives: 66.9 us -> 65.4 us
    all_to_all x1, blocking collectives: 17.4 us -> 16 us  [compact(): got = exchange(route(room, sends, mine, swap(mine)), plane)]
where the time goes in v7:
time: 113 us; the launch traced here: 112 us
  blocking collectives  65.4 us (58%)
  Pallas kernels  21.5 us (19%)
  starting transfers between devices  12.5 us (11%)
  waiting for transfers between devices  10.1 us (9%)
  between operations  2.13 us (2%)
    all_to_all x1, blocking collectives, on_device(): parts = exchange(sums.reshape(16, -1, B), plane)  33.1 us
    all_to_all x1, blocking collectives, on_device(): parts = exchange(section_sum(parts), 'z')  16.4 us
    all_to_all x1, blocking collectives, compact(): got = exchange(route(room, sends, mine, swap(mine)), plane)  16 us
    all_to_all x1, waiting for transfers between devices, on_device(): mine = exchange(inv, 'z')  7.6 us
    pallas_call x1, Pallas kernels, inverse(): pl.pallas_call(inverse_kernel, out_shape=(jax.ShapeDtypeStruct(old_cov.sh...  7.13 us
    pallas_call x1, Pallas kernels, away_grams(): pl.pallas_call(functools.partial(away_kernel, row_blocks, col_blocks), ou...  6.6 us
    ppermute x1, starting transfers between devices, compact(): got = exchange(route(room, sends, mine, swap(mine)), plane)  4.23 us
    all_to_all x1, starting transfers between devices, on_device(): mine = exchange(inv, 'z')  3.38 us
  transfers between devices with their start and end apart: 4, of which 4 were waited for; matrix products, arithmetic and copies ran while one was open for 0% of the time, Pallas kernels for 3%

profile of v7, /device:TPU:1, one launch (start us, length us, event | category | flops | bytes accessed | tf_op | source)
XLA Modules:
  0.0 112.5 jit_solution(7631842151038541983)
XLA Ops:
  1.3 0.0 copy-start.2
  1.3 6.6 %grams_away.1 = (bf16[8448,128]{1,0:T(8,128)(2,1)S(1)}, s32[1]{0:T(128)}, s32[16,128]{1,0:T(8,128)S(1)}, s32[8,128]{1,0:T(8,128)S(1)}, bf16[128,30720]{1,0:T(8,128)(2,1)S(1)}) custom-call(s32[256]{0:T(256)} %table_ref.3, s32[1]{0:T(128)S(6)} %copy.16.live_ref, bf16[128,6144]{1,0:T(8,128)(2,1)} %acts_ref.1, bf16[128,24576]{1,0:T(8,128)(2,1)} %grads_ref.1), custom_call_target="tpu_custom_call" | custom-call | bytes 37748736 | tf_op jit(solution)/shard_map/grams_away/pallas_call | solution.py:232
  7.9 3.3 %collective-permute-start.4 = (bf16[8448,128]{1,0:T(8,128)(2,1)S(1)}, bf16[8448,128]{1,0:T(8,128)(2,1)S(1)}, u32[]{:S(2)}, u32[]{:S(2)}) collective-permute-start(bf16[8448,128]{1,0:T(8,128)(2,1)S(1)} %get-tuple-element.46), channel_id=1, source_target_pairs={{0,1},{1,0},{2,3},{3,2},{4,5},{5,4},{6,7},{7,6},{8,9},{9,8},{10,11... | collective-permute-start | bytes 6488072 | tf_op jit(solution)/shard_map/ppermute | solution.py:452
  11.2 0.0 copy-done.2
  11.2 3.4 %grams_own.1 = bf16[8448,128]{1,0:T(8,128)(2,1)S(1)} custom-call(s32[256]{0:T(256)S(1)} %copy-done.2, s32[1]{0:T(128)S(6)} %copy.16.live_ref, bf16[128,30720]{1,0:T(8,128)(2,1)S(1)} %get-tuple-element.45.x_ref), custom_call_target="tpu_custom_call" | custom-call | bytes 18874368 | tf_op jit(solution)/shard_map/grams_own/pallas_call | solution.py:260
  14.6 0.5 collective-permute-done.4
  15.1 0.6 add_convert_fusion
  15.7 33.1 %all_to_all.35.parts_ref = bf16[16,528,128]{2,1,0:T(8,128)(2,1)S(1)} all-to-all(bf16[16,528,128]{2,1,0:T(8,128)(2,1)S(1)} %bitcast.2), channel_id=1, replica_groups=mesh['z'=8,'y'=4,'x'=4,'c'=2] {'y','x'}, dimensions={0} | all-to-all | bytes 4325376 | tf_op jit(solution)/shard_map/all_to_all | solution.py:455
  48.8 0.3 section_sum.1
  49.1 16.4 %all_to_all.36.parts_ref = bf16[8,80,128]{2,1,0:T(8,128)(2,1)S(1)} all-to-all(bf16[8,80,128]{2,1,0:T(8,128)(2,1)S(1)} %section_sum.1), channel_id=1, replica_groups=mesh['z'=8,'y'=4,'x'=4,'c'=2] {'z'}, dimensions={0} | all-to-all | bytes 327680 | tf_op jit(solution)/shard_map/all_to_all | solution.py:456
  65.5 0.0 copy-done.1
  65.5 7.1 %inverse.1 = (f32[1,1,128,128]{3,2,1,0:T(8,128)}, bf16[8,80,128]{2,1,0:T(8,128)(2,1)}) custom-call(bf16[8,80,128]{2,1,0:T(8,128)(2,1)S(1)} %all_to_all.36.parts_ref, f32[1,1,128,128]{3,2,1,0:T(8,128)S(1)} %copy-done.1), custom_call_target="tpu_custom_call" | custom-call | tf_op jit(solution)/shard_map/inverse/pallas_call | solution.py:320
  72.6 3.4 %all-to-all-start.6 = ((bf16[8,80,128]{2,1,0:T(8,128)(2,1)}), bf16[8,80,128]{2,1,0:T(8,128)(2,1)S(1)}, u32[]{:S(2)}, u32[]{:S(2)}) async-start(bf16[8,80,128]{2,1,0:T(8,128)(2,1)} %get-tuple-element.47), calls=%async_computation.6 | async-start | bytes 327680 | tf_op jit(solution)/shard_map/all_to_all | solution.py:458
  76.6 7.6 %all-to-all-done.6 = bf16[8,80,128]{2,1,0:T(8,128)(2,1)S(1)} async-done(((bf16[8,80,128]{2,1,0:T(8,128)(2,1)}), bf16[8,80,128]{2,1,0:T(8,128)(2,1)S(1)}, u32[]{:S(2)}, u32[]{:S(2)}) %all-to-all-start.6) | async-done | bytes 163872 | tf_op jit(solution)/shard_map/all_to_all | solution.py:458
  84.2 23.6 %conditional.1 = ((bf16[12,48,128]{2,1,0:T(8,128)(2,1)S(1)}, bf16[12,48,128]{2,1,0:T(8,128)(2,1)S(1)})) conditional(s32[]{:T(128)} %bitcast, (bf16[8,80,128]{2,1,0:T(8,128)(2,1)S(1)}, s32[16,128]{1,0:T(8,128)S(1)}, s32[8,128]{1,0:T(8,128)S(1)}) %tuple.20, (bf16[8,80,128]{2,1,0:T(8,128)(2,1)S(1)}, ...), branch_computations={%region_0.0_spmd, %region_1.0_spmd, %region_2.0_spmd, %region_3.0_... | conditional | bytes 18513968 | solution.py:469
  84.2 4.2 %collective-permute-start = (bf16[8,80,128]{2,1,0:T(8,128)(2,1)S(1)}, bf16[8,80,128]{2,1,0:T(8,128)(2,1)S(1)}, u32[]{:S(2)}, u32[]{:S(2)}) collective-permute-start(bf16[8,80,128]{2,1,0:T(8,128)(2,1)S(1)} %get-tuple-element.24.mine_ref), channel_id=1, source_target_pairs={{0,1},{1,0},{2,3},{3,2},{4,5},{5,4},{6,7},{7,6},{8,9},{9,8},{10,11... | collective-permute-start | bytes 491528 | tf_op jit(solution)/shard_map/cond/branch_0_fun/ppermute | solution.py:461
  88.5 1.0 collective-permute-done.other_ref
  89.5 1.3 %route.3 = bf16[16,176,128]{2,1,0:T(8,128)(2,1)S(1)} custom-call(s32[16,128]{1,0:T(8,128)S(1)} %get-tuple-element.23.send_ref, bf16[8,80,128]{2,1,0:T(8,128)(2,1)S(1)} %get-tuple-element.24.mine_ref, bf16[8,80,128]{2,1,0:T(8,128)(2,1)S(1)} %collective-permute-done.other_ref), custom_call_target="tpu_custom_call" | custom-call | tf_op jit(solution)/shard_map/cond/branch_0_fun/route/pallas_call | solution.py:349
  90.8 16.0 %all_to_all.31.got_ref = bf16[16,176,128]{2,1,0:T(8,128)(2,1)S(1)} all-to-all(bf16[16,176,128]{2,1,0:T(8,128)(2,1)S(1)} %route.3), channel_id=1, replica_groups=mesh['z'=8,'y'=4,'x'=4,'c'=2] {'y','x'}, dimensions={0} | all-to-all | bytes 1441792 | tf_op jit(solution)/shard_map/cond/branch_0_fun/all_to_all | solution.py:461
  106.8 0.8 pick.4
  107.8 1.6 %collective-permute-start.5 = (bf16[12,48,128]{2,1,0:T(8,128)(2,1)S(1)}, bf16[12,48,128]{2,1,0:T(8,128)(2,1)S(1)}, u32[]{:S(2)}, u32[]{:S(2)}) collective-permute-start(bf16[12,48,128]{2,1,0:T(8,128)(2,1)S(1)} %get-tuple-element.51), channel_id=1, source_target_pairs={{0,1},{1,0},{2,3},{3,2},{4,5},{5,4},{6,7},{7,6},{8,9},{9,8},{10,11... | collective-permute-start | bytes 442376 | tf_op jit(solution)/shard_map/ppermute | solution.py:470
  109.4 1.0 collective-permute-done.5.other_ref
  110.4 0.0 copy-done
  110.4 1.9 %final.1 = bf16[768,768]{1,0:T(8,128)(2,1)} custom-call(bf16[12,48,128]{2,1,0:T(8,128)(2,1)S(1)} %get-tuple-element.50.mine_ref, bf16[12,48,128]{2,1,0:T(8,128)(2,1)S(1)} %collective-permute-done.5.other_ref, bf16[768,768]{1,0:T(8,128)(2,1)S(1)} %copy-done), custom_call_target="tpu_custom_call" | custom-call | tf_op jit(solution)/shard_map/final/pallas_call | solution.py:427
  (2 shorter events, 0.0 us)
Async XLA Ops:
  1.3 10.0 %copy-start.2 = (s32[256]{0:T(256)S(1)}, s32[256]{0:T(256)}, u32[]{:S(2)}) copy-start(s32[256]{0:T(256)} %table_ref.3) | copy-start | bytes 3076
  7.9 7.2 %collective-permute-start.4 = (bf16[8448,128]{1,0:T(8,128)(2,1)S(1)}, bf16[8448,128]{1,0:T(8,128)(2,1)S(1)}, u32[]{:S(2)}, u32[]{:S(2)}) collective-permute-start(bf16[8448,128]{1,0:T(8,128)(2,1)S(1)} %get-tuple-element.46), channel_id=1, source_target_pairs={{0,1},{1,0},{2,3},{3,2},{4,5},{5,4},{6,7},{7,6},{8,9},{9,8},{10,11... | collective-permute-start | bytes 6488072 | tf_op jit(solution)/shard_map/ppermute | solution.py:452
  48.8 16.7 %copy-start.1 = (f32[1,1,128,128]{3,2,1,0:T(8,128)S(1)}, f32[1,1,128,128]{3,2,1,0:T(8,128)}, u32[]{:S(2)}) copy-start(f32[1,1,128,128]{3,2,1,0:T(8,128)} %old_ref.1) | copy-start | bytes 196612
  72.6 11.6 %all-to-all-start.6 = ((bf16[8,80,128]{2,1,0:T(8,128)(2,1)}), bf16[8,80,128]{2,1,0:T(8,128)(2,1)S(1)}, u32[]{:S(2)}, u32[]{:S(2)}) async-start(bf16[8,80,128]{2,1,0:T(8,128)(2,1)} %get-tuple-element.47), calls=%async_computation.6 | async-start | bytes 327680 | tf_op jit(solution)/shard_map/all_to_all | solution.py:458
  84.2 26.2 %copy-start = (bf16[768,768]{1,0:T(8,128)(2,1)S(1)}, bf16[768,768]{1,0:T(8,128)(2,1)}, u32[]{:S(2)}) copy-start(bf16[768,768]{1,0:T(8,128)(2,1)} %weight_ref.1) | copy-start | bytes 3538948
  84.2 5.3 %collective-permute-start = (bf16[8,80,128]{2,1,0:T(8,128)(2,1)S(1)}, bf16[8,80,128]{2,1,0:T(8,128)(2,1)S(1)}, u32[]{:S(2)}, u32[]{:S(2)}) collective-permute-start(bf16[8,80,128]{2,1,0:T(8,128)(2,1)S(1)} %get-tuple-element.24.mine_ref), channel_id=1, source_target_pairs={{0,1},{1,0},{2,3},{3,2},{4,5},{5,4},{6,7},{7,6},{8,9},{9,8},{10,11... | collective-permute-start | bytes 491528 | tf_op jit(solution)/shard_map/cond/branch_0_fun/ppermute | solution.py:461
  107.8 2.6 %collective-permute-start.5 = (bf16[12,48,128]{2,1,0:T(8,128)(2,1)S(1)}, bf16[12,48,128]{2,1,0:T(8,128)(2,1)S(1)}, u32[]{:S(2)}, u32[]{:S(2)}) collective-permute-start(bf16[12,48,128]{2,1,0:T(8,128)(2,1)S(1)} %get-tuple-element.51), channel_id=1, source_target_pairs={{0,1},{1,0},{2,3},{3,2},{4,5},{5,4},{6,7},{7,6},{8,9},{9,8},{10,11... | collective-permute-start | bytes 442376 | tf_op jit(solution)/shard_map/ppermute | solution.py:470

commit v8 on v7

--- a/solution.py
+++ b/solution.py
@@ -455,18 +455,19 @@
     parts = exchange(sums.reshape(16, -1, B), plane)
     parts = exchange(section_sum(parts), "z")
     new_cov, inv = inverse(parts, old_cov)
-    mine = exchange(inv, "z")
-
-    def compact(room, sends, finds, mine):
+
+    def compact(room, sends, finds, inv):
+        mine = exchange(inv, "z")
         got = exchange(route(room, sends, mine, swap(mine)), plane)
         return pick(functools.partial(pick_kernel, room, col_blocks), finds, (got,), row_blocks, col_blocks)
 
-    def full(sends, finds, mine):
+    def full(sends, finds, inv):
+        mine = exchange(inv, "z")
         got = exchange(jnp.broadcast_to(mine[None], (16,) + mine.shape), plane)
         return pick(functools.partial(pick_any_kernel, col_blocks), finds, (got, swap(got)), row_blocks, col_blocks)
 
     branches = [functools.partial(compact, room) for room in ROOMS] + [full]
-    keep, give = lax.switch(branch[0], branches, sends, finds, mine)
+    keep, give = lax.switch(branch[0], branches, sends, finds, inv)
     return final(keep, swap(give), weight_grad), new_cov
 
 

time: 113 us -> 113 us (level)
  blocking collectives: 65.4 us -> 59.9 us
  starting transfers between devices: 12.5 us -> 17.3 us
    all_to_all x1, blocking collectives: 16.4 us -> 10.8 us  [compact(): mine = exchange(inv, 'z')]
    all_to_all x1, starting transfers between devices: 3.38 us -> 8.19 us  [on_device(): parts = exchange(section_sum(parts), 'z')]
where the time goes in v8:
time: 113 us; the launch traced here: 112 us
  blocking collectives  59.9 us (53%)
  Pallas kernels  21.5 us (19%)
  starting transfers between devices  17.3 us (15%)
  waiting for transfers between devices  10.3 us (9%)
  between operations  2.15 us (2%)
    all_to_all x1, blocking collectives, on_device(): parts = exchange(sums.reshape(16, -1, B), plane)  33.1 us
    all_to_all x1, blocking collectives, compact(): got = exchange(route(room, sends, mine, swap(mine)), plane)  16 us
    all_to_all x1, blocking collectives, compact(): mine = exchange(inv, 'z')  10.8 us
    all_to_all x1, starting transfers between devices, on_device(): parts = exchange(section_sum(parts), 'z')  8.19 us
    all_to_all x1, waiting for transfers between devices, on_device(): parts = exchange(section_sum(parts), 'z')  7.73 us
    pallas_call x1, Pallas kernels, away_grams(): pl.pallas_call(functools.partial(away_kernel, row_blocks, col_blocks), ou...  6.63 us
    pallas_call x1, Pallas kernels, inverse(): pl.pallas_call(inverse_kernel, out_shape=(jax.ShapeDtypeStruct(old_cov.sh...  6.47 us
    ppermute x1, starting transfers between devices, compact(): got = exchange(route(room, sends, mine, swap(mine)), plane)  4.25 us
  transfers between devices with their start and end apart: 4, of which 4 were waited for; matrix products, arithmetic and copies ran while one was open for 0% of the time, Pallas kernels for 3%

profile of v8, /device:TPU:1, one launch (start us, length us, event | category | flops | bytes accessed | tf_op | source)
XLA Modules:
  0.0 111.9 jit_solution(2209227149046069910)
XLA Ops:
  1.3 0.0 copy-start.2
  1.3 6.6 %grams_away.1 = (bf16[8448,128]{1,0:T(8,128)(2,1)S(1)}, s32[1]{0:T(128)}, s32[16,128]{1,0:T(8,128)S(1)}, s32[8,128]{1,0:T(8,128)S(1)}, bf16[128,30720]{1,0:T(8,128)(2,1)S(1)}) custom-call(s32[256]{0:T(256)} %table_ref.3, s32[1]{0:T(128)S(6)} %copy.16.live_ref, bf16[128,6144]{1,0:T(8,128)(2,1)} %acts_ref.1, bf16[128,24576]{1,0:T(8,128)(2,1)} %grads_ref.1), custom_call_target="tpu_custom_call" | custom-call | bytes 37748736 | tf_op jit(solution)/shard_map/grams_away/pallas_call | solution.py:232
  7.9 3.3 %collective-permute-start.4 = (bf16[8448,128]{1,0:T(8,128)(2,1)S(1)}, bf16[8448,128]{1,0:T(8,128)(2,1)S(1)}, u32[]{:S(2)}, u32[]{:S(2)}) collective-permute-start(bf16[8448,128]{1,0:T(8,128)(2,1)S(1)} %get-tuple-element.46), channel_id=1, source_target_pairs={{0,1},{1,0},{2,3},{3,2},{4,5},{5,4},{6,7},{7,6},{8,9},{9,8},{10,11... | collective-permute-start | bytes 6488072 | tf_op jit(solution)/shard_map/ppermute | solution.py:452
  11.2 0.0 copy-done.2
  11.2 3.4 %grams_own.1 = bf16[8448,128]{1,0:T(8,128)(2,1)S(1)} custom-call(s32[256]{0:T(256)S(1)} %copy-done.2, s32[1]{0:T(128)S(6)} %copy.16.live_ref, bf16[128,30720]{1,0:T(8,128)(2,1)S(1)} %get-tuple-element.45.x_ref), custom_call_target="tpu_custom_call" | custom-call | bytes 18874368 | tf_op jit(solution)/shard_map/grams_own/pallas_call | solution.py:260
  14.6 0.5 collective-permute-done.4
  15.1 0.6 add_convert_fusion
  15.7 33.1 %all_to_all.50.parts_ref = bf16[16,528,128]{2,1,0:T(8,128)(2,1)S(1)} all-to-all(bf16[16,528,128]{2,1,0:T(8,128)(2,1)S(1)} %bitcast.2), channel_id=1, replica_groups=mesh['z'=8,'y'=4,'x'=4,'c'=2] {'y','x'}, dimensions={0} | all-to-all | bytes 4325376 | tf_op jit(solution)/shard_map/all_to_all | solution.py:455
  48.8 1.0 section_sum.1
  49.8 8.2 %all-to-all-start.9 = ((bf16[8,80,128]{2,1,0:T(8,128)(2,1)}), bf16[8,80,128]{2,1,0:T(8,128)(2,1)S(1)}, u32[]{:S(2)}, u32[]{:S(2)}) async-start(bf16[8,80,128]{2,1,0:T(8,128)(2,1)} %section_sum.1), calls=%async_computation.9 | async-start | bytes 327680 | tf_op jit(solution)/shard_map/all_to_all | solution.py:456
  58.6 7.7 %all-to-all-done.9.parts_ref = bf16[8,80,128]{2,1,0:T(8,128)(2,1)S(1)} async-done(((bf16[8,80,128]{2,1,0:T(8,128)(2,1)}), bf16[8,80,128]{2,1,0:T(8,128)(2,1)S(1)}, u32[]{:S(2)}, u32[]{:S(2)}) %all-to-all-start.9) | async-done | bytes 163872 | tf_op jit(solution)/shard_map/all_to_all | solution.py:456
  66.3 0.0 copy-done.1
  66.3 6.5 %inverse.1 = (f32[1,1,128,128]{3,2,1,0:T(8,128)}, bf16[8,80,128]{2,1,0:T(8,128)(2,1)S(1)}) custom-call(bf16[8,80,128]{2,1,0:T(8,128)(2,1)S(1)} %all-to-all-done.9.parts_ref, f32[1,1,128,128]{3,2,1,0:T(8,128)S(1)} %copy-done.1), custom_call_target="tpu_custom_call" | custom-call | tf_op jit(solution)/shard_map/inverse/pallas_call | solution.py:320
  72.8 0.0 copy-start
  72.8 34.4 %conditional.1 = ((bf16[12,48,128]{2,1,0:T(8,128)(2,1)S(1)}, bf16[12,48,128]{2,1,0:T(8,128)(2,1)S(1)})) conditional(s32[]{:T(128)} %bitcast, (bf16[8,80,128]{2,1,0:T(8,128)(2,1)S(1)}, s32[16,128]{1,0:T(8,128)S(1)}, s32[8,128]{1,0:T(8,128)S(1)}) %tuple.20, (bf16[8,80,128]{2,1,0:T(8,128)(2,1)S(1)}, ...), branch_computations={%region_0.0_spmd, %region_1.0_spmd, %region_2.0_spmd, %region_3.0_... | conditional | bytes 18841648 | solution.py:470
  72.8 10.8 %all_to_all.42.mine_ref = bf16[8,80,128]{2,1,0:T(8,128)(2,1)S(1)} all-to-all(bf16[8,80,128]{2,1,0:T(8,128)(2,1)S(1)} %get-tuple-element.24), channel_id=1, replica_groups=mesh['z'=8,'y'=4,'x'=4,'c'=2] {'z'}, dimensions={0} | all-to-all | bytes 327680 | tf_op jit(solution)/shard_map/cond/branch_0_fun/all_to_all | solution.py:460
  83.7 4.2 %collective-permute-start = (bf16[8,80,128]{2,1,0:T(8,128)(2,1)S(1)}, bf16[8,80,128]{2,1,0:T(8,128)(2,1)S(1)}, u32[]{:S(2)}, u32[]{:S(2)}) collective-permute-start(bf16[8,80,128]{2,1,0:T(8,128)(2,1)S(1)} %all_to_all.42.mine_ref), channel_id=1, source_target_pairs={{0,1},{1,0},{2,3},{3,2},{4,5},{5,4},{6,7},{7,6},{8,9},{9,8},{10,11... | collective-permute-start | bytes 491528 | tf_op jit(solution)/shard_map/cond/branch_0_fun/ppermute | solution.py:461
  87.9 1.0 collective-permute-done.other_ref
  88.9 1.3 %route.3 = bf16[16,176,128]{2,1,0:T(8,128)(2,1)S(1)} custom-call(s32[16,128]{1,0:T(8,128)S(1)} %get-tuple-element.23.send_ref, bf16[8,80,128]{2,1,0:T(8,128)(2,1)S(1)} %all_to_all.42.mine_ref, bf16[8,80,128]{2,1,0:T(8,128)(2,1)S(1)} %collective-permute-done.other_ref), custom_call_target="tpu_custom_call" | custom-call | tf_op jit(solution)/shard_map/cond/branch_0_fun/route/pallas_call | solution.py:349
  90.3 16.0 %all_to_all.43.got_ref = bf16[16,176,128]{2,1,0:T(8,128)(2,1)S(1)} all-to-all(bf16[16,176,128]{2,1,0:T(8,128)(2,1)S(1)} %route.3), channel_id=1, replica_groups=mesh['z'=8,'y'=4,'x'=4,'c'=2] {'y','x'}, dimensions={0} | all-to-all | bytes 1441792 | tf_op jit(solution)/shard_map/cond/branch_0_fun/all_to_all | solution.py:461
  106.3 0.8 pick.4
  107.3 1.6 %collective-permute-start.5 = (bf16[12,48,128]{2,1,0:T(8,128)(2,1)S(1)}, bf16[12,48,128]{2,1,0:T(8,128)(2,1)S(1)}, u32[]{:S(2)}, u32[]{:S(2)}) collective-permute-start(bf16[12,48,128]{2,1,0:T(8,128)(2,1)S(1)} %get-tuple-element.51), channel_id=1, source_target_pairs={{0,1},{1,0},{2,3},{3,2},{4,5},{5,4},{6,7},{7,6},{8,9},{9,8},{10,11... | collective-permute-start | bytes 442376 | tf_op jit(solution)/shard_map/ppermute | solution.py:471
  108.8 1.0 collective-permute-done.5.other_ref
  109.8 1.9 %final.1 = bf16[768,768]{1,0:T(8,128)(2,1)} custom-call(bf16[12,48,128]{2,1,0:T(8,128)(2,1)S(1)} %get-tuple-element.50.mine_ref, bf16[12,48,128]{2,1,0:T(8,128)(2,1)S(1)} %collective-permute-done.5.other_ref, bf16[768,768]{1,0:T(8,128)(2,1)S(1)} %copy-done), custom_call_target="tpu_custom_call" | custom-call | tf_op jit(solution)/shard_map/final/pallas_call | solution.py:427
  (2 shorter events, 0.0 us)
Async XLA Ops:
  1.3 10.0 %copy-start.2 = (s32[256]{0:T(256)S(1)}, s32[256]{0:T(256)}, u32[]{:S(2)}) copy-start(s32[256]{0:T(256)} %table_ref.3) | copy-start | bytes 3076
  7.9 7.2 %collective-permute-start.4 = (bf16[8448,128]{1,0:T(8,128)(2,1)S(1)}, bf16[8448,128]{1,0:T(8,128)(2,1)S(1)}, u32[]{:S(2)}, u32[]{:S(2)}) collective-permute-start(bf16[8448,128]{1,0:T(8,128)(2,1)S(1)} %get-tuple-element.46), channel_id=1, source_target_pairs={{0,1},{1,0},{2,3},{3,2},{4,5},{5,4},{6,7},{7,6},{8,9},{9,8},{10,11... | collective-permute-start | bytes 6488072 | tf_op jit(solution)/shard_map/ppermute | solution.py:452
  48.8 17.5 %copy-start.1 = (f32[1,1,128,128]{3,2,1,0:T(8,128)S(1)}, f32[1,1,128,128]{3,2,1,0:T(8,128)}, u32[]{:S(2)}) copy-start(f32[1,1,128,128]{3,2,1,0:T(8,128)} %old_ref.1) | copy-start | bytes 196612
  49.8 16.6 %all-to-all-start.9 = ((bf16[8,80,128]{2,1,0:T(8,128)(2,1)}), bf16[8,80,128]{2,1,0:T(8,128)(2,1)S(1)}, u32[]{:S(2)}, u32[]{:S(2)}) async-start(bf16[8,80,128]{2,1,0:T(8,128)(2,1)} %section_sum.1), calls=%async_computation.9 | async-start | bytes 327680 | tf_op jit(solution)/shard_map/all_to_all | solution.py:456
  72.8 37.0 %copy-start = (bf16[768,768]{1,0:T(8,128)(2,1)S(1)}, bf16[768,768]{1,0:T(8,128)(2,1)}, u32[]{:S(2)}) copy-start(bf16[768,768]{1,0:T(8,128)(2,1)} %weight_ref.1) | copy-start | bytes 3538948
  83.7 5.3 %collective-permute-start = (bf16[8,80,128]{2,1,0:T(8,128)(2,1)S(1)}, bf16[8,80,128]{2,1,0:T(8,128)(2,1)S(1)}, u32[]{:S(2)}, u32[]{:S(2)}) collective-permute-start(bf16[8,80,128]{2,1,0:T(8,128)(2,1)S(1)} %all_to_all.42.mine_ref), channel_id=1, source_target_pairs={{0,1},{1,0},{2,3},{3,2},{4,5},{5,4},{6,7},{7,6},{8,9},{9,8},{10,11... | collective-permute-start | bytes 491528 | tf_op jit(solution)/shard_map/cond/branch_0_fun/ppermute | solution.py:461
  107.3 2.6 %collective-permute-start.5 = (bf16[12,48,128]{2,1,0:T(8,128)(2,1)S(1)}, bf16[12,48,128]{2,1,0:T(8,128)(2,1)S(1)}, u32[]{:S(2)}, u32[]{:S(2)}) collective-permute-start(bf16[12,48,128]{2,1,0:T(8,128)(2,1)S(1)} %get-tuple-element.51), channel_id=1, source_target_pairs={{0,1},{1,0},{2,3},{3,2},{4,5},{5,4},{6,7},{7,6},{8,9},{9,8},{10,11... | collective-permute-start | bytes 442376 | tf_op jit(solution)/shard_map/ppermute | solution.py:471
